TPU v7x, 256 devices: a whole 4x4x8 slice. The times are simulated.
256 devices in a mesh: seq: 64 (over z, y, core), tp: 4 (over x).
Axes of the slice: x: 4, y: 4, z: 8, core: 2. Of those that a mesh axis runs over, the one named last changes fastest.
Arguments:
- query: bfloat16 [53248, 2048], P('seq', 'tp'), may hold values from -200 to 200
- d_attended: bfloat16 [53248, 2048], P('seq', 'tp'), may hold values from -6 to 6
- encoded: bfloat16 [1024, 128, 896], P('seq', 'tp'), may hold values from -6 to 6
- key_weight: bfloat16 [896, 2048], replicated, may hold values from -0.1875 to 0.1875
- value_weight: bfloat16 [896, 2048], replicated, may hold values from -0.1875 to 0.1875
- nbr_shard: int32 [832, 2], P('seq'), may hold values from 0 to 63, all different within a row; in each aligned block of 13 rows (0 to 12, 13 to 25, ...) at most 2 rows name the same one
- nbr_row: int32 [832, 2], P('seq'), may hold values from 0 to 15
Outputs:
- attended: bfloat16 [53248, 2048], P('seq', 'tp')
- d_query: bfloat16 [53248, 2048], P('seq', 'tp')
- d_encoded: bfloat16 [1024, 128, 896], P('seq', 'tp')
Inputs may be any that keep to these rules, and one draw needn't show every extreme that they name: `nbr_shard`: a span's 2 neighbours lie on different indices; among the 13 spans of one sequence no index is named more than 2 times, a bound that some block reaches.
All inputs are finite; a program needn't handle non-finite values.
Results may differ from a plain program's by a relative error of at most 0.017.
The roundings to bfloat16 on the way count: a program that leaves them out, or rounds other values in their place, can miss the bound.
Values may be sent and summed in bfloat16 or wider, within the bound.
No kernel may reach another device: no remote copies, remote signals or barrier semaphores. Data moves between devices by JAX's collectives and lax.ppermute only.
A program may use at most 192 MiB of HBM per device.

v0:
```python
import jax
import jax.numpy as jnp
from jax import lax
from jax.experimental import pallas as pl
from jax.experimental.pallas import tpu as pltpu
from jax.sharding import Mesh, PartitionSpec as P

HD = 128
SPAN = 64
PIECE = 4
PART = 256
BF = jnp.bfloat16
F32 = jnp.float32
I32 = jnp.int32
PARAMS = pltpu.CompilerParams(vmem_limit_bytes=48 * 1024 * 1024)


def matmul(left, right, left_dim=1, right_dim=0):
    return lax.dot_general(
        left, right, (((left_dim,), (right_dim,)), ((), ())), preferred_element_type=F32
    )


def cost(flops, bytes_accessed, transcendentals=0):
    return pl.CostEstimate(
        flops=int(flops), bytes_accessed=int(bytes_accessed), transcendentals=int(transcendentals)
    )


def send_ring(array, axis, step):
    size = lax.axis_size(axis)
    if step % size == 0:
        return array
    return lax.ppermute(array, axis, [(i, (i + step) % size) for i in range(size)])


def cuts(features):
    return [
        (part, start, min(start + PART, features))
        for part, start in enumerate(range(0, features, PART))
    ]


def piece_matrix(stored, quarter):
    shape = (stored * quarter, stored * quarter)
    to = lax.broadcasted_iota(I32, shape, 0)
    source = lax.broadcasted_iota(I32, shape, 1)
    token = to % stored * quarter + to // stored
    return (source == token).astype(F32).astype(BF)


def split_pieces(encoded, planes, columns):
    stored, quarter, features = encoded.shape
    size = stored * quarter

    def kernel(enc_ref, out_ref):
        pieces = matmul(piece_matrix(stored, quarter), enc_ref[...]).astype(BF)
        for plane in range(planes):
            for token in range(PIECE):
                first = (plane * PIECE + token) * stored
                for part, start, end in cuts(features):
                    at = token * PART
                    block = pieces[first : first + stored, start:end]
                    out_ref[plane * columns + part, :, at : at + end - start] = block
                    if end - start < PART:
                        blank = jnp.zeros((stored, PART - end + start), BF)
                        out_ref[plane * columns + part, :, at + end - start : at + PART] = blank

    return pl.pallas_call(
        kernel,
        out_shape=jax.ShapeDtypeStruct((planes * columns, stored, PIECE * PART), BF),
        compiler_params=PARAMS,
        cost_estimate=cost(2 * size * size * features, 4 * size * features),
        name="split_pieces",
    )(encoded.reshape(size, features))


def join_pieces(parts, planes, columns, quarter, features):
    stored = parts.shape[1]
    size = stored * quarter

    def kernel(part_ref, out_ref, rows_ref):
        for plane in range(planes):
            for token in range(PIECE):
                first = (plane * PIECE + token) * stored
                for part, start, end in cuts(features):
                    at = token * PART
                    block = part_ref[plane * columns + part, :, at : at + end - start]
                    rows_ref[first : first + stored, start:end] = block
        order = piece_matrix(stored, quarter)
        out_ref[...] = matmul(order, rows_ref[...], 0, 0).astype(BF)

    joined = pl.pallas_call(
        kernel,
        out_shape=jax.ShapeDtypeStruct((size, features), BF),
        scratch_shapes=[pltpu.VMEM((size, features), BF)],
        compiler_params=PARAMS,
        cost_estimate=cost(2 * size * size * features, 4 * size * features),
        name="join_pieces",
    )(parts)
    return joined.reshape(stored, quarter, features)


def pick_rows(store, target, other=None):
    rows, width = store.shape
    picks = target.shape[0]
    last = other is not None

    def kernel(target_ref, store_ref, *refs):
        column = lax.broadcasted_iota(I32, (picks, rows), 1)
        one_hot = (column == target_ref[...]).astype(F32).astype(BF)
        if not last:
            refs[0][...] = matmul(one_hot, store_ref[...]).astype(BF)
            return
        other_ref, out_ref, spread = refs
        for token in range(PIECE):
            for half in range(PART // HD):
                at = token * PART + half * HD
                total = matmul(one_hot, store_ref[:, at : at + HD])
                total = total + other_ref[:, at : at + HD].astype(F32)
                spread[half, pl.ds(token, picks, stride=PIECE), :] = total
        for half in range(PART // HD):
            out_ref[:, half * HD : (half + 1) * HD] = spread[half].astype(BF)

    shape = (picks * PIECE, PART) if last else (picks, width)
    return pl.pallas_call(
        kernel,
        out_shape=jax.ShapeDtypeStruct(shape, BF),
        scratch_shapes=[pltpu.VMEM((PART // HD, picks * PIECE, HD), F32)] if last else [],
        compiler_params=PARAMS,
        cost_estimate=cost(2 * picks * rows * width, 2 * (picks + rows) * width),
        name="pick_rows",
    )(target, store, *([other] if last else []))


def sum_rows(terms, target, rows):
    count = len(terms)
    picks = target.shape[1] // count
    width = PIECE * PART

    def kernel(target_ref, *refs):
        out_ref, spread = refs[count:]
        row = lax.broadcasted_iota(I32, (rows, count * picks), 0)
        one_hot = (row == target_ref[...]).astype(F32).astype(BF)
        for half in range(PART // HD):
            for which in range(count):
                spread[which, half] = refs[which][:, half * HD : (half + 1) * HD].astype(F32)
        for token in range(PIECE):
            for half in range(PART // HD):
                at = token * PART + half * HD
                joined = [
                    spread[which, half, pl.ds(token, picks, stride=PIECE), :].astype(BF)
                    for which in range(count)
                ]
                out_ref[:, at : at + HD] = matmul(one_hot, jnp.concatenate(joined, 0)).astype(BF)

    return pl.pallas_call(
        kernel,
        out_shape=jax.ShapeDtypeStruct((rows, width), BF),
        scratch_shapes=[pltpu.VMEM((count, PART // HD, picks * PIECE, HD), F32)],
        compiler_params=PARAMS,
        cost_estimate=cost(2 * count * picks * rows * width, 2 * (count * picks + rows) * width),
        name="sum_rows",
    )(target, *terms)


def move_tokens(arrays, forward):
    tokens, width = arrays[0].shape[-2:]
    spans = tokens // SPAN
    packed = jax.ShapeDtypeStruct((2, tokens, width), BF)
    apart = [jax.ShapeDtypeStruct((tokens, width), BF)] * 2

    def kernel(*refs):
        to = lax.broadcasted_iota(I32, (SPAN, 2 * SPAN), 0)
        source = lax.broadcasted_iota(I32, (SPAN, 2 * SPAN), 1)
        step = SPAN - 1 if forward else 1
        order = (source == to + step).astype(F32).astype(BF)
        blank = jnp.zeros((SPAN, width), BF)
        pack = refs[-1] if forward else refs[0]
        for which, ref in enumerate(refs[:2] if forward else refs[1:]):
            for span in range(spans):
                low = span if forward else span - 1
                pair = []
                for u in (low, low + 1):
                    if not 0 <= u < spans:
                        pair.append(blank)
                    elif forward:
                        pair.append(ref[u * SPAN : (u + 1) * SPAN])
                    else:
                        pair.append(pack[which, u * SPAN : (u + 1) * SPAN])
                moved = matmul(order, jnp.concatenate(pair, 0)).astype(BF)
                if forward:
                    pack[which, span * SPAN : (span + 1) * SPAN] = moved
                else:
                    ref[span * SPAN : (span + 1) * SPAN] = moved

    return pl.pallas_call(
        kernel,
        out_shape=packed if forward else apart,
        compiler_params=PARAMS,
        cost_estimate=cost(8 * tokens * SPAN * width, 8 * tokens * width),
        name="move_tokens",
    )(*arrays)


def two_heads(pair):
    column = lax.broadcasted_iota(I32, (2 * SPAN, 2 * HD), 1)
    row = lax.broadcasted_iota(I32, (2 * SPAN, 2 * HD), 0)
    mask = ((column < HD) == (row < SPAN)).astype(F32).astype(BF)
    return jnp.concatenate([pair, pair], 0) * mask


def score_spans(fetched, key_weight, value_weight, moved):
    count, columns = fetched.shape[:2]
    features, all_width = key_weight.shape
    groups, _, tokens, width = moved.shape
    spans = tokens // SPAN
    piece_rows = fetched.shape[2] // spans
    keys = count * piece_rows
    per_group = width // (2 * HD)
    pairs = all_width // (2 * HD)
    factor = HD ** (-0.5)

    def kernel(
        part_ref, wk_ref, wv_ref, moved_ref, k_ref, v_ref, w_ref, gp_ref, stat_ref, rows_ref
    ):
        @pl.when(pl.program_id(0) == 0)
        def _():
            for part, start, end in cuts(features):
                block = part_ref[:, part, :, : end - start]
                rows_ref[:, start:end] = block.reshape(count * spans * piece_rows, end - start)

        rows = rows_ref[...]

        def project(weight):
            out = matmul(rows, weight).reshape(count, spans, piece_rows, 2 * HD)
            return out.transpose(1, 0, 2, 3).reshape(spans, keys, 2 * HD).astype(BF)

        k_ref[...] = project(wk_ref[...])
        v_ref[...] = project(wv_ref[...])
        for span in range(spans):
            tok = pl.ds(span * SPAN, SPAN)
            scores = matmul(k_ref[span], two_heads(moved_ref[0, 0, tok, :]), 1, 1) * factor
            grad = matmul(v_ref[span], two_heads(moved_ref[0, 1, tok, :]), 1, 1)
            top = jnp.max(scores, axis=0, keepdims=True)
            weights = jnp.exp(scores - top)
            w_ref[0, span] = weights
            gp_ref[0, span] = grad
            stat_ref[0, 0, pl.ds(span, 1), :] = top
            stat_ref[0, 1, pl.ds(span, 1), :] = jnp.sum(weights, axis=0, keepdims=True)
            stat_ref[0, 2, pl.ds(span, 1), :] = jnp.sum(weights * grad, axis=0, keepdims=True)

    whole = pl.BlockSpec(fetched.shape, lambda i: (0, 0, 0, 0))
    weight_spec = pl.BlockSpec((features, 2 * HD), lambda i: (0, i))
    token_spec = pl.BlockSpec(
        (1, 2, tokens, 2 * HD), lambda i: (i // per_group, 0, 0, i % per_group)
    )
    kv_spec = pl.BlockSpec((spans, keys, 2 * HD), lambda i: (0, 0, i))
    score_spec = pl.BlockSpec((1, spans, keys, 2 * SPAN), lambda i: (i, 0, 0, 0))
    return pl.pallas_call(
        kernel,
        grid=(pairs,),
        in_specs=[whole, weight_spec, weight_spec, token_spec],
        out_specs=[
            kv_spec,
            kv_spec,
            score_spec,
            score_spec,
            pl.BlockSpec((1, 3, spans, 2 * SPAN), lambda i: (i, 0, 0, 0)),
        ],
        out_shape=[
            jax.ShapeDtypeStruct((spans, keys, all_width), BF),
            jax.ShapeDtypeStruct((spans, keys, all_width), BF),
            jax.ShapeDtypeStruct((pairs, spans, keys, 2 * SPAN), F32),
            jax.ShapeDtypeStruct((pairs, spans, keys, 2 * SPAN), F32),
            jax.ShapeDtypeStruct((pairs, 3, spans, 2 * SPAN), F32),
        ],
        scratch_shapes=[pltpu.VMEM((count * spans * piece_rows, features), BF)],
        compiler_params=PARAMS,
        cost_estimate=cost(
            4 * spans * keys * (features + SPAN) * all_width,
            8 * spans * keys * all_width,
            spans * keys * SPAN * 2 * pairs,
        ),
        name="score_spans",
    )(fetched, key_weight, value_weight, moved)


def blend_spans(scored, stats, key_weight, value_weight, moved, planes, columns):
    key_rows, value_rows, weights, grad_probs = scored
    features, all_width = key_weight.shape
    groups, _, tokens, width = moved.shape
    spans, keys, _ = key_rows.shape
    count = planes
    piece_rows = keys // count
    per_group = width // (2 * HD)
    pairs = all_width // (2 * HD)
    factor = HD ** (-0.5)
    devices = len(stats)

    def kernel(k_ref, v_ref, w_ref, gp_ref, *refs):
        stat_refs = refs[:devices]
        wk_ref, wv_ref, moved_ref, out_ref, part_ref, total, gk_ref, gv_ref = refs[devices:]
        step = pl.program_id(0)

        own_top = stat_refs[0][0, 0]
        top = own_top
        for ref in stat_refs[1:]:
            top = jnp.maximum(top, ref[0, 0])
        sums = jnp.zeros_like(top)
        inner = jnp.zeros_like(top)
        for ref in stat_refs:
            scale = jnp.exp(ref[0, 0] - top)
            sums = sums + ref[0, 1] * scale
            inner = inner + ref[0, 2] * scale
        scale = jnp.exp(own_top - top) / sums
        inner = inner / sums

        for span in range(spans):
            tok = pl.ds(span * SPAN, SPAN)
            probs = w_ref[0, span] * scale[span : span + 1]
            probs_b = probs.astype(BF)
            grad_scores = (
                probs * (gp_ref[0, span] - inner[span : span + 1]) * factor
            ).astype(BF)
            k, v = k_ref[span], v_ref[span]
            blended = matmul(probs_b, v, 0, 0)
            shifted_grad = matmul(grad_scores, k, 0, 0)
            out_ref[0, 0, tok, :HD] = blended[:SPAN, :HD].astype(BF)
            out_ref[0, 0, tok, HD:] = blended[SPAN:, HD:].astype(BF)
            out_ref[0, 1, tok, :HD] = shifted_grad[:SPAN, :HD].astype(BF)
            out_ref[0, 1, tok, HD:] = shifted_grad[SPAN:, HD:].astype(BF)
            gk = matmul(grad_scores, two_heads(moved_ref[0, 0, tok, :]))
            gv = matmul(probs_b, two_heads(moved_ref[0, 1, tok, :]))
            gk_ref[:, span] = gk.reshape(count, piece_rows, 2 * HD)
            gv_ref[:, span] = gv.reshape(count, piece_rows, 2 * HD)

        flat = (count * spans * piece_rows, 2 * HD)
        term = matmul(gk_ref[...].reshape(flat).astype(BF), wk_ref[...], 1, 1)
        term = term + matmul(gv_ref[...].reshape(flat).astype(BF), wv_ref[...], 1, 1)

        @pl.when(step == 0)
        def _():
            total[...] = term

        @pl.when(step > 0)
        def _():
            total[...] += term

        @pl.when(step == pairs - 1)
        def _():
            each = spans * piece_rows
            for part, start, end in cuts(features):
                for plane in range(count):
                    piece = total[plane * each : (plane + 1) * each, start:end].astype(BF)
                    part_ref[plane, part, :, : end - start] = piece
                    if end - start < PART:
                        blank = jnp.zeros((each, PART - end + start), BF)
                        part_ref[plane, part, :, end - start :] = blank

    weight_spec = pl.BlockSpec((features, 2 * HD), lambda i: (0, i))
    token_spec = pl.BlockSpec(
        (1, 2, tokens, 2 * HD), lambda i: (i // per_group, 0, 0, i % per_group)
    )
    kv_spec = pl.BlockSpec((spans, keys, 2 * HD), lambda i: (0, 0, i))
    score_spec = pl.BlockSpec((1, spans, keys, 2 * SPAN), lambda i: (i, 0, 0, 0))
    stat_spec = pl.BlockSpec((1, 3, spans, 2 * SPAN), lambda i: (i, 0, 0, 0))
    result = (count, columns, spans * piece_rows, PART)
    return pl.pallas_call(
        kernel,
        grid=(pairs,),
        in_specs=[kv_spec, kv_spec, score_spec, score_spec]
        + [stat_spec] * devices
        + [weight_spec, weight_spec, token_spec],
        out_specs=[token_spec, pl.BlockSpec(result, lambda i: (0, 0, 0, 0))],
        out_shape=[
            jax.ShapeDtypeStruct((groups, 2, tokens, width), BF),
            jax.ShapeDtypeStruct(result, BF),
        ],
        scratch_shapes=[
            pltpu.VMEM((count * spans * piece_rows, features), F32),
            pltpu.VMEM((count, spans, piece_rows, 2 * HD), F32),
            pltpu.VMEM((count, spans, piece_rows, 2 * HD), F32),
        ],
        compiler_params=PARAMS,
        cost_estimate=cost(
            4 * spans * keys * (features + 2 * SPAN) * all_width, 12 * spans * keys * all_width
        ),
        name="blend_spans",
    )(key_rows, value_rows, weights, grad_probs, *stats, key_weight, value_weight, moved)


def after(value, *others):
    return lax.optimization_barrier((value, *others))[0]


def shards(query, d_attended, encoded, key_weight, value_weight, nbr_shard, nbr_row):
    planes = lax.axis_size("z")
    columns = lax.axis_size("y")
    groups = lax.axis_size("x")
    c = lax.axis_index("c").astype(I32)
    spans, neighbours = nbr_shard.shape
    stored, quarter, features = encoded.shape
    lanes = planes * columns
    rows = lanes * stored
    requested = spans * neighbours

    pieces = split_pieces(encoded, planes, columns)
    store = lax.all_to_all(pieces, ("z", "y"), 0, 0, tiled=True).reshape(rows, PIECE * PART)

    moved = move_tokens([after(query, pieces), d_attended], True)
    moved = lax.all_gather(moved, "x")

    picks = (nbr_shard * stored + nbr_row).reshape(requested)
    picks = lax.all_gather(after(picks, pieces), ("z", "y", "c"), tiled=True)
    picks = picks.reshape(lanes, 2, requested)
    picks = jnp.stack([jnp.where(c == 0, picks[:, i], picks[:, 1 - i]) for i in range(2)])
    owner = picks // stored
    target = jnp.where(owner % 2 == c, owner // 2 * stored + picks % stored, -1)
    target = target.reshape(2, lanes * requested)

    theirs = pick_rows(store, target[1].reshape(-1, 1))
    picked = pick_rows(store, target[0].reshape(-1, 1), send_ring(theirs, "c", 1))
    picked = picked.reshape(lanes, requested * PIECE, PART)
    fetched = lax.all_to_all(picked, ("z", "y"), 0, 0, tiled=True)

    *scored, stat = score_spans(
        fetched.reshape(planes, columns, requested * PIECE, PART), key_weight, value_weight, moved
    )
    stats = [send_ring(stat, "x", away) for away in range(groups)]
    output, terms = blend_spans(scored, stats, key_weight, value_weight, moved, planes, columns)
    output = lax.psum_scatter(output, "x", scatter_dimension=0)

    terms = terms.reshape(lanes, requested * PIECE, PART)
    home = lax.all_to_all(terms, ("z", "y"), 0, 0, tiled=True)
    home = home.reshape(lanes * requested * PIECE, PART)
    sums = sum_rows([home, send_ring(home, "c", 1)], target.reshape(1, -1), rows)
    returned = sums.reshape(lanes, stored, PIECE * PART)
    returned = lax.all_to_all(returned, ("z", "y"), 0, 0, tiled=True)
    d_encoded = join_pieces(returned, planes, columns, quarter, features)
    attended, d_query = move_tokens([output], False)
    return (attended, d_query, d_encoded)


def solution(mesh):
    groups = mesh.devices.shape[1]
    fine = Mesh(mesh.devices.reshape(-1, 4, 2, groups), ("z", "y", "c", "x"))
    seq = ("z", "y", "c")
    placed = (
        P(seq, "x"),
        P(seq, "x"),
        P(seq, "x", None),
        P(),
        P(),
        P(seq, None),
        P(seq, None),
    )
    return jax.shard_map(
        shards,
        mesh=fine,
        in_specs=placed,
        out_specs=(P(seq, "x"), P(seq, "x"), P(seq, "x", None)),
        check_vma=False,
    )
```

profile of v0, /device:TPU:16, one launch (start us, length us, event | category | flops | bytes accessed | tf_op | source)
XLA Modules:
  0.0 268.3 jit_solution(690319340529826771)
XLA Ops:
  7.2 1.2 copy-done.1
  8.4 1.8 split_pieces.1
  10.2 1.9 move_tokens.2
  12.1 11.7 %all-to-all-start = ((bf16[32,16,1024]{2,1,0:T(8,128)(2,1)}), bf16[32,16,1024]{2,1,0:T(8,128)(2,1)S(1)}, u32[]{:S(2)}, u32[]{:S(2)}) async-start(bf16[32,16,1024]{2,1,0:T(8,128)(2,1)} %split_pieces.1), calls=%async_computation | async-start | bytes 2097152 | tf_op jit(solution)/shard_map/all_to_all | solution.py:409
  25.7 30.2 %all-reduce = s32[1664]{0:T(1024)S(1)} all-reduce(s32[1664]{0:T(1024)S(1)} %dynamic-update-slice), channel_id=1, replica_groups=mesh['z'=8,'y'=4,'c'=2,'x'=4] {'z','y','c'}, use_global_device_ids=true, to_apply=%add | all-reduce | flops 1664 | bytes 13312
  56.4 2.3 pick_rows.2
  58.9 3.6 %collective-permute-done.refs_0_ = bf16[832,1024]{1,0:T(8,128)(2,1)S(1)} collective-permute-done((bf16[832,1024]{1,0:T(8,128)(2,1)}, bf16[832,1024]{1,0:T(8,128)(2,1)S(1)}, u32[]{:S(2)}, u32[]{:S(2)}) %collective-permute-start) | collective-permute-done | bytes 1703968 | tf_op jit(solution)/shard_map/ppermute | solution.py:34
  62.5 2.1 pick_rows.3
  64.7 50.7 %all_to_all.20 = bf16[32,104,256]{2,1,0:T(8,128)(2,1)S(1)} all-to-all(bf16[32,104,256]{2,1,0:T(8,128)(2,1)S(1)} %bitcast.18), channel_id=1, replica_groups=mesh['z'=8,'y'=4,'c'=2,'x'=4] {'z','y'}, dimensions={0} | all-to-all | bytes 3407872 | tf_op jit(solution)/shard_map/all_to_all | solution.py:425
  115.3 17.2 %score_spans.1 = (bf16[13,64,2048]{2,1,0:T(8,128)(2,1)S(1)}, bf16[13,64,2048]{2,1,0:T(8,128)(2,1)}, f32[8,13,64,128]{3,2,1,0:T(8,128)}, f32[8,13,64,128]{3,2,1,0:T(8,128)}, f32[8,3,13,128]{3,2,1,0:T(8,128)S(1)}) custom-call(bf16[8,4,104,256]{3,2,1,0:T(8,128)(2,1)S(1)} %bitcast.25, bf16[896,2048]{1,0:T(8,128)(2,1)} %refs_4_.1, bf16[896,2048]{1,0:T(8,128)(2,1)} %refs_5_.1, ...), custom_call_target="tpu_custom_call" | custom-call | flops 6543114240 | bytes 13631488 | tf_op jit(solution)/shard_map/score_spans/pallas_call | solution.py:260
  132.6 2.8 %collective-permute-start.3 = (f32[8,3,13,128]{3,2,1,0:T(8,128)S(1)}, f32[8,3,13,128]{3,2,1,0:T(8,128)S(1)}, u32[]{:S(2)}, u32[]{:S(2)}) collective-permute-start(f32[8,3,13,128]{3,2,1,0:T(8,128)S(1)} %get-tuple-element.20.refs_0_), channel_id=1, source_target_pairs={{0,3},{1,0},{2,1},{3,2},{4,7},{5,4},{6,5},{7,6},{8,11},{9,8},{10,9... | collective-permute-start | bytes 479240 | tf_op jit(solution)/shard_map/ppermute | solution.py:34
  135.3 0.8 collective-permute-start.2
  136.1 0.9 collective-permute-start.1
  137.0 5.7 %collective-permute-done.3.refs_3_ = f32[8,3,13,128]{3,2,1,0:T(8,128)S(1)} collective-permute-done((f32[8,3,13,128]{3,2,1,0:T(8,128)S(1)}, f32[8,3,13,128]{3,2,1,0:T(8,128)S(1)}, u32[]{:S(2)}, u32[]{:S(2)}) %collective-permute-start.3) | collective-permute-done | bytes 159776 | tf_op jit(solution)/shard_map/ppermute | solution.py:34
  142.7 1.7 collective-permute-done.2.refs_2_
  144.4 2.0 collective-permute-done.1.refs_1_
  146.4 21.3 %blend_spans.1 = (bf16[4,2,832,512]{3,2,1,0:T(8,128)(2,1)}, bf16[8,4,104,256]{3,2,1,0:T(8,128)(2,1)S(1)}) custom-call(bf16[13,64,2048]{2,1,0:T(8,128)(2,1)S(1)} %get-tuple-element.16.k_ref, bf16[13,64,2048]{2,1,0:T(8,128)(2,1)} %get-tuple-element.17.v_ref, f32[8,13,64,128]{3,2,1,0:T(8,128)} %get-tuple-element.18.w_ref, ...), custom_call_target="tpu_custom_call" | custom-call | flops 6979321856 | bytes 20447232 | tf_op jit(solution)/shard_map/blend_spans/pallas_call | solution.py:369
  167.8 47.6 %all_to_all.21 = bf16[32,104,256]{2,1,0:T(8,128)(2,1)S(1)} all-to-all(bf16[32,104,256]{2,1,0:T(8,128)(2,1)S(1)} %bitcast.22), channel_id=1, replica_groups=mesh['z'=8,'y'=4,'c'=2,'x'=4] {'z','y'}, dimensions={0} | all-to-all | bytes 3407872 | tf_op jit(solution)/shard_map/all_to_all | solution.py:435
  215.7 3.3 %collective-permute-done.4.refs_1_ = bf16[3328,256]{1,0:T(8,128)(2,1)S(1)} collective-permute-done((bf16[3328,256]{1,0:T(8,128)(2,1)S(1)}, bf16[3328,256]{1,0:T(8,128)(2,1)S(1)}, u32[]{:S(2)}, u32[]{:S(2)}) %collective-permute-start.4) | collective-permute-done | bytes 1703968 | tf_op jit(solution)/shard_map/ppermute | solution.py:34
  219.0 3.9 %sum_rows.1 = bf16[512,1024]{1,0:T(8,128)(2,1)S(1)} custom-call(s32[1,1664]{1,0:T(1,128)S(1)} %compare_select_fusion.target_ref, bf16[3328,256]{1,0:T(8,128)(2,1)S(1)} %bitcast.24, bf16[3328,256]{1,0:T(8,128)(2,1)S(1)} %collective-permute-done.4.refs_1_), custom_call_target="tpu_custom_call" | custom-call | flops 1744830464 | bytes 4456448 | tf_op jit(solution)/shard_map/sum_rows/pallas_call | solution.py:157
  222.9 33.7 %all_to_all.22.part_ref = bf16[32,16,1024]{2,1,0:T(8,128)(2,1)S(1)} all-to-all(bf16[32,16,1024]{2,1,0:T(8,128)(2,1)S(1)} %bitcast.26), channel_id=1, replica_groups=mesh['z'=8,'y'=4,'c'=2,'x'=4] {'z','y'}, dimensions={0} | all-to-all | bytes 2097152 | tf_op jit(solution)/shard_map/all_to_all | solution.py:439
  256.7 1.7 join_pieces.1
  258.4 1.5 copy-done
  259.8 1.6 move_tokens.3
  (36 shorter events, 2.1 us)
Async XLA Ops:
  7.2 108.2 %all-gather.3.cloned.1.call-start = ((), (), s32[]{:S(2)}) async-start(), calls=%async_computation.6 | async-start | bytes 8519680 | tf_op jit(solution)/shard_map/all_gather | solution.py:412
  7.2 1.2 copy-start.1
  8.4 1.8 copy-start.2
  8.4 1.8 copy-start.3
  12.1 11.8 %copy-start.4 = (s32[13,2]{0,1:T(2,128)S(1)}, s32[13,2]{0,1:T(2,128)}, u32[]{:S(2)}) copy-start(s32[13,2]{0,1:T(2,128)} %param.13) | copy-start | bytes 316
  12.1 11.8 %copy-start.5 = (s32[13,2]{0,1:T(2,128)S(1)}, s32[13,2]{0,1:T(2,128)}, u32[]{:S(2)}) copy-start(s32[13,2]{0,1:T(2,128)} %param.12) | copy-start | bytes 316
  12.1 12.0 %copy-start.6 = (u32[256]{0:T(256)S(1)}, u32[256]{0:T(256)}, u32[]{:S(2)}) copy-start(u32[256]{0:T(256)} %constant.65) | copy-start | bytes 3076
  12.1 44.3 %all-to-all-start = ((bf16[32,16,1024]{2,1,0:T(8,128)(2,1)}), bf16[32,16,1024]{2,1,0:T(8,128)(2,1)S(1)}, u32[]{:S(2)}, u32[]{:S(2)}) async-start(bf16[32,16,1024]{2,1,0:T(8,128)(2,1)} %split_pieces.1), calls=%async_computation | async-start | bytes 2097152 | tf_op jit(solution)/shard_map/all_to_all | solution.py:409
  23.9 234.5 %reduce-scatter.2.cloned.1.call-start = ((), (), s32[]{:S(2)}) async-start(), calls=%async_computation.5 | async-start | bytes 8519680 | tf_op jit(solution)/shard_map/reduce_scatter | solution.py:432
  58.7 3.8 %collective-permute-start = (bf16[832,1024]{1,0:T(8,128)(2,1)}, bf16[832,1024]{1,0:T(8,128)(2,1)S(1)}, u32[]{:S(2)}, u32[]{:S(2)}) collective-permute-start(bf16[832,1024]{1,0:T(8,128)(2,1)} %pick_rows.2), channel_id=1, source_target_pairs={{0,4},{4,0},{1,5},{5,1},{2,6},{6,2},{3,7},{7,3},{8,12},{12,8},{9,1... | collective-permute-start | bytes 5111816 | tf_op jit(solution)/shard_map/ppermute | solution.py:34
  132.6 10.2 %collective-permute-start.3 = (f32[8,3,13,128]{3,2,1,0:T(8,128)S(1)}, f32[8,3,13,128]{3,2,1,0:T(8,128)S(1)}, u32[]{:S(2)}, u32[]{:S(2)}) collective-permute-start(f32[8,3,13,128]{3,2,1,0:T(8,128)S(1)} %get-tuple-element.20.refs_0_), channel_id=1, source_target_pairs={{0,3},{1,0},{2,1},{3,2},{4,7},{5,4},{6,5},{7,6},{8,11},{9,8},{10,9... | collective-permute-start | bytes 479240 | tf_op jit(solution)/shard_map/ppermute | solution.py:34
  135.3 9.1 %collective-permute-start.2 = (f32[8,3,13,128]{3,2,1,0:T(8,128)S(1)}, f32[8,3,13,128]{3,2,1,0:T(8,128)S(1)}, u32[]{:S(2)}, u32[]{:S(2)}) collective-permute-start(f32[8,3,13,128]{3,2,1,0:T(8,128)S(1)} %get-tuple-element.20.refs_0_), channel_id=1, source_target_pairs={{0,2},{1,3},{2,0},{3,1},{4,6},{5,7},{6,4},{7,5},{8,10},{9,11},{10,... | collective-permute-start | bytes 479240 | tf_op jit(solution)/shard_map/ppermute | solution.py:34
  136.1 10.3 %collective-permute-start.1 = (f32[8,3,13,128]{3,2,1,0:T(8,128)S(1)}, f32[8,3,13,128]{3,2,1,0:T(8,128)S(1)}, u32[]{:S(2)}, u32[]{:S(2)}) collective-permute-start(f32[8,3,13,128]{3,2,1,0:T(8,128)S(1)} %get-tuple-element.20.refs_0_), channel_id=1, source_target_pairs={{0,1},{1,2},{2,3},{3,0},{4,5},{5,6},{6,7},{7,4},{8,9},{9,10},{10,1... | collective-permute-start | bytes 479240 | tf_op jit(solution)/shard_map/ppermute | solution.py:34
  215.4 3.6 %collective-permute-start.4 = (bf16[3328,256]{1,0:T(8,128)(2,1)S(1)}, bf16[3328,256]{1,0:T(8,128)(2,1)S(1)}, u32[]{:S(2)}, u32[]{:S(2)}) collective-permute-start(bf16[3328,256]{1,0:T(8,128)(2,1)S(1)} %bitcast.23), channel_id=1, source_target_pairs={{0,4},{4,0},{1,5},{5,1},{2,6},{6,2},{3,7},{7,3},{8,12},{12,8},{9,1... | collective-permute-start | bytes 5111816 | tf_op jit(solution)/shard_map/ppermute | solution.py:34
  258.4 1.5 copy-start
Sparse Core Ops, SparseCore 0:
  12.2 75.3 all-gather.2
  167.9 65.3 reduce-scatter.1
where the time goes:
time: 269 us; the launch traced here: 268 us
  blocking collectives  162 us (60%)
  Pallas kernels  54 us (20%)
  waiting for transfers between devices  16.4 us (6%)
  starting transfers between devices  16.3 us (6%)
  between operations  14.9 us (6%)
  local copies, waits for them, and re-layouts  4.33 us (2%)
    all_to_all x1, blocking collectives, shards(): fetched = lax.all_to_all(picked, ('z', 'y'), 0, 0, tiled=True)  50.7 us
    all_to_all x1, blocking collectives, shards(): home = lax.all_to_all(terms, ('z', 'y'), 0, 0, tiled=True)  47.6 us
    all_to_all x1, blocking collectives, shards(): returned = lax.all_to_all(returned, ('z', 'y'), 0, 0, tiled=True)  33.7 us
    unnamed x1, blocking collectives  30.2 us
    pallas_call x1, Pallas kernels, blend_spans(): pl.pallas_call(kernel, grid=(pairs,), in_specs=[kv_spec, kv_spec, score_s...  21.3 us
    pallas_call x1, Pallas kernels, score_spans(): pl.pallas_call(kernel, grid=(pairs,), in_specs=[whole, weight_spec, weigh...  17.2 us
    ppermute x5, waiting for transfers between devices, send_ring(): lax.ppermute(array, axis, [(i, (i + step) % size) for i in range(size)])  16.4 us
    all_to_all x1, starting transfers between devices, shards(): lax.all_to_all(pieces, ('z', 'y'), 0, 0, tiled=True)  11.7 us
  transfers between devices with their start and end apart: 8, of which 5 were waited for; matrix products, arithmetic and copies ran while one was open for 1% of the time, Pallas kernels for 4%

commit v1 on v0

v1 whole, which is shorter than its diff:
```python
import jax
import jax.numpy as jnp
from jax import lax
from jax.experimental import pallas as pl
from jax.experimental.pallas import tpu as pltpu
from jax.sharding import Mesh, PartitionSpec as P

HD = 128
SPAN = 64
NBRS = 2
SPARE = 128
BF = jnp.bfloat16
F32 = jnp.float32
I32 = jnp.int32
PARAMS = pltpu.CompilerParams(vmem_limit_bytes=48 * 1024 * 1024)


def matmul(left, right, left_dim=1, right_dim=0):
    return lax.dot_general(
        left, right, (((left_dim,), (right_dim,)), ((), ())), preferred_element_type=F32
    )


def cost(flops, bytes_accessed, transcendentals=0):
    return pl.CostEstimate(
        flops=int(flops), bytes_accessed=int(bytes_accessed), transcendentals=int(transcendentals)
    )


def send_ring(array, axis, step):
    size = lax.axis_size(axis)
    if step % size == 0:
        return array
    return lax.ppermute(array, axis, [(i, (i + step) % size) for i in range(size)])


def piece_matrix(stored, quarter):
    shape = (stored * quarter, stored * quarter)
    to = lax.broadcasted_iota(I32, shape, 0)
    source = lax.broadcasted_iota(I32, shape, 1)
    token = to % stored * quarter + to // stored
    return (source == token).astype(F32).astype(BF)


def split_pieces(encoded, nbr_shard, nbr_row):
    stored, quarter, features = encoded.shape
    size = stored * quarter
    spans, neighbours = nbr_shard.shape

    def kernel(enc_ref, shard_ref, row_ref, out_ref, names):
        names[...] = jnp.zeros_like(names)
        names[:spans, :neighbours] = shard_ref[...].astype(F32)
        names[:spans, neighbours : 2 * neighbours] = row_ref[...].astype(F32)
        named = names[...].astype(BF)
        pieces = matmul(piece_matrix(stored, quarter), enc_ref[...]).astype(BF)
        for token in range(quarter):
            out_ref[token, :, :features] = pieces[token * stored : (token + 1) * stored]
            out_ref[token, :, features:] = named

    return pl.pallas_call(
        kernel,
        out_shape=jax.ShapeDtypeStruct((quarter, stored, features + SPARE), BF),
        scratch_shapes=[pltpu.VMEM((stored, SPARE), F32)],
        compiler_params=PARAMS,
        cost_estimate=cost(2 * size * size * features, 4 * size * features),
        name="split_pieces",
    )(encoded.reshape(size, features), nbr_shard, nbr_row)


def join_pieces(parts):
    quarter, stored, features = parts.shape
    size = stored * quarter

    def kernel(part_ref, out_ref):
        out_ref[...] = matmul(piece_matrix(stored, quarter), part_ref[...], 0, 0).astype(BF)

    joined = pl.pallas_call(
        kernel,
        out_shape=jax.ShapeDtypeStruct((size, features), BF),
        compiler_params=PARAMS,
        cost_estimate=cost(2 * size * size * features, 4 * size * features),
        name="join_pieces",
    )(parts.reshape(size, features))
    return joined.reshape(stored, quarter, features)


def message_rows(picks, blocks):
    return -(-picks * blocks // 8) * 8


def pick_rows(stores, target, lanes, picks, features):
    rows = stores[0].shape[0]
    each = target.shape[0] // lanes
    blocks = features // HD
    length = message_rows(picks, blocks)

    def kernel(target_ref, own_ref, other_ref, out_ref, spread):
        column = lax.broadcasted_iota(I32, (lanes * each, rows), 1)
        own_hot = (column == target_ref[...]).astype(F32).astype(BF)
        other_hot = (column == target_ref[...] - rows).astype(F32).astype(BF)
        spread[:, length - 8 :, :] = jnp.zeros((lanes, 8, HD), F32)
        for block in range(blocks):
            cols = slice(block * HD, (block + 1) * HD)
            total = matmul(own_hot, own_ref[:, cols]) + matmul(other_hot, other_ref[:, cols])
            for lane in range(lanes):
                part = total[lane * each : lane * each + picks]
                spread[lane, pl.ds(block, picks, stride=blocks), :] = part
        out_ref[...] = spread[...].astype(BF)

    return pl.pallas_call(
        kernel,
        out_shape=jax.ShapeDtypeStruct((lanes, length, HD), BF),
        scratch_shapes=[pltpu.VMEM((lanes, length, HD), F32)],
        compiler_params=PARAMS,
        cost_estimate=cost(
            4 * lanes * each * rows * features, 2 * (lanes * each + 2 * rows) * features
        ),
        name="pick_rows",
    )(target, *stores)


def sum_rows(terms, target, picks, rows, features):
    count = len(terms)
    lanes, length, _ = terms[0].shape
    each = target.shape[1] // (count * lanes)
    blocks = features // HD
    size = count * lanes * each

    def kernel(target_ref, *refs):
        out_ref, spread, flat = refs[count:]
        row = lax.broadcasted_iota(I32, (rows, size), 0)
        one_hot = (row == target_ref[...]).astype(F32).astype(BF)
        for which in range(count):
            spread[which] = refs[which][...].astype(F32)
        for lane in range(count * lanes):
            low = lane * each + picks // 8 * 8
            flat[low : (lane + 1) * each, :] = jnp.zeros(((lane + 1) * each - low, HD), F32)
        for block in range(blocks):
            for which in range(count):
                for lane in range(lanes):
                    at = (which * lanes + lane) * each
                    flat[at : at + picks, :] = spread[
                        which, lane, pl.ds(block, picks, stride=blocks), :
                    ]
            total = matmul(one_hot, flat[...].astype(BF))
            out_ref[:, block * HD : (block + 1) * HD] = total.astype(BF)

    return pl.pallas_call(
        kernel,
        out_shape=jax.ShapeDtypeStruct((rows, features), BF),
        scratch_shapes=[pltpu.VMEM((count, lanes, length, HD), F32), pltpu.VMEM((size, HD), F32)],
        compiler_params=PARAMS,
        cost_estimate=cost(2 * size * rows * features, 2 * (size + rows) * features),
        name="sum_rows",
    )(target, *terms)


def move_tokens(arrays, forward):
    tokens, width = arrays[0].shape[-2:]
    spans = tokens // SPAN
    packed = jax.ShapeDtypeStruct((2, tokens, width), BF)
    apart = [jax.ShapeDtypeStruct((tokens, width), BF)] * 2

    def kernel(*refs):
        to = lax.broadcasted_iota(I32, (SPAN, 2 * SPAN), 0)
        source = lax.broadcasted_iota(I32, (SPAN, 2 * SPAN), 1)
        step = SPAN - 1 if forward else 1
        order = (source == to + step).astype(F32).astype(BF)
        blank = jnp.zeros((SPAN, width), BF)
        pack = refs[-1] if forward else refs[0]
        for which, ref in enumerate(refs[:2] if forward else refs[1:]):
            for span in range(spans):
                low = span if forward else span - 1
                pair = []
                for u in (low, low + 1):
                    if not 0 <= u < spans:
                        pair.append(blank)
                    elif forward:
                        pair.append(ref[u * SPAN : (u + 1) * SPAN])
                    else:
                        pair.append(pack[which, u * SPAN : (u + 1) * SPAN])
                moved = matmul(order, jnp.concatenate(pair, 0)).astype(BF)
                if forward:
                    pack[which, span * SPAN : (span + 1) * SPAN] = moved
                else:
                    ref[span * SPAN : (span + 1) * SPAN] = moved

    return pl.pallas_call(
        kernel,
        out_shape=packed if forward else apart,
        compiler_params=PARAMS,
        cost_estimate=cost(8 * tokens * SPAN * width, 8 * tokens * width),
        name="move_tokens",
    )(*arrays)


def two_heads(pair):
    column = lax.broadcasted_iota(I32, (2 * SPAN, 2 * HD), 1)
    row = lax.broadcasted_iota(I32, (2 * SPAN, 2 * HD), 0)
    mask = ((column < HD) == (row < SPAN)).astype(F32).astype(BF)
    return jnp.concatenate([pair, pair], 0) * mask


def score_spans(fetched, key_weight, value_weight, moved):
    lanes = fetched.shape[0]
    features, all_width = key_weight.shape
    groups, _, tokens, width = moved.shape
    spans = tokens // SPAN
    keys = lanes * NBRS
    count = keys // 8
    blocks = features // HD
    per_group = width // (2 * HD)
    pairs = all_width // (2 * HD)
    factor = HD ** (-0.5)

    def kernel(
        part_ref,
        wk_ref,
        wv_ref,
        moved_ref,
        k_ref,
        v_ref,
        w_ref,
        gp_ref,
        stat_ref,
        rows_ref,
        spread,
        flat,
    ):
        @pl.when(pl.program_id(0) == 0)
        def _():
            spread[...] = part_ref[...].astype(F32)
            for block in range(blocks):
                for lane in range(lanes):
                    for nbr in range(NBRS):
                        to = lane * NBRS // 8 * 8 * spans + lane * NBRS % 8 + nbr
                        flat[pl.ds(to, spans, stride=8), :] = spread[
                            lane, pl.ds(nbr * blocks + block, spans, stride=NBRS * blocks), :
                        ]
                rows_ref[:, block * HD : (block + 1) * HD] = flat[...].astype(BF)

        rows = rows_ref[...]

        def project(weight):
            out = matmul(rows, weight).reshape(count, spans, 8, 2 * HD)
            return out.transpose(1, 0, 2, 3).reshape(spans, keys, 2 * HD).astype(BF)

        k_ref[...] = project(wk_ref[...])
        v_ref[...] = project(wv_ref[...])
        for span in range(spans):
            tok = pl.ds(span * SPAN, SPAN)
            scores = matmul(k_ref[span], two_heads(moved_ref[0, 0, tok, :]), 1, 1) * factor
            grad = matmul(v_ref[span], two_heads(moved_ref[0, 1, tok, :]), 1, 1)
            top = jnp.max(scores, axis=0, keepdims=True)
            weights = jnp.exp(scores - top)
            w_ref[0, span] = weights
            gp_ref[0, span] = grad
            stat_ref[0, 0, pl.ds(span, 1), :] = top
            stat_ref[0, 1, pl.ds(span, 1), :] = jnp.sum(weights, axis=0, keepdims=True)
            stat_ref[0, 2, pl.ds(span, 1), :] = jnp.sum(weights * grad, axis=0, keepdims=True)

    whole = pl.BlockSpec(fetched.shape, lambda i: (0, 0, 0))
    weight_spec = pl.BlockSpec((features, 2 * HD), lambda i: (0, i))
    token_spec = pl.BlockSpec(
        (1, 2, tokens, 2 * HD), lambda i: (i // per_group, 0, 0, i % per_group)
    )
    kv_spec = pl.BlockSpec((spans, keys, 2 * HD), lambda i: (0, 0, i))
    score_spec = pl.BlockSpec((1, spans, keys, 2 * SPAN), lambda i: (i, 0, 0, 0))
    return pl.pallas_call(
        kernel,
        grid=(pairs,),
        in_specs=[whole, weight_spec, weight_spec, token_spec],
        out_specs=[
            kv_spec,
            kv_spec,
            score_spec,
            score_spec,
            pl.BlockSpec((1, 3, spans, 2 * SPAN), lambda i: (i, 0, 0, 0)),
        ],
        out_shape=[
            jax.ShapeDtypeStruct((spans, keys, all_width), BF),
            jax.ShapeDtypeStruct((spans, keys, all_width), BF),
            jax.ShapeDtypeStruct((pairs, spans, keys, 2 * SPAN), F32),
            jax.ShapeDtypeStruct((pairs, spans, keys, 2 * SPAN), F32),
            jax.ShapeDtypeStruct((pairs, 3, spans, 2 * SPAN), F32),
        ],
        scratch_shapes=[
            pltpu.VMEM((spans * keys, features), BF),
            pltpu.VMEM(fetched.shape, F32),
            pltpu.VMEM((spans * keys, HD), F32),
        ],
        compiler_params=PARAMS,
        cost_estimate=cost(
            4 * spans * keys * (features + SPAN) * all_width,
            8 * spans * keys * all_width,
            spans * keys * SPAN * 2 * pairs,
        ),
        name="score_spans",
    )(fetched, key_weight, value_weight, moved)


def blend_spans(scored, stats, key_weight, value_weight, moved):
    key_rows, value_rows, weights, grad_probs = scored
    features, all_width = key_weight.shape
    groups, _, tokens, width = moved.shape
    spans, keys, _ = key_rows.shape
    count = keys // 8
    lanes = keys // NBRS
    blocks = features // HD
    per_group = width // (2 * HD)
    pairs = all_width // (2 * HD)
    factor = HD ** (-0.5)
    devices = len(stats)

    def kernel(k_ref, v_ref, w_ref, gp_ref, *refs):
        stat_refs = refs[:devices]
        wk_ref, wv_ref, moved_ref, out_ref, part_ref = refs[devices : devices + 5]
        total, gk_ref, gv_ref, spread = refs[devices + 5 :]
        step = pl.program_id(0)

        own_top = stat_refs[0][0, 0]
        top = own_top
        for ref in stat_refs[1:]:
            top = jnp.maximum(top, ref[0, 0])
        sums = jnp.zeros_like(top)
        inner = jnp.zeros_like(top)
        for ref in stat_refs:
            scale = jnp.exp(ref[0, 0] - top)
            sums = sums + ref[0, 1] * scale
            inner = inner + ref[0, 2] * scale
        scale = jnp.exp(own_top - top) / sums
        inner = inner / sums

        for span in range(spans):
            tok = pl.ds(span * SPAN, SPAN)
            probs = w_ref[0, span] * scale[span : span + 1]
            probs_b = probs.astype(BF)
            grad_scores = (
                probs * (gp_ref[0, span] - inner[span : span + 1]) * factor
            ).astype(BF)
            k, v = k_ref[span], v_ref[span]
            blended = matmul(probs_b, v, 0, 0)
            shifted_grad = matmul(grad_scores, k, 0, 0)
            out_ref[0, 0, tok, :HD] = blended[:SPAN, :HD].astype(BF)
            out_ref[0, 0, tok, HD:] = blended[SPAN:, HD:].astype(BF)
            out_ref[0, 1, tok, :HD] = shifted_grad[:SPAN, :HD].astype(BF)
            out_ref[0, 1, tok, HD:] = shifted_grad[SPAN:, HD:].astype(BF)
            gk = matmul(grad_scores, two_heads(moved_ref[0, 0, tok, :]))
            gv = matmul(probs_b, two_heads(moved_ref[0, 1, tok, :]))
            gk_ref[:, span] = gk.reshape(count, 8, 2 * HD)
            gv_ref[:, span] = gv.reshape(count, 8, 2 * HD)

        flat = (spans * keys, 2 * HD)
        term = matmul(gk_ref[...].reshape(flat).astype(BF), wk_ref[...], 1, 1)
        term = term + matmul(gv_ref[...].reshape(flat).astype(BF), wv_ref[...], 1, 1)

        @pl.when(step == 0)
        def _():
            for block in range(blocks):
                total[block] = term[:, block * HD : (block + 1) * HD]

        @pl.when(step > 0)
        def _():
            for block in range(blocks):
                total[block] += term[:, block * HD : (block + 1) * HD]

        @pl.when(step == pairs - 1)
        def _():
            spread[:, length - 8 :, :] = jnp.zeros((lanes, 8, HD), F32)
            for block in range(blocks):
                for lane in range(lanes):
                    for nbr in range(NBRS):
                        at = lane * NBRS // 8 * 8 * spans + lane * NBRS % 8 + nbr
                        to = pl.ds(nbr * blocks + block, spans, stride=NBRS * blocks)
                        spread[lane, to, :] = total[block, pl.ds(at, spans, stride=8), :]
            part_ref[...] = spread[...].astype(BF)

    weight_spec = pl.BlockSpec((features, 2 * HD), lambda i: (0, i))
    token_spec = pl.BlockSpec(
        (1, 2, tokens, 2 * HD), lambda i: (i // per_group, 0, 0, i % per_group)
    )
    kv_spec = pl.BlockSpec((spans, keys, 2 * HD), lambda i: (0, 0, i))
    score_spec = pl.BlockSpec((1, spans, keys, 2 * SPAN), lambda i: (i, 0, 0, 0))
    stat_spec = pl.BlockSpec((1, 3, spans, 2 * SPAN), lambda i: (i, 0, 0, 0))
    length = message_rows(spans * NBRS, blocks)
    result = (lanes, length, HD)
    return pl.pallas_call(
        kernel,
        grid=(pairs,),
        in_specs=[kv_spec, kv_spec, score_spec, score_spec]
        + [stat_spec] * devices
        + [weight_spec, weight_spec, token_spec],
        out_specs=[token_spec, pl.BlockSpec(result, lambda i: (0, 0, 0))],
        out_shape=[
            jax.ShapeDtypeStruct((groups, 2, tokens, width), BF),
            jax.ShapeDtypeStruct(result, BF),
        ],
        scratch_shapes=[
            pltpu.VMEM((blocks, spans * keys, HD), F32),
            pltpu.VMEM((count, spans, 8, 2 * HD), F32),
            pltpu.VMEM((count, spans, 8, 2 * HD), F32),
            pltpu.VMEM(result, F32),
        ],
        compiler_params=PARAMS,
        cost_estimate=cost(
            4 * spans * keys * (features + 2 * SPAN) * all_width, 12 * spans * keys * all_width
        ),
        name="blend_spans",
    )(key_rows, value_rows, weights, grad_probs, *stats, key_weight, value_weight, moved)


def after(value, *others):
    return lax.optimization_barrier((value, *others))[0]


def shards(query, d_attended, encoded, key_weight, value_weight, nbr_shard, nbr_row):
    lanes = lax.axis_size(("z", "y"))
    groups = lax.axis_size("x")
    c = lax.axis_index("c").astype(I32)
    spans, neighbours = nbr_shard.shape
    stored, quarter, features = encoded.shape
    rows = lanes * stored
    picks = spans * neighbours

    pieces = split_pieces(encoded, nbr_shard, nbr_row)
    store = lax.all_to_all(pieces, ("z", "y"), 0, 0, tiled=True).reshape(rows, features + SPARE)

    moved = move_tokens([after(query, pieces), d_attended], True)
    moved = lax.all_gather(moved, "x")

    stores = [store, send_ring(store, "c", 1)]
    live = (jnp.arange(stored) < spans)[None, :, None]

    def places(held):
        named = held[:, features : features + 2 * neighbours].astype(I32)
        named = named.reshape(lanes, stored, 2 * neighbours)
        owner, row = named[..., :neighbours], named[..., neighbours:]
        place = owner // 2 * stored + row
        return place, owner % 2 == c, live

    place, here, valid = places(stores[0])
    target = jnp.where(valid, jnp.where(here, place, place + rows), -1)
    picked = pick_rows(stores, target.reshape(-1, 1), lanes, picks, features)
    fetched = lax.all_to_all(picked, ("z", "y"), 0, 0, tiled=True)

    *scored, stat = score_spans(fetched, key_weight, value_weight, moved)
    stats = [send_ring(stat, "x", away) for away in range(groups)]
    output, terms = blend_spans(scored, stats, key_weight, value_weight, moved)
    output = lax.psum_scatter(output, "x", scatter_dimension=0)

    home = lax.all_to_all(terms, ("z", "y"), 0, 0, tiled=True)
    target = []
    for held in stores:
        place, here, valid = places(held)
        target.append(jnp.where(valid & here, place, -1).reshape(1, -1))
    target = jnp.concatenate(target, 1)
    sums = sum_rows([home, send_ring(home, "c", 1)], target, picks, rows, features)
    returned = sums.reshape(lanes, stored, features)
    returned = lax.all_to_all(returned, ("z", "y"), 0, 0, tiled=True)
    attended, d_query = move_tokens([output], False)
    d_encoded = join_pieces(after(returned, attended))
    return (attended, d_query, d_encoded)


def solution(mesh):
    groups = mesh.devices.shape[1]
    fine = Mesh(mesh.devices.reshape(-1, 4, 2, groups), ("z", "y", "c", "x"))
    seq = ("z", "y", "c")
    placed = (
        P(seq, "x"),
        P(seq, "x"),
        P(seq, "x", None),
        P(),
        P(),
        P(seq, None),
        P(seq, None),
    )
    return jax.shard_map(
        shards,
        mesh=fine,
        in_specs=placed,
        out_specs=(P(seq, "x"), P(seq, "x"), P(seq, "x", None)),
        check_vma=False,
    )
```

time: 269 us -> 253 us (0.941)
  blocking collectives: 162 us -> 127 us
  waiting for transfers between devices: 16.4 us -> 37 us
  starting transfers between devices: 16.3 us -> 10.1 us
  local copies, waits for them, and re-layouts: 4.33 us -> 7.96 us
    unnamed x1 -> x0, blocking collectives: 30.2 us -> none
    all_to_all x1, waiting for transfers between devices: 0.01 us -> 14.8 us  [shards(): returned = lax.all_to_all(returned, ('z', 'y'), 0, 0, tiled=True)]
    reduce_scatter x1, waiting for transfers between devices: 0.01 us -> 7.63 us  [shards(): output = lax.psum_scatter(output, 'x', scatter_dimension=0)]
    all_to_all x1, blocking collectives: 50.7 us -> 43.6 us  [shards(): fetched = lax.all_to_all(picked, ('z', 'y'), 0, 0, tiled=True)]
    all_to_all x1, starting transfers between devices: 11.7 us -> 5.57 us  [shards(): returned = lax.all_to_all(returned, ('z', 'y'), 0, 0, tiled=True)]
    all_to_all x1, blocking collectives: 33.7 us -> 39.4 us  [shards(): lax.all_to_all(pieces, ('z', 'y'), 0, 0, tiled=True)]
    all_to_all x1, blocking collectives: 47.6 us -> 43.7 us  [shards(): home = lax.all_to_all(terms, ('z', 'y'), 0, 0, tiled=True)]
    unnamed x17 -> x12, local copies, waits for them, and re-layouts: 3.51 us -> 7.39 us
  transfers between devices with their start and end apart: 8 -> 8, of which waited for: 5 -> 7; matrix products, arithmetic and copies ran while one was open for 1% -> 1% of each run, Pallas kernels for 4% -> 4%
where the time goes in v1:
time: 253 us; the launch traced here: 252 us
  blocking collectives  127 us (50%)
  Pallas kernels  55.1 us (22%)
  waiting for transfers between devices  37 us (15%)
  between operations  14.2 us (6%)
  starting transfers between devices  10.1 us (4%)
  local copies, waits for them, and re-layouts  7.96 us (3%)
    all_to_all x1, blocking collectives, shards(): home = lax.all_to_all(terms, ('z', 'y'), 0, 0, tiled=True)  43.7 us
    all_to_all x1, blocking collectives, shards(): fetched = lax.all_to_all(picked, ('z', 'y'), 0, 0, tiled=True)  43.6 us
    all_to_all x1, blocking collectives, shards(): lax.all_to_all(pieces, ('z', 'y'), 0, 0, tiled=True)  39.4 us
    pallas_call x1, Pallas kernels, blend_spans(): pl.pallas_call(kernel, grid=(pairs,), in_specs=[kv_spec, kv_spec, score_s...  22.1 us
    pallas_call x1, Pallas kernels, score_spans(): pl.pallas_call(kernel, grid=(pairs,), in_specs=[whole, weight_spec, weigh...  18.2 us
    all_to_all x1, waiting for transfers between devices, shards(): returned = lax.all_to_all(returned, ('z', 'y'), 0, 0, tiled=True)  14.8 us
    ppermute x5, waiting for transfers between devices, send_ring(): lax.ppermute(array, axis, [(i, (i + step) % size) for i in range(size)])  14.5 us
    reduce_scatter x1, waiting for transfers between devices, shards(): output = lax.psum_scatter(output, 'x', scatter_dimension=0)  7.63 us
  transfers between devices with their start and end apart: 8, of which 7 were waited for; matrix products, arithmetic and copies ran while one was open for 1% of the time, Pallas kernels for 4%

profile of v1, /device:TPU:16, one launch (start us, length us, event | category | flops | bytes accessed | tf_op | source)
XLA Modules:
  0.0 251.9 jit_solution(3439862325205606991)
XLA Ops:
  8.7 1.2 copy-done.2
  10.7 1.1 copy-done.3
  11.8 1.2 copy-done.4
  13.0 1.9 move_tokens.2
  14.9 39.4 %all_to_all.20 = bf16[32,16,1024]{2,1,0:T(8,128)(2,1)S(1)} all-to-all(bf16[32,16,1024]{2,1,0:T(8,128)(2,1)S(1)} %split_pieces.1), channel_id=1, replica_groups=mesh['z'=8,'y'=4,'c'=2,'x'=4] {'z','y'}, dimensions={0} | all-to-all | bytes 2097152 | tf_op jit(solution)/shard_map/all_to_all | solution.py:426
  54.8 2.2 collective-permute-done.other_ref
  57.8 4.1 %pick_rows.1 = bf16[32,184,128]{2,1,0:T(8,128)(2,1)S(1)} custom-call(s32[1024,1]{1,0:T(8,128)S(1)} %reshape.64.target_ref, bf16[512,1024]{1,0:T(8,128)(2,1)S(1)} %bitcast.15, bf16[512,1024]{1,0:T(8,128)(2,1)S(1)} %collective-permute-done.other_ref), custom_call_target="tpu_custom_call" | custom-call | flops 1879048192 | bytes 3670016 | tf_op jit(solution)/shard_map/pick_rows/pallas_call | solution.py:110
  62.0 43.6 %all_to_all.21.part_ref = bf16[32,184,128]{2,1,0:T(8,128)(2,1)S(1)} all-to-all(bf16[32,184,128]{2,1,0:T(8,128)(2,1)S(1)} %pick_rows.1), channel_id=1, replica_groups=mesh['z'=8,'y'=4,'c'=2,'x'=4] {'z','y'}, dimensions={0} | all-to-all | bytes 3014656 | tf_op jit(solution)/shard_map/all_to_all | solution.py:444
  105.5 18.2 %score_spans.1 = (bf16[13,64,2048]{2,1,0:T(8,128)(2,1)S(1)}, bf16[13,64,2048]{2,1,0:T(8,128)(2,1)}, f32[8,13,64,128]{3,2,1,0:T(8,128)}, f32[8,13,64,128]{3,2,1,0:T(8,128)}, f32[8,3,13,128]{3,2,1,0:T(8,128)S(1)}) custom-call(bf16[32,184,128]{2,1,0:T(8,128)(2,1)S(1)} %all_to_all.21.part_ref, bf16[896,2048]{1,0:T(8,128)(2,1)} %refs_4_.1, ...), custom_call_target="tpu_custom_call" | custom-call | flops 6543114240 | bytes 13631488 | tf_op jit(solution)/shard_map/score_spans/pallas_call | solution.py:269
  123.7 2.8 %collective-permute-start.3 = (f32[8,3,13,128]{3,2,1,0:T(8,128)S(1)}, f32[8,3,13,128]{3,2,1,0:T(8,128)S(1)}, u32[]{:S(2)}, u32[]{:S(2)}) collective-permute-start(f32[8,3,13,128]{3,2,1,0:T(8,128)S(1)} %get-tuple-element.19.refs_0_), channel_id=1, source_target_pairs={{0,3},{1,0},{2,1},{3,2},{4,7},{5,4},{6,5},{7,6},{8,11},{9,8},{10,9... | collective-permute-start | bytes 479240 | tf_op jit(solution)/shard_map/ppermute | solution.py:34
  128.1 5.6 %collective-permute-done.3.refs_3_ = f32[8,3,13,128]{3,2,1,0:T(8,128)S(1)} collective-permute-done((f32[8,3,13,128]{3,2,1,0:T(8,128)S(1)}, f32[8,3,13,128]{3,2,1,0:T(8,128)S(1)}, u32[]{:S(2)}, u32[]{:S(2)}) %collective-permute-start.3) | collective-permute-done | bytes 159776 | tf_op jit(solution)/shard_map/ppermute | solution.py:34
  133.7 1.7 collective-permute-done.2.refs_2_
  135.4 2.0 collective-permute-done.1.refs_1_
  137.4 22.1 %blend_spans.1 = (bf16[4,2,832,512]{3,2,1,0:T(8,128)(2,1)}, bf16[32,184,128]{2,1,0:T(8,128)(2,1)S(1)}) custom-call(bf16[13,64,2048]{2,1,0:T(8,128)(2,1)S(1)} %get-tuple-element.15.k_ref, bf16[13,64,2048]{2,1,0:T(8,128)(2,1)} %get-tuple-element.16.v_ref, f32[8,13,64,128]{3,2,1,0:T(8,128)} %get-tuple-element.17.w_ref, ...), custom_call_target="tpu_custom_call" | custom-call | flops 6979321856 | bytes 20447232 | tf_op jit(solution)/shard_map/blend_spans/pallas_call | solution.py:387
  159.6 43.7 %all_to_all.22.refs_0_ = bf16[32,184,128]{2,1,0:T(8,128)(2,1)S(1)} all-to-all(bf16[32,184,128]{2,1,0:T(8,128)(2,1)S(1)} %get-tuple-element.23), channel_id=1, replica_groups=mesh['z'=8,'y'=4,'c'=2,'x'=4] {'z','y'}, dimensions={0} | all-to-all | bytes 3014656 | tf_op jit(solution)/shard_map/all_to_all | solution.py:451
  203.7 2.9 %collective-permute-done.4.refs_1_ = bf16[32,184,128]{2,1,0:T(8,128)(2,1)S(1)} collective-permute-done((bf16[32,184,128]{2,1,0:T(8,128)(2,1)S(1)}, bf16[32,184,128]{2,1,0:T(8,128)(2,1)S(1)}, u32[]{:S(2)}, u32[]{:S(2)}) %collective-permute-start.4) | collective-permute-done | bytes 1507360 | tf_op jit(solution)/shard_map/ppermute | solution.py:34
  206.6 4.7 %sum_rows.1 = bf16[512,896]{1,0:T(8,128)(2,1)S(1)} custom-call(s32[1,2048]{1,0:T(1,128)S(1)} %pad_add_fusion.target_ref, bf16[32,184,128]{2,1,0:T(8,128)(2,1)S(1)} %all_to_all.22.refs_0_, bf16[32,184,128]{2,1,0:T(8,128)(2,1)S(1)} %collective-permute-done.4.refs_1_), custom_call_target="tpu_custom_call" | custom-call | flops 1879048192 | bytes 4587520 | tf_op jit(solution)/shard_map/sum_rows/pallas_call | solution.py:148
  211.3 0.9 copy-done.1
  212.2 5.6 %all-to-all-start.3 = ((bf16[32,16,896]{2,1,0:T(8,128)(2,1)}), bf16[32,16,896]{2,1,0:T(8,128)(2,1)S(1)}, u32[]{:S(2)}, u32[]{:S(2)}) async-start(bf16[32,16,896]{2,1,0:T(8,128)(2,1)} %bitcast.16), calls=%async_computation.4 | async-start | bytes 1835008 | tf_op jit(solution)/shard_map/all_to_all | solution.py:459
  217.8 7.6 %reduce-scatter.2.cloned.1.call-done = bf16[1,2,832,512]{3,2,1,0:T(8,128)(2,1)} async-done(((bf16[4,2,832,512]{3,2,1,0:T(8,128)(2,1)}), bf16[1,2,832,512]{3,2,1,0:T(8,128)(2,1)}) %reduce-scatter.2.cloned.1.call-update) | async-done | bytes 1703952 | tf_op jit(solution)/shard_map/reduce_scatter | solution.py:449
  225.4 1.5 copy-done
  226.9 1.6 move_tokens.3
  228.5 14.8 %all-to-all-done.3 = bf16[32,16,896]{2,1,0:T(8,128)(2,1)S(1)} async-done(((bf16[32,16,896]{2,1,0:T(8,128)(2,1)}), bf16[32,16,896]{2,1,0:T(8,128)(2,1)S(1)}, u32[]{:S(2)}, u32[]{:S(2)}) %all-to-all-start.3) | async-done | bytes 917536 | tf_op jit(solution)/shard_map/all_to_all | solution.py:459
  243.4 1.7 join_pieces.1
  (28 shorter events, 5.6 us)
Async XLA Ops:
  7.2 98.4 %all-gather.3.cloned.1.call-start = ((), (), s32[]{:S(2)}) async-start(), calls=%async_computation.6 | async-start | bytes 8519680 | tf_op jit(solution)/shard_map/all_gather | solution.py:429
  8.7 1.2 copy-start.2
  10.7 1.2 copy-start.3
  11.8 1.2 copy-start.4
  14.9 210.5 %reduce-scatter.2.cloned.1.call-start = ((), (), s32[]{:S(2)}) async-start(), calls=%async_computation.5 | async-start | bytes 8519680 | tf_op jit(solution)/shard_map/reduce_scatter | solution.py:449
  54.4 2.7 %collective-permute-start = (bf16[512,1024]{1,0:T(8,128)(2,1)S(1)}, bf16[512,1024]{1,0:T(8,128)(2,1)S(1)}, u32[]{:S(2)}, u32[]{:S(2)}) collective-permute-start(bf16[512,1024]{1,0:T(8,128)(2,1)S(1)} %bitcast.13), channel_id=1, source_target_pairs={{0,4},{4,0},{1,5},{5,1},{2,6},{6,2},{3,7},{7,3},{8,12},{12,8},{9,1... | collective-permute-start | bytes 3145736 | tf_op jit(solution)/shard_map/ppermute | solution.py:34
  123.7 10.0 %collective-permute-start.3 = (f32[8,3,13,128]{3,2,1,0:T(8,128)S(1)}, f32[8,3,13,128]{3,2,1,0:T(8,128)S(1)}, u32[]{:S(2)}, u32[]{:S(2)}) collective-permute-start(f32[8,3,13,128]{3,2,1,0:T(8,128)S(1)} %get-tuple-element.19.refs_0_), channel_id=1, source_target_pairs={{0,3},{1,0},{2,1},{3,2},{4,7},{5,4},{6,5},{7,6},{8,11},{9,8},{10,9... | collective-permute-start | bytes 479240 | tf_op jit(solution)/shard_map/ppermute | solution.py:34
  126.5 9.0 %collective-permute-start.2 = (f32[8,3,13,128]{3,2,1,0:T(8,128)S(1)}, f32[8,3,13,128]{3,2,1,0:T(8,128)S(1)}, u32[]{:S(2)}, u32[]{:S(2)}) collective-permute-start(f32[8,3,13,128]{3,2,1,0:T(8,128)S(1)} %get-tuple-element.19.refs_0_), channel_id=1, source_target_pairs={{0,2},{1,3},{2,0},{3,1},{4,6},{5,7},{6,4},{7,5},{8,10},{9,11},{10,... | collective-permute-start | bytes 479240 | tf_op jit(solution)/shard_map/ppermute | solution.py:34
  127.2 10.2 %collective-permute-start.1 = (f32[8,3,13,128]{3,2,1,0:T(8,128)S(1)}, f32[8,3,13,128]{3,2,1,0:T(8,128)S(1)}, u32[]{:S(2)}, u32[]{:S(2)}) collective-permute-start(f32[8,3,13,128]{3,2,1,0:T(8,128)S(1)} %get-tuple-element.19.refs_0_), channel_id=1, source_target_pairs={{0,1},{1,2},{2,3},{3,0},{4,5},{5,6},{6,7},{7,4},{8,9},{9,10},{10,1... | collective-permute-start | bytes 479240 | tf_op jit(solution)/shard_map/ppermute | solution.py:34
  203.3 3.3 %collective-permute-start.4 = (bf16[32,184,128]{2,1,0:T(8,128)(2,1)S(1)}, bf16[32,184,128]{2,1,0:T(8,128)(2,1)S(1)}, u32[]{:S(2)}, u32[]{:S(2)}) collective-permute-start(bf16[32,184,128]{2,1,0:T(8,128)(2,1)S(1)} %all_to_all.22.refs_0_), channel_id=1, source_target_pairs={{0,4},{4,0},{1,5},{5,1},{2,6},{6,2},{3,7},{7,3},{8,12},{12,8},{9,1... | collective-permute-start | bytes 4521992 | tf_op jit(solution)/shard_map/ppermute | solution.py:34
  211.3 0.9 copy-start.1
  212.2 31.1 %all-to-all-start.3 = ((bf16[32,16,896]{2,1,0:T(8,128)(2,1)}), bf16[32,16,896]{2,1,0:T(8,128)(2,1)S(1)}, u32[]{:S(2)}, u32[]{:S(2)}) async-start(bf16[32,16,896]{2,1,0:T(8,128)(2,1)} %bitcast.16), calls=%async_computation.4 | async-start | bytes 1835008 | tf_op jit(solution)/shard_map/all_to_all | solution.py:459
  225.4 1.5 copy-start
Sparse Core Ops, SparseCore 0:
  15.0 75.3 all-gather.2
  159.7 65.7 reduce-scatter.1

commit v2 on v1

v2 whole, which is shorter than its diff:
```python
import jax
import jax.numpy as jnp
from jax import lax
from jax.experimental import pallas as pl
from jax.experimental.pallas import tpu as pltpu
from jax.sharding import Mesh, PartitionSpec as P

HD = 128
SPAN = 64
NBRS = 2
SPARE = 128
BF = jnp.bfloat16
F32 = jnp.float32
I32 = jnp.int32
PARAMS = pltpu.CompilerParams(vmem_limit_bytes=48 * 1024 * 1024)
SMALL = pltpu.CompilerParams(vmem_limit_bytes=28 * 1024 * 1024)


def matmul(left, right, left_dim=1, right_dim=0):
    return lax.dot_general(
        left, right, (((left_dim,), (right_dim,)), ((), ())), preferred_element_type=F32
    )


def cost(flops, bytes_accessed, transcendentals=0):
    return pl.CostEstimate(
        flops=int(flops), bytes_accessed=int(bytes_accessed), transcendentals=int(transcendentals)
    )


def send_ring(array, axis, step):
    size = lax.axis_size(axis)
    if step % size == 0:
        return array
    return lax.ppermute(array, axis, [(i, (i + step) % size) for i in range(size)])


def piece_matrix(stored, quarter):
    shape = (stored * quarter, stored * quarter)
    to = lax.broadcasted_iota(I32, shape, 0)
    source = lax.broadcasted_iota(I32, shape, 1)
    token = to % stored * quarter + to // stored
    return (source == token).astype(F32).astype(BF)


def shift_matrix(step):
    to = lax.broadcasted_iota(I32, (SPAN, 2 * SPAN), 0)
    source = lax.broadcasted_iota(I32, (SPAN, 2 * SPAN), 1)
    return (source == to + step).astype(F32).astype(BF)


def prepare(encoded, nbr_shard, nbr_row, query, d_attended):
    stored, quarter, features = encoded.shape
    size = stored * quarter
    spans, neighbours = nbr_shard.shape
    tokens, width = query.shape

    def kernel(enc_ref, shard_ref, row_ref, q_ref, g_ref, out_ref, moved_ref, names):
        names[...] = jnp.zeros_like(names)
        names[:neighbours, :spans] = shard_ref[...].astype(F32)
        names[neighbours : 2 * neighbours, :spans] = row_ref[...].astype(F32)
        named = names[...].astype(BF)
        pieces = matmul(piece_matrix(stored, quarter), enc_ref[...]).astype(BF)
        for token in range(quarter):
            out_ref[token, :, :features] = pieces[token * stored : (token + 1) * stored]
            out_ref[token, :, features:] = named
        order = shift_matrix(SPAN - 1)
        blank = jnp.zeros((SPAN, width), BF)
        for which, ref in enumerate((q_ref, g_ref)):
            for span in range(spans):
                at = span * SPAN
                after = ref[at + SPAN : at + 2 * SPAN] if span < spans - 1 else blank
                pair = jnp.concatenate([ref[at : at + SPAN], after], 0)
                moved_ref[which, at : at + SPAN] = matmul(order, pair).astype(BF)

    return pl.pallas_call(
        kernel,
        out_shape=[
            jax.ShapeDtypeStruct((quarter, stored, features + SPARE), BF),
            jax.ShapeDtypeStruct((2, tokens, width), BF),
        ],
        scratch_shapes=[pltpu.VMEM((stored, SPARE), F32)],
        compiler_params=PARAMS,
        cost_estimate=cost(2 * size * size * features, 4 * size * features + 8 * tokens * width),
        name="prepare",
    )(encoded.reshape(size, features), nbr_shard.T, nbr_row.T, query, d_attended)


def join_pieces(parts):
    quarter, stored, features = parts.shape
    size = stored * quarter

    def kernel(part_ref, out_ref):
        out_ref[...] = matmul(piece_matrix(stored, quarter), part_ref[...], 0, 0).astype(BF)

    joined = pl.pallas_call(
        kernel,
        out_shape=jax.ShapeDtypeStruct((size, features), BF),
        compiler_params=PARAMS,
        cost_estimate=cost(2 * size * size * features, 4 * size * features),
        name="join_pieces",
    )(parts.reshape(size, features))
    return joined.reshape(stored, quarter, features)


def message_rows(picks, blocks):
    return -(-picks * blocks // 8) * 8


def pick_rows(store, target, lanes, picks, features, before=None):
    rows = store.shape[0]
    size = target.shape[0]
    each = size // lanes
    blocks = features // HD
    length = message_rows(picks, blocks)

    def kernel(target_ref, store_ref, *refs):
        column = lax.broadcasted_iota(I32, (size, rows), 1)
        one_hot = (column == target_ref[...]).astype(F32).astype(BF)
        if before is None:
            refs[0][...] = matmul(one_hot, store_ref[:, :features]).astype(BF)
            return
        before_ref, out_ref, spread = refs
        spread[:, length - 8 :, :] = jnp.zeros((lanes, 8, HD), F32)
        for block in range(blocks):
            cols = slice(block * HD, (block + 1) * HD)
            total = matmul(one_hot, store_ref[:, cols]) + before_ref[:, cols].astype(F32)
            for lane in range(lanes):
                part = total[lane * each : lane * each + picks]
                spread[lane, pl.ds(block, picks, stride=blocks), :] = part
        out_ref[...] = spread[...].astype(BF)

    last = before is not None
    shape = (lanes, length, HD) if last else (size, features)
    return pl.pallas_call(
        kernel,
        out_shape=jax.ShapeDtypeStruct(shape, BF),
        scratch_shapes=[pltpu.VMEM(shape, F32)] if last else [],
        compiler_params=PARAMS,
        cost_estimate=cost(2 * size * rows * features, 2 * (2 * size + rows) * features),
        name="pick_rows",
    )(target, store, *([before] if last else []))


def sum_rows(term, target, picks, rows, features, before=None):
    lanes, length, _ = term.shape
    size = target.shape[1]
    each = size // lanes
    blocks = features // HD
    last = before is not None

    def kernel(target_ref, term_ref, *refs):
        out_ref, spread, flat = refs[-3:]
        row = lax.broadcasted_iota(I32, (rows, size), 0)
        one_hot = (row == target_ref[...]).astype(F32).astype(BF)
        spread[...] = term_ref[...].astype(F32)
        for lane in range(lanes):
            low = lane * each + picks // 8 * 8
            flat[low : (lane + 1) * each, :] = jnp.zeros(((lane + 1) * each - low, HD), F32)
        for block in range(blocks):
            cols = slice(block * HD, (block + 1) * HD)
            for lane in range(lanes):
                part = spread[lane, pl.ds(block, picks, stride=blocks), :]
                flat[lane * each : lane * each + picks, :] = part
            total = matmul(one_hot, flat[...].astype(BF))
            if last:
                total = total + refs[0][:, cols]
            out_ref[:, cols] = total.astype(out_ref.dtype)

    return pl.pallas_call(
        kernel,
        out_shape=jax.ShapeDtypeStruct((rows, features), BF if last else F32),
        scratch_shapes=[pltpu.VMEM((lanes, length, HD), F32), pltpu.VMEM((size, HD), F32)],
        compiler_params=PARAMS,
        cost_estimate=cost(2 * size * rows * features, 2 * (size + 2 * rows) * features),
        name="sum_rows",
    )(target, term, *([before] if last else []))


def move_back(moved):
    tokens, width = moved.shape[-2:]
    spans = tokens // SPAN

    def kernel(moved_ref, *outs):
        order = shift_matrix(1)
        blank = jnp.zeros((SPAN, width), BF)
        for which, out in enumerate(outs):
            for span in range(spans):
                at = span * SPAN
                before = moved_ref[which, at - SPAN : at] if span else blank
                pair = jnp.concatenate([before, moved_ref[which, at : at + SPAN]], 0)
                out[at : at + SPAN] = matmul(order, pair).astype(BF)

    return pl.pallas_call(
        kernel,
        out_shape=[jax.ShapeDtypeStruct((tokens, width), BF)] * 2,
        compiler_params=PARAMS,
        cost_estimate=cost(8 * tokens * SPAN * width, 8 * tokens * width),
        name="move_back",
    )(moved.reshape(2, tokens, width))


def two_heads(pair):
    blank = jnp.zeros((SPAN, HD), pair.dtype)
    upper = jnp.concatenate([pair[:, :HD], blank], 1)
    lower = jnp.concatenate([blank, pair[:, HD:]], 1)
    return jnp.concatenate([upper, lower], 0)


def score_spans(fetched, key_weight, value_weight, moved):
    lanes = fetched.shape[0]
    features, all_width = key_weight.shape
    groups, _, tokens, width = moved.shape
    spans = tokens // SPAN
    keys = lanes * NBRS
    count = keys // 8
    blocks = features // HD
    per_group = width // (2 * HD)
    pairs = all_width // (2 * HD)
    factor = HD ** (-0.5)

    def kernel(
        part_ref,
        wk_ref,
        wv_ref,
        moved_ref,
        k_ref,
        v_ref,
        w_ref,
        gp_ref,
        top_ref,
        stat_ref,
        rows_ref,
        spread,
        flat,
    ):
        @pl.when(pl.program_id(0) == 0)
        def _():
            spread[...] = part_ref[...].astype(F32)
            for block in range(blocks):
                for lane in range(lanes):
                    for nbr in range(NBRS):
                        to = lane * NBRS // 8 * 8 * spans + lane * NBRS % 8 + nbr
                        flat[pl.ds(to, spans, stride=8), :] = spread[
                            lane, pl.ds(nbr * blocks + block, spans, stride=NBRS * blocks), :
                        ]
                rows_ref[:, block * HD : (block + 1) * HD] = flat[...].astype(BF)

        rows = rows_ref[...]

        def project(weight):
            out = matmul(rows, weight).reshape(count, spans, 8, 2 * HD)
            return out.transpose(1, 0, 2, 3).reshape(spans, keys, 2 * HD).astype(BF)

        step = pl.program_id(0)
        k_ref[step] = project(wk_ref[...])
        v_ref[step] = project(wv_ref[...])
        for span in range(spans):
            tok = pl.ds(span * SPAN, SPAN)
            scores = matmul(k_ref[step, span], two_heads(moved_ref[0, 0, tok, :]), 1, 1) * factor
            grad = matmul(v_ref[step, span], two_heads(moved_ref[0, 1, tok, :]), 1, 1)
            top = jnp.max(scores, axis=0, keepdims=True)
            weights = jnp.exp(scores - top)
            w_ref[step, span] = weights
            gp_ref[step, span] = grad
            mass = jnp.sum(weights, axis=0, keepdims=True)
            mean = jnp.sum(weights * grad, axis=0, keepdims=True) / mass
            top_ref[step, pl.ds(span, 1), :] = top
            stat_ref[pl.ds(2 * spans * step + span, 1), :] = top + jnp.log(mass)
            stat_ref[pl.ds(2 * spans * step + spans + span, 1), :] = mean

    whole = pl.BlockSpec(fetched.shape, lambda i: (0, 0, 0))
    weight_spec = pl.BlockSpec((features, 2 * HD), lambda i: (0, i))
    token_spec = pl.BlockSpec(
        (1, 2, tokens, 2 * HD), lambda i: (i // per_group, 0, 0, i % per_group)
    )
    held = pl.BlockSpec(memory_space=pltpu.VMEM)
    size = (2 * spans * pairs, 2 * SPAN)
    return pl.pallas_call(
        kernel,
        grid=(pairs,),
        in_specs=[whole, weight_spec, weight_spec, token_spec],
        out_specs=[held] * 5 + [pl.BlockSpec(size, lambda i: (0, 0))],
        out_shape=[
            pltpu.VMEM((pairs, spans, keys, 2 * HD), BF),
            pltpu.VMEM((pairs, spans, keys, 2 * HD), BF),
            pltpu.VMEM((pairs, spans, keys, 2 * SPAN), F32),
            pltpu.VMEM((pairs, spans, keys, 2 * SPAN), F32),
            pltpu.VMEM((pairs, spans, 2 * SPAN), F32),
            jax.ShapeDtypeStruct(size, F32),
        ],
        scratch_shapes=[
            pltpu.VMEM((spans * keys, features), BF),
            pltpu.VMEM(fetched.shape, F32),
            pltpu.VMEM((spans * keys, HD), F32),
        ],
        compiler_params=SMALL,
        cost_estimate=cost(
            4 * spans * keys * (features + SPAN) * all_width,
            8 * spans * keys * all_width,
            spans * keys * SPAN * 2 * pairs,
        ),
        name="score_spans",
    )(fetched, key_weight, value_weight, moved)


def blend_spans(scored, stats, key_weight, value_weight, moved):
    scored = [pltpu.with_memory_space_constraint(array, pltpu.VMEM) for array in scored]
    features, all_width = key_weight.shape
    groups, _, tokens, width = moved.shape
    _, spans, keys, _ = scored[0].shape
    count = keys // 8
    lanes = keys // NBRS
    blocks = features // HD
    per_group = width // (2 * HD)
    pairs = all_width // (2 * HD)
    factor = HD ** (-0.5)
    devices = len(stats)

    def kernel(k_ref, v_ref, w_ref, gp_ref, top_ref, *refs):
        stat_refs = refs[:devices]
        wk_ref, wv_ref, moved_ref, out_ref, part_ref = refs[devices : devices + 5]
        total, gk_ref, gv_ref, spread = refs[devices + 5 :]
        step = pl.program_id(0)

        first = 2 * spans * step
        logs = [ref[pl.ds(first, spans), :] for ref in stat_refs]
        means = [ref[pl.ds(first + spans, spans), :] for ref in stat_refs]
        most = logs[0]
        for log in logs[1:]:
            most = jnp.maximum(most, log)
        shares = [jnp.exp(log - most) for log in logs]
        whole = shares[0]
        inner = shares[0] * means[0]
        for share, mean in zip(shares[1:], means[1:]):
            whole = whole + share
            inner = inner + share * mean
        inner = inner / whole
        scale = jnp.exp(top_ref[step] - most) / whole

        for span in range(spans):
            tok = pl.ds(span * SPAN, SPAN)
            probs = w_ref[step, span] * scale[span : span + 1]
            probs_b = probs.astype(BF)
            grad_scores = (
                probs * (gp_ref[step, span] - inner[span : span + 1]) * factor
            ).astype(BF)
            k, v = k_ref[step, span], v_ref[step, span]
            blended = matmul(probs_b, v, 0, 0)
            shifted_grad = matmul(grad_scores, k, 0, 0)
            out_ref[0, 0, tok, :HD] = blended[:SPAN, :HD].astype(BF)
            out_ref[0, 0, tok, HD:] = blended[SPAN:, HD:].astype(BF)
            out_ref[0, 1, tok, :HD] = shifted_grad[:SPAN, :HD].astype(BF)
            out_ref[0, 1, tok, HD:] = shifted_grad[SPAN:, HD:].astype(BF)
            gk = matmul(grad_scores, two_heads(moved_ref[0, 0, tok, :]))
            gv = matmul(probs_b, two_heads(moved_ref[0, 1, tok, :]))
            gk_ref[:, span] = gk.reshape(count, 8, 2 * HD)
            gv_ref[:, span] = gv.reshape(count, 8, 2 * HD)

        flat = (spans * keys, 2 * HD)
        term = matmul(gk_ref[...].reshape(flat).astype(BF), wk_ref[...], 1, 1)
        term = term + matmul(gv_ref[...].reshape(flat).astype(BF), wv_ref[...], 1, 1)

        @pl.when(step == 0)
        def _():
            for block in range(blocks):
                total[block] = term[:, block * HD : (block + 1) * HD]

        @pl.when(step > 0)
        def _():
            for block in range(blocks):
                total[block] += term[:, block * HD : (block + 1) * HD]

        @pl.when(step == pairs - 1)
        def _():
            spread[:, length - 8 :, :] = jnp.zeros((lanes, 8, HD), F32)
            for block in range(blocks):
                for lane in range(lanes):
                    for nbr in range(NBRS):
                        at = lane * NBRS // 8 * 8 * spans + lane * NBRS % 8 + nbr
                        to = pl.ds(nbr * blocks + block, spans, stride=NBRS * blocks)
                        spread[lane, to, :] = total[block, pl.ds(at, spans, stride=8), :]
            part_ref[...] = spread[...].astype(BF)

    weight_spec = pl.BlockSpec((features, 2 * HD), lambda i: (0, i))
    token_spec = pl.BlockSpec(
        (1, 2, tokens, 2 * HD), lambda i: (i // per_group, 0, 0, i % per_group)
    )
    held = pl.BlockSpec(memory_space=pltpu.VMEM)
    stat_spec = pl.BlockSpec(stats[0].shape, lambda i: (0, 0))
    length = message_rows(spans * NBRS, blocks)
    result = (lanes, length, HD)
    return pl.pallas_call(
        kernel,
        grid=(pairs,),
        in_specs=[held] * 5
        + [stat_spec] * devices
        + [weight_spec, weight_spec, token_spec],
        out_specs=[token_spec, pl.BlockSpec(result, lambda i: (0, 0, 0))],
        out_shape=[
            jax.ShapeDtypeStruct((groups, 2, tokens, width), BF),
            jax.ShapeDtypeStruct(result, BF),
        ],
        scratch_shapes=[
            pltpu.VMEM((blocks, spans * keys, HD), F32),
            pltpu.VMEM((count, spans, 8, 2 * HD), F32),
            pltpu.VMEM((count, spans, 8, 2 * HD), F32),
            pltpu.VMEM(result, F32),
        ],
        compiler_params=SMALL,
        cost_estimate=cost(
            4 * spans * keys * (features + 2 * SPAN) * all_width, 12 * spans * keys * all_width
        ),
        name="blend_spans",
    )(*scored, *stats, key_weight, value_weight, moved)


def after(value, *others):
    return lax.optimization_barrier((value, *others))[0]


def shards(query, d_attended, encoded, key_weight, value_weight, nbr_shard, nbr_row):
    lanes = lax.axis_size(("z", "y"))
    groups = lax.axis_size("x")
    c = lax.axis_index("c").astype(I32)
    spans, neighbours = nbr_shard.shape
    stored, quarter, features = encoded.shape
    rows = lanes * stored
    picks = spans * neighbours

    pieces, moved = prepare(encoded, nbr_shard, nbr_row, query, d_attended)
    store = lax.all_to_all(pieces, ("z", "y"), 0, 0, tiled=True).reshape(rows, features + SPARE)

    moved = lax.all_gather(moved, "x")

    def places(held):
        named = held.reshape(lanes, stored, -1)[:, : 2 * neighbours, features : features + stored]
        named = named.astype(I32).transpose(0, 2, 1)
        owner, row = named[..., :neighbours], named[..., neighbours:]
        place = owner // 2 * stored + row
        live = (jnp.arange(stored) < spans)[None, :, None]
        here = owner % 2 == c
        return [jnp.where(live & there, place, -1).reshape(-1) for there in (here, ~here)]

    others = send_ring(store, "c", 1)
    own_here, own_there = places(store)
    picked = pick_rows(store, own_here.reshape(-1, 1), lanes, picks, features)
    picked = pick_rows(others, own_there.reshape(-1, 1), lanes, picks, features, picked)
    fetched = lax.all_to_all(picked, ("z", "y"), 0, 0, tiled=True)

    *scored, stat = score_spans(fetched, key_weight, value_weight, moved)
    stats = [send_ring(stat, "x", away) for away in range(groups)]
    output, terms = blend_spans(scored, stats, key_weight, value_weight, moved)
    output = lax.psum_scatter(output, "x", scatter_dimension=0)

    home = lax.all_to_all(terms, ("z", "y"), 0, 0, tiled=True)
    others_here = places(others)[0]
    sums = sum_rows(home, own_here.reshape(1, -1), picks, rows, features)
    home = send_ring(home, "c", 1)
    sums = sum_rows(home, others_here.reshape(1, -1), picks, rows, features, sums)
    returned = sums.reshape(lanes, stored, features)
    returned = lax.all_to_all(returned, ("z", "y"), 0, 0, tiled=True)
    attended, d_query = move_back(output)
    d_encoded = join_pieces(after(returned, attended))
    return (attended, d_query, d_encoded)


def solution(mesh):
    groups = mesh.devices.shape[1]
    fine = Mesh(mesh.devices.reshape(-1, 4, 2, groups), ("z", "y", "c", "x"))
    seq = ("z", "y", "c")
    placed = (
        P(seq, "x"),
        P(seq, "x"),
        P(seq, "x", None),
        P(),
        P(),
        P(seq, None),
        P(seq, None),
    )
    return jax.shard_map(
        shards,
        mesh=fine,
        in_specs=placed,
        out_specs=(P(seq, "x"), P(seq, "x"), P(seq, "x", None)),
        check_vma=False,
    )
```

time: 253 us -> 248 us (0.980)
  waiting for transfers between devices: 37 us -> 31.2 us
  local copies, waits for them, and re-layouts: 7.96 us -> 11.8 us
    ppermute x5, waiting for transfers between devices: 14.5 us -> 8.56 us  [send_ring(): lax.ppermute(array, axis, [(i, (i + step) % size) for i in range(size)])]
    unnamed x12 -> x20, local copies, waits for them, and re-layouts: 7.39 us -> 10.4 us
    reduce_scatter x1, waiting for transfers between devices: 7.63 us -> 10.6 us  [shards(): output = lax.psum_scatter(output, 'x', scatter_dimension=0)]
    all_to_all x1, waiting for transfers between devices: 14.8 us -> 12 us  [shards(): returned = lax.all_to_all(returned, ('z', 'y'), 0, 0, tiled=True)]
    pallas_call x1 -> x2, Pallas kernels: 4.69 us -> 5.8 us  [sum_rows(): pl.pallas_call(kernel, out_shape=jax.ShapeDtypeStruct((rows, features), B...]
where the time goes in v2:
time: 248 us; the launch traced here: 247 us
  blocking collectives  126 us (51%)
  Pallas kernels  53.8 us (22%)
  waiting for transfers between devices  31.2 us (13%)
  between operations  14.1 us (6%)
  local copies, waits for them, and re-layouts  11.8 us (5%)
  starting transfers between devices  10.2 us (4%)
    all_to_all x1, blocking collectives, shards(): fetched = lax.all_to_all(picked, ('z', 'y'), 0, 0, tiled=True)  43.6 us
    all_to_all x1, blocking collectives, shards(): home = lax.all_to_all(terms, ('z', 'y'), 0, 0, tiled=True)  42.8 us
    all_to_all x1, blocking collectives, shards(): lax.all_to_all(pieces, ('z', 'y'), 0, 0, tiled=True)  39.4 us
    pallas_call x1, Pallas kernels, blend_spans(): pl.pallas_call(kernel, grid=(pairs,), in_specs=[held] * 5 + [stat_spec] *...  21.6 us
    pallas_call x1, Pallas kernels, score_spans(): pl.pallas_call(kernel, grid=(pairs,), in_specs=[whole, weight_spec, weigh...  17.1 us
    all_to_all x1, waiting for transfers between devices, shards(): returned = lax.all_to_all(returned, ('z', 'y'), 0, 0, tiled=True)  12 us
    reduce_scatter x1, waiting for transfers between devices, shards(): output = lax.psum_scatter(output, 'x', scatter_dimension=0)  10.6 us
    unnamed x20, local copies, waits for them, and re-layouts  10.4 us
  transfers between devices with their start and end apart: 8, of which 7 were waited for; matrix products, arithmetic and copies ran while one was open for 1% of the time, Pallas kernels for 4%

profile of v2, /device:TPU:16, one launch (start us, length us, event | category | flops | bytes accessed | tf_op | source)
XLA Modules:
  0.0 247.3 jit_solution(11461312459180843443)
XLA Ops:
  7.2 1.2 copy-done.5
  9.6 1.2 copy-done.7
  12.1 2.5 prepare.1
  14.6 39.4 %all_to_all.20 = bf16[32,16,1024]{2,1,0:T(8,128)(2,1)S(1)} all-to-all(bf16[32,16,1024]{2,1,0:T(8,128)(2,1)S(1)} %get-tuple-element.16), channel_id=1, replica_groups=mesh['z'=8,'y'=4,'c'=2,'x'=4] {'z','y'}, dimensions={0} | all-to-all | bytes 2097152 | tf_op jit(solution)/shard_map/all_to_all | solution.py:432
  54.1 2.6 %collective-permute-done.store_ref = bf16[512,1024]{1,0:T(8,128)(2,1)S(1)} collective-permute-done((bf16[512,1024]{1,0:T(8,128)(2,1)S(1)}, bf16[512,1024]{1,0:T(8,128)(2,1)S(1)}, u32[]{:S(2)}, u32[]{:S(2)}) %collective-permute-start) | collective-permute-done | bytes 1048608 | tf_op jit(solution)/shard_map/ppermute | solution.py:35
  57.9 1.3 pick_rows.2.refs_0_
  59.2 2.2 pick_rows.3
  61.5 43.6 %all_to_all.21.part_ref = bf16[32,184,128]{2,1,0:T(8,128)(2,1)S(1)} all-to-all(bf16[32,184,128]{2,1,0:T(8,128)(2,1)S(1)} %pick_rows.3), channel_id=1, replica_groups=mesh['z'=8,'y'=4,'c'=2,'x'=4] {'z','y'}, dimensions={0} | all-to-all | bytes 3014656 | tf_op jit(solution)/shard_map/all_to_all | solution.py:449
  105.0 2.0 copy-done
  107.1 2.0 copy-done.2
  109.1 17.1 %score_spans.1 = (bf16[8,13,64,256]{3,2,1,0:T(8,128)(2,1)S(1)}, bf16[8,13,64,256]{3,2,1,0:T(8,128)(2,1)S(1)}, f32[8,13,64,128]{3,2,1,0:T(8,128)S(1)}, f32[8,13,6...) custom-call(bf16[32,184,128]{2,1,0:T(8,128)(2,1)S(1)} %all_to_all.21.part_ref, ...), custom_call_target="tpu_custom_call" | custom-call | flops 6543114240 | bytes 13631488 | tf_op jit(solution)/shard_map/score_spans/pallas_call | solution.py:279
  126.2 2.9 %collective-permute-start.3 = (f32[208,128]{1,0:T(8,128)S(1)}, f32[208,128]{1,0:T(8,128)S(1)}, u32[]{:S(2)}, u32[]{:S(2)}) collective-permute-start(f32[208,128]{1,0:T(8,128)S(1)} %get-tuple-element.23.refs_0_), channel_id=1, source_target_pairs={{0,3},{1,0},{2,1},{3,2},{4,7},{5,4},{6,5},{7,6},{8,11},{9,8},{10,9... | collective-permute-start | bytes 319496 | tf_op jit(solution)/shard_map/ppermute | solution.py:35
  130.8 2.1 collective-permute-done.3.refs_3_
  132.9 2.5 %collective-permute-done.2.refs_2_ = f32[208,128]{1,0:T(8,128)S(1)} collective-permute-done((f32[208,128]{1,0:T(8,128)S(1)}, f32[208,128]{1,0:T(8,128)S(1)}, u32[]{:S(2)}, u32[]{:S(2)}) %collective-permute-start.2) | collective-permute-done | bytes 106528 | tf_op jit(solution)/shard_map/ppermute | solution.py:35
  136.5 21.6 %blend_spans.1 = (bf16[4,2,832,512]{3,2,1,0:T(8,128)(2,1)}, bf16[32,184,128]{2,1,0:T(8,128)(2,1)S(1)}) custom-call(bf16[8,13,64,256]{3,2,1,0:T(8,128)(2,1)S(1)} %get-tuple-element.18.k_ref, bf16[8,13,64,256]{3,2,1,0:T(8,128)(2,1)S(1)} %get-tuple-element.19.v_ref, f32[8,13,64,128]{3,2,1,0:T(8,128)S(1)} %get-tuple-element.20.w_ref, ...), custom_call_target="tpu_custom_call" | custom-call | flops 6979321856 | bytes 20447232 | tf_op jit(solution)/shard_map/blend_spans/pallas_call | solution.py:393
  158.1 42.8 %all_to_all.22.term_ref = bf16[32,184,128]{2,1,0:T(8,128)(2,1)S(1)} all-to-all(bf16[32,184,128]{2,1,0:T(8,128)(2,1)S(1)} %get-tuple-element.27), channel_id=1, replica_groups=mesh['z'=8,'y'=4,'c'=2,'x'=4] {'z','y'}, dimensions={0} | all-to-all | bytes 3014656 | tf_op jit(solution)/shard_map/all_to_all | solution.py:456
  201.5 2.4 sum_rows.2.refs_0_
  204.2 3.4 %sum_rows.3 = bf16[512,896]{1,0:T(8,128)(2,1)} custom-call(s32[1,1024]{1,0:T(1,128)S(1)} %reshape_reshape.14.target_ref, bf16[32,184,128]{2,1,0:T(8,128)(2,1)S(1)} %collective-permute-done.4.term_ref, f32[512,896]{1,0:T(8,128)S(1)} %sum_rows.2.refs_0_), custom_call_target="tpu_custom_call" | custom-call | flops 939524096 | bytes 3670016 | tf_op jit(solution)/shard_map/sum_rows/pallas_call | solution.py:170
  207.5 5.6 %all-to-all-start.3 = ((bf16[32,16,896]{2,1,0:T(8,128)(2,1)}), bf16[32,16,896]{2,1,0:T(8,128)(2,1)S(1)}, u32[]{:S(2)}, u32[]{:S(2)}) async-start(bf16[32,16,896]{2,1,0:T(8,128)(2,1)} %bitcast.9), calls=%async_computation.4 | async-start | bytes 1835008 | tf_op jit(solution)/shard_map/all_to_all | solution.py:462
  213.1 10.6 %reduce-scatter.2.cloned.1.call-done = bf16[1,2,832,512]{3,2,1,0:T(8,128)(2,1)} async-done(((bf16[4,2,832,512]{3,2,1,0:T(8,128)(2,1)}), bf16[1,2,832,512]{3,2,1,0:T(8,128)(2,1)}) %reduce-scatter.2.cloned.1.call-update) | async-done | bytes 1703952 | tf_op jit(solution)/shard_map/reduce_scatter | solution.py:454
  223.7 1.5 copy-done.4
  225.2 1.6 move_back.1
  226.8 12.0 %all-to-all-done.3 = bf16[32,16,896]{2,1,0:T(8,128)(2,1)S(1)} async-done(((bf16[32,16,896]{2,1,0:T(8,128)(2,1)}), bf16[32,16,896]{2,1,0:T(8,128)(2,1)S(1)}, u32[]{:S(2)}, u32[]{:S(2)}) %all-to-all-start.3) | async-done | bytes 917536 | tf_op jit(solution)/shard_map/all_to_all | solution.py:462
  238.8 1.7 join_pieces.1
  (38 shorter events, 7.5 us)
Async XLA Ops:
  7.2 97.9 %all-gather.3.cloned.1.call-start = ((), (), s32[]{:S(2)}) async-start(), calls=%async_computation.6 | async-start | bytes 8519680 | tf_op jit(solution)/shard_map/all_gather | solution.py:434
  7.2 1.2 copy-start.5
  8.4 1.2 copy-start.6
  9.5 1.2 copy-start.7
  10.7 0.7 copy-start.8
  11.4 0.7 copy-start.9
  14.6 209.2 %reduce-scatter.2.cloned.1.call-start = ((), (), s32[]{:S(2)}) async-start(), calls=%async_computation.5 | async-start | bytes 8519680 | tf_op jit(solution)/shard_map/reduce_scatter | solution.py:454
  54.0 2.7 %collective-permute-start = (bf16[512,1024]{1,0:T(8,128)(2,1)S(1)}, bf16[512,1024]{1,0:T(8,128)(2,1)S(1)}, u32[]{:S(2)}, u32[]{:S(2)}) collective-permute-start(bf16[512,1024]{1,0:T(8,128)(2,1)S(1)} %bitcast.17), channel_id=1, source_target_pairs={{0,4},{4,0},{1,5},{5,1},{2,6},{6,2},{3,7},{7,3},{8,12},{12,8},{9,1... | collective-permute-start | bytes 3145736 | tf_op jit(solution)/shard_map/ppermute | solution.py:35
  105.0 2.0 copy-start
  107.1 2.0 copy-start.2
  109.1 27.3 %copy-start.1 = (bf16[896,2048]{1,0:T(8,128)(2,1)S(1)}, bf16[896,2048]{1,0:T(8,128)(2,1)}, u32[]{:S(2)}) copy-start(bf16[896,2048]{1,0:T(8,128)(2,1)} %refs_4_.1) | copy-start | bytes 11010052
  109.1 27.3 %copy-start.3 = (bf16[896,2048]{1,0:T(8,128)(2,1)S(1)}, bf16[896,2048]{1,0:T(8,128)(2,1)}, u32[]{:S(2)}) copy-start(bf16[896,2048]{1,0:T(8,128)(2,1)} %refs_5_.1) | copy-start | bytes 11010052
  126.2 6.6 %collective-permute-start.3 = (f32[208,128]{1,0:T(8,128)S(1)}, f32[208,128]{1,0:T(8,128)S(1)}, u32[]{:S(2)}, u32[]{:S(2)}) collective-permute-start(f32[208,128]{1,0:T(8,128)S(1)} %get-tuple-element.23.refs_0_), channel_id=1, source_target_pairs={{0,3},{1,0},{2,1},{3,2},{4,7},{5,4},{6,5},{7,6},{8,11},{9,8},{10,9... | collective-permute-start | bytes 319496 | tf_op jit(solution)/shard_map/ppermute | solution.py:35
  129.1 6.3 %collective-permute-start.2 = (f32[208,128]{1,0:T(8,128)S(1)}, f32[208,128]{1,0:T(8,128)S(1)}, u32[]{:S(2)}, u32[]{:S(2)}) collective-permute-start(f32[208,128]{1,0:T(8,128)S(1)} %get-tuple-element.23.refs_0_), channel_id=1, source_target_pairs={{0,2},{1,3},{2,0},{3,1},{4,6},{5,7},{6,4},{7,5},{8,10},{9,11},{10,... | collective-permute-start | bytes 319496 | tf_op jit(solution)/shard_map/ppermute | solution.py:35
  129.9 6.6 %collective-permute-start.1 = (f32[208,128]{1,0:T(8,128)S(1)}, f32[208,128]{1,0:T(8,128)S(1)}, u32[]{:S(2)}, u32[]{:S(2)}) collective-permute-start(f32[208,128]{1,0:T(8,128)S(1)} %get-tuple-element.23.refs_0_), channel_id=1, source_target_pairs={{0,1},{1,2},{2,3},{3,0},{4,5},{5,6},{6,7},{7,4},{8,9},{9,10},{10,1... | collective-permute-start | bytes 319496 | tf_op jit(solution)/shard_map/ppermute | solution.py:35
  200.8 3.3 %collective-permute-start.4 = (bf16[32,184,128]{2,1,0:T(8,128)(2,1)S(1)}, bf16[32,184,128]{2,1,0:T(8,128)(2,1)S(1)}, u32[]{:S(2)}, u32[]{:S(2)}) collective-permute-start(bf16[32,184,128]{2,1,0:T(8,128)(2,1)S(1)} %all_to_all.22.term_ref), channel_id=1, source_target_pairs={{0,4},{4,0},{1,5},{5,1},{2,6},{6,2},{3,7},{7,3},{8,12},{12,8},{9,1... | collective-permute-start | bytes 4521992 | tf_op jit(solution)/shard_map/ppermute | solution.py:35
  207.5 31.3 %all-to-all-start.3 = ((bf16[32,16,896]{2,1,0:T(8,128)(2,1)}), bf16[32,16,896]{2,1,0:T(8,128)(2,1)S(1)}, u32[]{:S(2)}, u32[]{:S(2)}) async-start(bf16[32,16,896]{2,1,0:T(8,128)(2,1)} %bitcast.9), calls=%async_computation.4 | async-start | bytes 1835008 | tf_op jit(solution)/shard_map/all_to_all | solution.py:462
  223.7 1.5 copy-start.4
Sparse Core Ops, SparseCore 0:
  14.7 75.3 all-gather.2
  158.2 65.4 reduce-scatter.1

commit v3 on v2

--- a/solution.py
+++ b/solution.py
@@ -13,7 +13,7 @@
 F32 = jnp.float32
 I32 = jnp.int32
 PARAMS = pltpu.CompilerParams(vmem_limit_bytes=48 * 1024 * 1024)
-SMALL = pltpu.CompilerParams(vmem_limit_bytes=28 * 1024 * 1024)
+SMALL = pltpu.CompilerParams(vmem_limit_bytes=48 * 1024 * 1024)
 
 
 def matmul(left, right, left_dim=1, right_dim=0):
@@ -55,16 +55,34 @@
     spans, neighbours = nbr_shard.shape
     tokens, width = query.shape
 
-    def kernel(enc_ref, shard_ref, row_ref, q_ref, g_ref, out_ref, moved_ref, names):
+    operands = [encoded.reshape(size, features), nbr_shard.T, nbr_row.T, query, d_attended]
+    held = [pltpu.with_memory_space_constraint(array, pltpu.HBM) for array in operands]
+
+    def kernel(*refs):
+        sources = refs[:5]
+        out_ref, moved_ref, names = refs[5:8]
+        landed, sems = refs[8:13], refs[13]
+        copies = [
+            pltpu.make_async_copy(source, target, sems.at[i])
+            for i, (source, target) in enumerate(zip(sources, landed))
+        ]
+        for copy in copies:
+            copy.start()
+        enc_ref, shard_ref, row_ref, q_ref, g_ref = landed
         names[...] = jnp.zeros_like(names)
+        source_matrix = piece_matrix(stored, quarter)
+        for copy in copies[:3]:
+            copy.wait()
         names[:neighbours, :spans] = shard_ref[...].astype(F32)
         names[neighbours : 2 * neighbours, :spans] = row_ref[...].astype(F32)
         named = names[...].astype(BF)
-        pieces = matmul(piece_matrix(stored, quarter), enc_ref[...]).astype(BF)
+        pieces = matmul(source_matrix, enc_ref[...]).astype(BF)
         for token in range(quarter):
             out_ref[token, :, :features] = pieces[token * stored : (token + 1) * stored]
             out_ref[token, :, features:] = named
         order = shift_matrix(SPAN - 1)
+        for copy in copies[3:]:
+            copy.wait()
         blank = jnp.zeros((SPAN, width), BF)
         for which, ref in enumerate((q_ref, g_ref)):
             for span in range(spans):
@@ -79,11 +97,14 @@
             jax.ShapeDtypeStruct((quarter, stored, features + SPARE), BF),
             jax.ShapeDtypeStruct((2, tokens, width), BF),
         ],
-        scratch_shapes=[pltpu.VMEM((stored, SPARE), F32)],
+        in_specs=[pl.BlockSpec(memory_space=pltpu.HBM)] * 5,
+        scratch_shapes=[pltpu.VMEM((stored, SPARE), F32)]
+        + [pltpu.VMEM(array.shape, array.dtype) for array in operands]
+        + [pltpu.SemaphoreType.DMA((5,))],
         compiler_params=PARAMS,
         cost_estimate=cost(2 * size * size * features, 4 * size * features + 8 * tokens * width),
         name="prepare",
-    )(encoded.reshape(size, features), nbr_shard.T, nbr_row.T, query, d_attended)
+    )(*held)
 
 
 def join_pieces(parts):

time: 248 us -> 243 us (0.980)
  local copies, waits for them, and re-layouts: 11.8 us -> 4.89 us
    unnamed x20 -> x10, local copies, waits for them, and re-layouts: 10.4 us -> 3.46 us
  transfers between devices with their start and end apart: 8 -> 8, of which waited for: 7 -> 7; matrix products, arithmetic and copies ran while one was open for 1% -> 1% of each run, Pallas kernels for 4% -> 5%
where the time goes in v3:
time: 243 us
  blocking collectives  126 us (52%)
  Pallas kernels  56.2 us (23%)
  waiting for transfers between devices  31.4 us (13%)
  between operations  14.1 us (6%)
  starting transfers between devices  10.1 us (4%)
  local copies, waits for them, and re-layouts  4.89 us (2%)
    all_to_all x1, blocking collectives, shards(): fetched = lax.all_to_all(picked, ('z', 'y'), 0, 0, tiled=True)  43.7 us
    all_to_all x1, blocking collectives, shards(): home = lax.all_to_all(terms, ('z', 'y'), 0, 0, tiled=True)  42.8 us
    all_to_all x1, blocking collectives, shards(): lax.all_to_all(pieces, ('z', 'y'), 0, 0, tiled=True)  39.5 us
    pallas_call x1, Pallas kernels, blend_spans(): pl.pallas_call(kernel, grid=(pairs,), in_specs=[held] * 5 + [stat_spec] *...  21.8 us
    pallas_call x1, Pallas kernels, score_spans(): pl.pallas_call(kernel, grid=(pairs,), in_specs=[whole, weight_spec, weigh...  17.9 us
    all_to_all x1, waiting for transfers between devices, shards(): returned = lax.all_to_all(returned, ('z', 'y'), 0, 0, tiled=True)  13.3 us
    reduce_scatter x1, waiting for transfers between devices, shards(): output = lax.psum_scatter(output, 'x', scatter_dimension=0)  9.28 us
    ppermute x5, waiting for transfers between devices, send_ring(): lax.ppermute(array, axis, [(i, (i + step) % size) for i in range(size)])  8.73 us
  transfers between devices with their start and end apart: 8, of which 7 were waited for; matrix products, arithmetic and copies ran while one was open for 1% of the time, Pallas kernels for 5%

profile of v3, /device:TPU:16, one launch (start us, length us, event | category | flops | bytes accessed | tf_op | source)
XLA Modules:
  0.0 243.0 jit_solution(6722634959696913125)
XLA Ops:
  7.2 3.8 %prepare.1 = (bf16[32,16,1024]{2,1,0:T(8,128)(2,1)S(1)}, bf16[2,832,512]{2,1,0:T(8,128)(2,1)}) custom-call(bf16[512,896]{1,0:T(8,128)(2,1)} %bitcast.22, s32[2,13]{1,0:T(2,128)} %bitcast.23, s32[2,13]{1,0:T(2,128)} %bitcast.24, bf16[832,512]{1,0:T(8,128)(2,1)} %refs_3_.1, bf16[832,512]{1,0:T(8,128)(2,1)} %refs_4_.2), custom_call_target="tpu_custom_call" | custom-call | flops 469762048 | bytes 5242880 | tf_op jit(solution)/shard_map/prepare/pallas_call | solution.py:94
  11.1 39.5 %all_to_all.20 = bf16[32,16,1024]{2,1,0:T(8,128)(2,1)S(1)} all-to-all(bf16[32,16,1024]{2,1,0:T(8,128)(2,1)S(1)} %get-tuple-element.16), channel_id=1, replica_groups=mesh['z'=8,'y'=4,'c'=2,'x'=4] {'z','y'}, dimensions={0} | all-to-all | bytes 2097152 | tf_op jit(solution)/shard_map/all_to_all | solution.py:453
  50.6 2.6 %collective-permute-done.store_ref = bf16[512,1024]{1,0:T(8,128)(2,1)S(1)} collective-permute-done((bf16[512,1024]{1,0:T(8,128)(2,1)S(1)}, bf16[512,1024]{1,0:T(8,128)(2,1)S(1)}, u32[]{:S(2)}, u32[]{:S(2)}) %collective-permute-start) | collective-permute-done | bytes 1048608 | tf_op jit(solution)/shard_map/ppermute | solution.py:35
  54.5 1.3 pick_rows.2.refs_0_
  55.8 2.2 pick_rows.3
  58.0 43.7 %all_to_all.21.part_ref = bf16[32,184,128]{2,1,0:T(8,128)(2,1)} all-to-all(bf16[32,184,128]{2,1,0:T(8,128)(2,1)S(1)} %pick_rows.3), channel_id=1, replica_groups=mesh['z'=8,'y'=4,'c'=2,'x'=4] {'z','y'}, dimensions={0} | all-to-all | bytes 3014656 | tf_op jit(solution)/shard_map/all_to_all | solution.py:470
  101.7 17.9 %score_spans.1 = (bf16[8,13,64,256]{3,2,1,0:T(8,128)(2,1)S(1)}, bf16[8,13,64,256]{3,2,1,0:T(8,128)(2,1)S(1)}, f32[8,13,64,128]{3,2,1,0:T(8,128)S(1)}, f32[8,13,6...) custom-call(bf16[32,184,128]{2,1,0:T(8,128)(2,1)} %all_to_all.21.part_ref, ...), custom_call_target="tpu_custom_call" | custom-call | flops 6543114240 | bytes 13631488 | tf_op jit(solution)/shard_map/score_spans/pallas_call | solution.py:300
  119.6 2.8 %collective-permute-start.3 = (f32[208,128]{1,0:T(8,128)}, f32[208,128]{1,0:T(8,128)S(1)}, u32[]{:S(2)}, u32[]{:S(2)}) collective-permute-start(f32[208,128]{1,0:T(8,128)} %get-tuple-element.23.refs_0_), channel_id=1, source_target_pairs={{0,3},{1,0},{2,1},{3,2},{4,7},{5,4},{6,5},{7,6},{8,11},{9,8},{10,9... | collective-permute-start | bytes 319496 | tf_op jit(solution)/shard_map/ppermute | solution.py:35
  122.3 0.8 collective-permute-start.2
  123.1 0.9 collective-permute-start.1
  124.0 2.4 collective-permute-done.3.refs_3_
  126.4 2.4 collective-permute-done.2.refs_2_
  128.8 1.1 collective-permute-done.1.refs_1_
  130.5 21.8 %blend_spans.1 = (bf16[4,2,832,512]{3,2,1,0:T(8,128)(2,1)}, bf16[32,184,128]{2,1,0:T(8,128)(2,1)}) custom-call(bf16[8,13,64,256]{3,2,1,0:T(8,128)(2,1)S(1)} %get-tuple-element.18.k_ref, bf16[8,13,64,256]{3,2,1,0:T(8,128)(2,1)S(1)} %get-tuple-element.19.v_ref, f32[8,13,64,128]{3,2,1,0:T(8,128)S(1)} %get-tuple-element.20.w_ref, ...), custom_call_target="tpu_custom_call" | custom-call | flops 6979321856 | bytes 20447232 | tf_op jit(solution)/shard_map/blend_spans/pallas_call | solution.py:414
  152.4 1.4 copy-done.1
  153.7 42.8 %all_to_all.22.term_ref = bf16[32,184,128]{2,1,0:T(8,128)(2,1)S(1)} all-to-all(bf16[32,184,128]{2,1,0:T(8,128)(2,1)S(1)} %copy-done.1), channel_id=1, replica_groups=mesh['z'=8,'y'=4,'c'=2,'x'=4] {'z','y'}, dimensions={0} | all-to-all | bytes 3014656 | tf_op jit(solution)/shard_map/all_to_all | solution.py:477
  197.1 2.4 %sum_rows.2.refs_0_ = f32[512,896]{1,0:T(8,128)S(1)} custom-call(s32[1,1024]{1,0:T(1,128)S(1)} %reshape_reshape.15.target_ref, bf16[32,184,128]{2,1,0:T(8,128)(2,1)S(1)} %all_to_all.22.term_ref), custom_call_target="tpu_custom_call" | custom-call | flops 939524096 | bytes 3670016 | tf_op jit(solution)/shard_map/sum_rows/pallas_call | solution.py:191
  199.8 3.4 %sum_rows.3 = bf16[512,896]{1,0:T(8,128)(2,1)} custom-call(s32[1,1024]{1,0:T(1,128)S(1)} %reshape_reshape.14.target_ref, bf16[32,184,128]{2,1,0:T(8,128)(2,1)S(1)} %collective-permute-done.4.term_ref, f32[512,896]{1,0:T(8,128)S(1)} %sum_rows.2.refs_0_), custom_call_target="tpu_custom_call" | custom-call | flops 939524096 | bytes 3670016 | tf_op jit(solution)/shard_map/sum_rows/pallas_call | solution.py:191
  203.2 5.6 %all-to-all-start.3 = ((bf16[32,16,896]{2,1,0:T(8,128)(2,1)}), bf16[32,16,896]{2,1,0:T(8,128)(2,1)S(1)}, u32[]{:S(2)}, u32[]{:S(2)}) async-start(bf16[32,16,896]{2,1,0:T(8,128)(2,1)} %bitcast.9), calls=%async_computation.4 | async-start | bytes 1835008 | tf_op jit(solution)/shard_map/all_to_all | solution.py:483
  208.7 9.3 %reduce-scatter.2.cloned.1.call-done = bf16[1,2,832,512]{3,2,1,0:T(8,128)(2,1)} async-done(((bf16[4,2,832,512]{3,2,1,0:T(8,128)(2,1)}), bf16[1,2,832,512]{3,2,1,0:T(8,128)(2,1)}) %reduce-scatter.2.cloned.1.call-update) | async-done | bytes 1703952 | tf_op jit(solution)/shard_map/reduce_scatter | solution.py:475
  218.0 1.5 copy-done
  219.5 1.6 move_back.1
  221.1 13.3 %all-to-all-done.3 = bf16[32,16,896]{2,1,0:T(8,128)(2,1)S(1)} async-done(((bf16[32,16,896]{2,1,0:T(8,128)(2,1)}), bf16[32,16,896]{2,1,0:T(8,128)(2,1)S(1)}, u32[]{:S(2)}, u32[]{:S(2)}) %all-to-all-start.3) | async-done | bytes 917536 | tf_op jit(solution)/shard_map/all_to_all | solution.py:483
  234.4 1.7 join_pieces.1
  (28 shorter events, 2.8 us)
Async XLA Ops:
  7.2 94.5 %all-gather.3.cloned.1.call-start = ((), (), s32[]{:S(2)}) async-start(), calls=%async_computation.6 | async-start | bytes 8519680 | tf_op jit(solution)/shard_map/all_gather | solution.py:455
  11.1 206.9 %reduce-scatter.2.cloned.1.call-start = ((), (), s32[]{:S(2)}) async-start(), calls=%async_computation.5 | async-start | bytes 8519680 | tf_op jit(solution)/shard_map/reduce_scatter | solution.py:475
  50.6 2.7 %collective-permute-start = (bf16[512,1024]{1,0:T(8,128)(2,1)S(1)}, bf16[512,1024]{1,0:T(8,128)(2,1)S(1)}, u32[]{:S(2)}, u32[]{:S(2)}) collective-permute-start(bf16[512,1024]{1,0:T(8,128)(2,1)S(1)} %bitcast.17), channel_id=1, source_target_pairs={{0,4},{4,0},{1,5},{5,1},{2,6},{6,2},{3,7},{7,3},{8,12},{12,8},{9,1... | collective-permute-start | bytes 3145736 | tf_op jit(solution)/shard_map/ppermute | solution.py:35
  119.6 6.9 %collective-permute-start.3 = (f32[208,128]{1,0:T(8,128)}, f32[208,128]{1,0:T(8,128)S(1)}, u32[]{:S(2)}, u32[]{:S(2)}) collective-permute-start(f32[208,128]{1,0:T(8,128)} %get-tuple-element.23.refs_0_), channel_id=1, source_target_pairs={{0,3},{1,0},{2,1},{3,2},{4,7},{5,4},{6,5},{7,6},{8,11},{9,8},{10,9... | collective-permute-start | bytes 319496 | tf_op jit(solution)/shard_map/ppermute | solution.py:35
  122.3 6.5 %collective-permute-start.2 = (f32[208,128]{1,0:T(8,128)}, f32[208,128]{1,0:T(8,128)S(1)}, u32[]{:S(2)}, u32[]{:S(2)}) collective-permute-start(f32[208,128]{1,0:T(8,128)} %get-tuple-element.23.refs_0_), channel_id=1, source_target_pairs={{0,2},{1,3},{2,0},{3,1},{4,6},{5,7},{6,4},{7,5},{8,10},{9,11},{10,... | collective-permute-start | bytes 319496 | tf_op jit(solution)/shard_map/ppermute | solution.py:35
  123.1 6.8 %collective-permute-start.1 = (f32[208,128]{1,0:T(8,128)}, f32[208,128]{1,0:T(8,128)S(1)}, u32[]{:S(2)}, u32[]{:S(2)}) collective-permute-start(f32[208,128]{1,0:T(8,128)} %get-tuple-element.23.refs_0_), channel_id=1, source_target_pairs={{0,1},{1,2},{2,3},{3,0},{4,5},{5,6},{6,7},{7,4},{8,9},{9,10},{10,1... | collective-permute-start | bytes 319496 | tf_op jit(solution)/shard_map/ppermute | solution.py:35
  126.4 3.5 %copy-start.2 = (f32[208,128]{1,0:T(8,128)}, f32[208,128]{1,0:T(8,128)S(1)}, u32[]{:S(2)}) copy-start(f32[208,128]{1,0:T(8,128)S(1)} %collective-permute-done.3.refs_3_) | copy-start | bytes 319492
  128.8 1.1 copy-start.3
  129.9 0.6 copy-start.4
  152.3 1.4 copy-start.1
  196.5 3.3 %collective-permute-start.4 = (bf16[32,184,128]{2,1,0:T(8,128)(2,1)S(1)}, bf16[32,184,128]{2,1,0:T(8,128)(2,1)S(1)}, u32[]{:S(2)}, u32[]{:S(2)}) collective-permute-start(bf16[32,184,128]{2,1,0:T(8,128)(2,1)S(1)} %all_to_all.22.term_ref), channel_id=1, source_target_pairs={{0,4},{4,0},{1,5},{5,1},{2,6},{6,2},{3,7},{7,3},{8,12},{12,8},{9,1... | collective-permute-start | bytes 4521992 | tf_op jit(solution)/shard_map/ppermute | solution.py:35
  203.2 31.3 %all-to-all-start.3 = ((bf16[32,16,896]{2,1,0:T(8,128)(2,1)}), bf16[32,16,896]{2,1,0:T(8,128)(2,1)S(1)}, u32[]{:S(2)}, u32[]{:S(2)}) async-start(bf16[32,16,896]{2,1,0:T(8,128)(2,1)} %bitcast.9), calls=%async_computation.4 | async-start | bytes 1835008 | tf_op jit(solution)/shard_map/all_to_all | solution.py:483
  218.0 1.5 copy-start
Sparse Core Ops, SparseCore 0:
  11.2 75.3 all-gather.2
  152.5 65.4 reduce-scatter.1

commit v4 on v3

--- a/solution.py
+++ b/solution.py
@@ -8,7 +8,8 @@
 HD = 128
 SPAN = 64
 NBRS = 2
-SPARE = 128
+SPARE = 8
+TURN = 4
 BF = jnp.bfloat16
 F32 = jnp.float32
 I32 = jnp.int32
@@ -75,11 +76,12 @@
             copy.wait()
         names[:neighbours, :spans] = shard_ref[...].astype(F32)
         names[neighbours : 2 * neighbours, :spans] = row_ref[...].astype(F32)
-        named = names[...].astype(BF)
-        pieces = matmul(source_matrix, enc_ref[...]).astype(BF)
+        named = names[...]
+        pieces = matmul(source_matrix, enc_ref[...])
         for token in range(quarter):
-            out_ref[token, :, :features] = pieces[token * stored : (token + 1) * stored]
-            out_ref[token, :, features:] = named
+            piece = pieces[token * stored : (token + 1) * stored]
+            parts = [piece[:, at : at + HD] for at in range(0, features, HD)]
+            out_ref[token] = jnp.concatenate([*parts, named], 0).astype(BF)
         order = shift_matrix(SPAN - 1)
         for copy in copies[3:]:
             copy.wait()
@@ -94,11 +96,11 @@
     return pl.pallas_call(
         kernel,
         out_shape=[
-            jax.ShapeDtypeStruct((quarter, stored, features + SPARE), BF),
+            jax.ShapeDtypeStruct((quarter, features // HD * stored + SPARE, HD), BF),
             jax.ShapeDtypeStruct((2, tokens, width), BF),
         ],
         in_specs=[pl.BlockSpec(memory_space=pltpu.HBM)] * 5,
-        scratch_shapes=[pltpu.VMEM((stored, SPARE), F32)]
+        scratch_shapes=[pltpu.VMEM((SPARE, HD), F32)]
         + [pltpu.VMEM(array.shape, array.dtype) for array in operands]
         + [pltpu.SemaphoreType.DMA((5,))],
         compiler_params=PARAMS,
@@ -128,24 +130,33 @@
     return -(-picks * blocks // 8) * 8
 
 
-def pick_rows(store, target, lanes, picks, features, before=None):
-    rows = store.shape[0]
+def pick_rows(store, target, picks, before=None):
+    lanes = store.shape[0]
     size = target.shape[0]
     each = size // lanes
-    blocks = features // HD
+    stored = each // NBRS
+    rows = lanes * stored
+    blocks = (store.shape[1] - SPARE) // stored
+    features = blocks * HD
     length = message_rows(picks, blocks)
 
     def kernel(target_ref, store_ref, *refs):
         column = lax.broadcasted_iota(I32, (size, rows), 1)
         one_hot = (column == target_ref[...]).astype(F32).astype(BF)
+
+        def part_of(block):
+            part = store_ref[:, block * stored : (block + 1) * stored, :].reshape(rows, HD)
+            return matmul(one_hot, part)
+
         if before is None:
-            refs[0][...] = matmul(one_hot, store_ref[:, :features]).astype(BF)
+            for block in range(blocks):
+                refs[0][:, block * HD : (block + 1) * HD] = part_of(block).astype(BF)
             return
         before_ref, out_ref, spread = refs
         spread[:, length - 8 :, :] = jnp.zeros((lanes, 8, HD), F32)
         for block in range(blocks):
             cols = slice(block * HD, (block + 1) * HD)
-            total = matmul(one_hot, store_ref[:, cols]) + before_ref[:, cols].astype(F32)
+            total = part_of(block) + before_ref[:, cols].astype(F32)
             for lane in range(lanes):
                 part = total[lane * each : lane * each + picks]
                 spread[lane, pl.ds(block, picks, stride=blocks), :] = part
@@ -341,7 +352,7 @@
     def kernel(k_ref, v_ref, w_ref, gp_ref, top_ref, *refs):
         stat_refs = refs[:devices]
         wk_ref, wv_ref, moved_ref, out_ref, part_ref = refs[devices : devices + 5]
-        total, gk_ref, gv_ref, spread = refs[devices + 5 :]
+        total, keys_ref, values_ref, spread = refs[devices + 5 :]
         step = pl.program_id(0)
 
         first = 2 * spans * step
@@ -375,20 +386,26 @@
             out_ref[0, 1, tok, HD:] = shifted_grad[SPAN:, HD:].astype(BF)
             gk = matmul(grad_scores, two_heads(moved_ref[0, 0, tok, :]))
             gv = matmul(probs_b, two_heads(moved_ref[0, 1, tok, :]))
-            gk_ref[:, span] = gk.reshape(count, 8, 2 * HD)
-            gv_ref[:, span] = gv.reshape(count, 8, 2 * HD)
-
-        flat = (spans * keys, 2 * HD)
-        term = matmul(gk_ref[...].reshape(flat).astype(BF), wk_ref[...], 1, 1)
-        term = term + matmul(gv_ref[...].reshape(flat).astype(BF), wv_ref[...], 1, 1)
-
-        @pl.when(step == 0)
+            at = pl.ds(pl.multiple_of(step % TURN * 2 * HD, 2 * HD), 2 * HD)
+            gk = gk.reshape(count, 8, 2 * HD)
+            gv = gv.reshape(count, 8, 2 * HD)
+            keys_ref[:, span, :, at] = gk
+            values_ref[:, span, :, at] = gv
+
+        def project():
+            left = jnp.concatenate([keys_ref[...], values_ref[...]], 3)
+            left = left.reshape(spans * keys, 4 * TURN * HD).astype(BF)
+            return matmul(left, jnp.concatenate([wk_ref[...], wv_ref[...]], 1), 1, 1)
+
+        @pl.when(step == TURN - 1)
         def _():
+            term = project()
             for block in range(blocks):
                 total[block] = term[:, block * HD : (block + 1) * HD]
 
-        @pl.when(step > 0)
+        @pl.when((step % TURN == TURN - 1) & (step >= TURN))
         def _():
+            term = project()
             for block in range(blocks):
                 total[block] += term[:, block * HD : (block + 1) * HD]
 
@@ -403,7 +420,7 @@
                         spread[lane, to, :] = total[block, pl.ds(at, spans, stride=8), :]
             part_ref[...] = spread[...].astype(BF)
 
-    weight_spec = pl.BlockSpec((features, 2 * HD), lambda i: (0, i))
+    weight_spec = pl.BlockSpec((features, 2 * TURN * HD), lambda i: (0, i // TURN))
     token_spec = pl.BlockSpec(
         (1, 2, tokens, 2 * HD), lambda i: (i // per_group, 0, 0, i % per_group)
     )
@@ -420,12 +437,12 @@
         out_specs=[token_spec, pl.BlockSpec(result, lambda i: (0, 0, 0))],
         out_shape=[
             jax.ShapeDtypeStruct((groups, 2, tokens, width), BF),
-            jax.ShapeDtypeStruct(result, BF),
+            pltpu.HBM(result, BF),
         ],
         scratch_shapes=[
             pltpu.VMEM((blocks, spans * keys, HD), F32),
-            pltpu.VMEM((count, spans, 8, 2 * HD), F32),
-            pltpu.VMEM((count, spans, 8, 2 * HD), F32),
+            pltpu.VMEM((count, spans, 8, 2 * TURN * HD), F32),
+            pltpu.VMEM((count, spans, 8, 2 * TURN * HD), F32),
             pltpu.VMEM(result, F32),
         ],
         compiler_params=SMALL,
@@ -450,13 +467,12 @@
     picks = spans * neighbours
 
     pieces, moved = prepare(encoded, nbr_shard, nbr_row, query, d_attended)
-    store = lax.all_to_all(pieces, ("z", "y"), 0, 0, tiled=True).reshape(rows, features + SPARE)
+    store = lax.all_to_all(pieces, ("z", "y"), 0, 0, tiled=True)
 
     moved = lax.all_gather(moved, "x")
 
     def places(held):
-        named = held.reshape(lanes, stored, -1)[:, : 2 * neighbours, features : features + stored]
-        named = named.astype(I32).transpose(0, 2, 1)
+        named = held[:, -SPARE : 2 * neighbours - SPARE, :stored].astype(I32).transpose(0, 2, 1)
         owner, row = named[..., :neighbours], named[..., neighbours:]
         place = owner // 2 * stored + row
         live = (jnp.arange(stored) < spans)[None, :, None]
@@ -465,8 +481,8 @@
 
     others = send_ring(store, "c", 1)
     own_here, own_there = places(store)
-    picked = pick_rows(store, own_here.reshape(-1, 1), lanes, picks, features)
-    picked = pick_rows(others, own_there.reshape(-1, 1), lanes, picks, features, picked)
+    picked = pick_rows(store, own_here.reshape(-1, 1), picks)
+    picked = pick_rows(others, own_there.reshape(-1, 1), picks, picked)
     fetched = lax.all_to_all(picked, ("z", "y"), 0, 0, tiled=True)
 
     *scored, stat = score_spans(fetched, key_weight, value_weight, moved)
@@ -475,7 +491,7 @@
     output = lax.psum_scatter(output, "x", scatter_dimension=0)
 
     home = lax.all_to_all(terms, ("z", "y"), 0, 0, tiled=True)
-    others_here = places(others)[0]
+    others_here = places(after(others, terms))[0]
     sums = sum_rows(home, own_here.reshape(1, -1), picks, rows, features)
     home = send_ring(home, "c", 1)
     sums = sum_rows(home, others_here.reshape(1, -1), picks, rows, features, sums)

time: 243 us -> 242 us (level)
  transfers between devices with their start and end apart: 8 -> 8, of which waited for: 7 -> 5; matrix products, arithmetic and copies ran while one was open for 1% -> 1% of each run, Pallas kernels for 5% -> 5%
where the time goes in v4:
time: 242 us; the launch traced here: 241 us
  blocking collectives  124 us (51%)
  Pallas kernels  56.4 us (23%)
  waiting for transfers between devices  29.7 us (12%)
  between operations  14.2 us (6%)
  starting transfers between devices  10.1 us (4%)
  local copies, waits for them, and re-layouts  4.9 us (2%)
    all_to_all x1, blocking collectives, shards(): fetched = lax.all_to_all(picked, ('z', 'y'), 0, 0, tiled=True)  44 us
    all_to_all x1, blocking collectives, shards(): home = lax.all_to_all(terms, ('z', 'y'), 0, 0, tiled=True)  42.4 us
    all_to_all x1, blocking collectives, shards(): store = lax.all_to_all(pieces, ('z', 'y'), 0, 0, tiled=True)  38 us
    pallas_call x1, Pallas kernels, blend_spans(): pl.pallas_call(kernel, grid=(pairs,), in_specs=[held] * 5 + [stat_spec] *...  21.3 us
    pallas_call x1, Pallas kernels, score_spans(): pl.pallas_call(kernel, grid=(pairs,), in_specs=[whole, weight_spec, weigh...  17.9 us
    all_to_all x1, waiting for transfers between devices, shards(): returned = lax.all_to_all(returned, ('z', 'y'), 0, 0, tiled=True)  14.7 us
    reduce_scatter x1, waiting for transfers between devices, shards(): output = lax.psum_scatter(output, 'x', scatter_dimension=0)  8.08 us
    ppermute x5, waiting for transfers between devices, send_ring(): lax.ppermute(array, axis, [(i, (i + step) % size) for i in range(size)])  6.79 us
  transfers between devices with their start and end apart: 8, of which 5 were waited for; matrix products, arithmetic and copies ran while one was open for 1% of the time, Pallas kernels for 5%

profile of v4, /device:TPU:16, one launch (start us, length us, event | category | flops | bytes accessed | tf_op | source)
XLA Modules:
  0.0 240.9 jit_solution(15389539681720193871)
XLA Ops:
  7.2 3.8 %prepare.1 = (bf16[32,120,128]{2,1,0:T(8,128)(2,1)S(1)}, bf16[2,832,512]{2,1,0:T(8,128)(2,1)}) custom-call(bf16[512,896]{1,0:T(8,128)(2,1)} %bitcast.17, s32[2,13]{1,0:T(2,128)} %bitcast.18, s32[2,13]{1,0:T(2,128)} %bitcast.19, bf16[832,512]{1,0:T(8,128)(2,1)} %refs_3_.1, bf16[832,512]{1,0:T(8,128)(2,1)} %refs_4_.2), custom_call_target="tpu_custom_call" | custom-call | flops 469762048 | bytes 5242880 | tf_op jit(solution)/shard_map/prepare/pallas_call | solution.py:96
  11.1 38.0 %all_to_all.20.store_ref = bf16[32,120,128]{2,1,0:T(8,128)(2,1)S(1)} all-to-all(bf16[32,120,128]{2,1,0:T(8,128)(2,1)S(1)} %get-tuple-element.17), channel_id=1, replica_groups=mesh['z'=8,'y'=4,'c'=2,'x'=4] {'z','y'}, dimensions={0} | all-to-all | bytes 1966080 | tf_op jit(solution)/shard_map/all_to_all | solution.py:470
  50.2 2.1 pick_rows.2.refs_0_
  52.4 2.2 pick_rows.3
  54.6 44.0 %all_to_all.21.part_ref = bf16[32,184,128]{2,1,0:T(8,128)(2,1)} all-to-all(bf16[32,184,128]{2,1,0:T(8,128)(2,1)S(1)} %pick_rows.3), channel_id=1, replica_groups=mesh['z'=8,'y'=4,'c'=2,'x'=4] {'z','y'}, dimensions={0} | all-to-all | bytes 3014656 | tf_op jit(solution)/shard_map/all_to_all | solution.py:486
  98.7 17.9 %score_spans.1 = (bf16[8,13,64,256]{3,2,1,0:T(8,128)(2,1)S(1)}, bf16[8,13,64,256]{3,2,1,0:T(8,128)(2,1)S(1)}, f32[8,13,64,128]{3,2,1,0:T(8,128)S(1)}, f32[8,13,6...) custom-call(bf16[32,184,128]{2,1,0:T(8,128)(2,1)} %all_to_all.21.part_ref, ...), custom_call_target="tpu_custom_call" | custom-call | flops 6543114240 | bytes 13631488 | tf_op jit(solution)/shard_map/score_spans/pallas_call | solution.py:311
  116.5 2.8 %collective-permute-start.3 = (f32[208,128]{1,0:T(8,128)}, f32[208,128]{1,0:T(8,128)S(1)}, u32[]{:S(2)}, u32[]{:S(2)}) collective-permute-start(f32[208,128]{1,0:T(8,128)} %get-tuple-element.24.refs_0_), channel_id=1, source_target_pairs={{0,3},{1,0},{2,1},{3,2},{4,7},{5,4},{6,5},{7,6},{8,11},{9,8},{10,9... | collective-permute-start | bytes 319496 | tf_op jit(solution)/shard_map/ppermute | solution.py:36
  119.3 0.8 collective-permute-start.2
  120.1 0.9 collective-permute-start.1
  121.0 3.2 %collective-permute-done.3.refs_3_ = f32[208,128]{1,0:T(8,128)S(1)} collective-permute-done((f32[208,128]{1,0:T(8,128)}, f32[208,128]{1,0:T(8,128)S(1)}, u32[]{:S(2)}, u32[]{:S(2)}) %collective-permute-start.3) | collective-permute-done | bytes 106528 | tf_op jit(solution)/shard_map/ppermute | solution.py:36
  124.2 2.5 %collective-permute-done.2.refs_2_ = f32[208,128]{1,0:T(8,128)S(1)} collective-permute-done((f32[208,128]{1,0:T(8,128)}, f32[208,128]{1,0:T(8,128)S(1)}, u32[]{:S(2)}, u32[]{:S(2)}) %collective-permute-start.2) | collective-permute-done | bytes 106528 | tf_op jit(solution)/shard_map/ppermute | solution.py:36
  126.7 1.1 collective-permute-done.1.refs_1_
  128.4 21.3 %blend_spans.1 = (bf16[4,2,832,512]{3,2,1,0:T(8,128)(2,1)}, bf16[32,184,128]{2,1,0:T(8,128)(2,1)}) custom-call(bf16[8,13,64,256]{3,2,1,0:T(8,128)(2,1)S(1)} %get-tuple-element.19.k_ref, bf16[8,13,64,256]{3,2,1,0:T(8,128)(2,1)S(1)} %get-tuple-element.20.v_ref, f32[8,13,64,128]{3,2,1,0:T(8,128)S(1)} %get-tuple-element.21.w_ref, ...), custom_call_target="tpu_custom_call" | custom-call | flops 6979321856 | bytes 20447232 | tf_op jit(solution)/shard_map/blend_spans/pallas_call | solution.py:431
  149.7 1.4 copy-done.2
  151.1 42.4 %all_to_all.22.term_ref = bf16[32,184,128]{2,1,0:T(8,128)(2,1)S(1)} all-to-all(bf16[32,184,128]{2,1,0:T(8,128)(2,1)S(1)} %copy-done.2), channel_id=1, replica_groups=mesh['z'=8,'y'=4,'c'=2,'x'=4] {'z','y'}, dimensions={0} | all-to-all | bytes 3014656 | tf_op jit(solution)/shard_map/all_to_all | solution.py:493
  193.6 0.9 convert_bitcast_fusion
  195.1 2.4 %sum_rows.2.refs_0_ = f32[512,896]{1,0:T(8,128)S(1)} custom-call(s32[1,1024]{1,0:T(1,128)S(1)} %reshape_reshape.15.target_ref, bf16[32,184,128]{2,1,0:T(8,128)(2,1)S(1)} %all_to_all.22.term_ref), custom_call_target="tpu_custom_call" | custom-call | flops 939524096 | bytes 3670016 | tf_op jit(solution)/shard_map/sum_rows/pallas_call | solution.py:202
  197.6 3.4 %sum_rows.3 = bf16[512,896]{1,0:T(8,128)(2,1)} custom-call(s32[1,1024]{1,0:T(1,128)S(1)} %reshape_reshape.14.target_ref, bf16[32,184,128]{2,1,0:T(8,128)(2,1)S(1)} %collective-permute-done.4.term_ref, f32[512,896]{1,0:T(8,128)S(1)} %sum_rows.2.refs_0_), custom_call_target="tpu_custom_call" | custom-call | flops 939524096 | bytes 3670016 | tf_op jit(solution)/shard_map/sum_rows/pallas_call | solution.py:202
  200.9 5.6 %all-to-all-start.3 = ((bf16[32,16,896]{2,1,0:T(8,128)(2,1)}), bf16[32,16,896]{2,1,0:T(8,128)(2,1)S(1)}, u32[]{:S(2)}, u32[]{:S(2)}) async-start(bf16[32,16,896]{2,1,0:T(8,128)(2,1)} %bitcast.7), calls=%async_computation.4 | async-start | bytes 1835008 | tf_op jit(solution)/shard_map/all_to_all | solution.py:499
  206.5 8.1 %reduce-scatter.2.cloned.1.call-done = bf16[1,2,832,512]{3,2,1,0:T(8,128)(2,1)} async-done(((bf16[4,2,832,512]{3,2,1,0:T(8,128)(2,1)}), bf16[1,2,832,512]{3,2,1,0:T(8,128)(2,1)}) %reduce-scatter.2.cloned.1.call-update) | async-done | bytes 1703952 | tf_op jit(solution)/shard_map/reduce_scatter | solution.py:491
  214.6 1.5 copy-done
  216.0 1.6 move_back.1
  217.7 14.7 %all-to-all-done.3 = bf16[32,16,896]{2,1,0:T(8,128)(2,1)S(1)} async-done(((bf16[32,16,896]{2,1,0:T(8,128)(2,1)}), bf16[32,16,896]{2,1,0:T(8,128)(2,1)S(1)}, u32[]{:S(2)}, u32[]{:S(2)}) %all-to-all-start.3) | async-done | bytes 917536 | tf_op jit(solution)/shard_map/all_to_all | solution.py:499
  232.4 1.7 join_pieces.1
  (31 shorter events, 2.6 us)
Async XLA Ops:
  7.2 91.5 %all-gather.3.cloned.1.call-start = ((), (), s32[]{:S(2)}) async-start(), calls=%async_computation.6 | async-start | bytes 8519680 | tf_op jit(solution)/shard_map/all_gather | solution.py:472
  11.1 203.5 %reduce-scatter.2.cloned.1.call-start = ((), (), s32[]{:S(2)}) async-start(), calls=%async_computation.5 | async-start | bytes 8519680 | tf_op jit(solution)/shard_map/reduce_scatter | solution.py:491
  49.2 3.2 %collective-permute-start = (bf16[32,120,128]{2,1,0:T(8,128)(2,1)S(1)}, bf16[32,120,128]{2,1,0:T(8,128)(2,1)S(1)}, u32[]{:S(2)}, u32[]{:S(2)}) collective-permute-start(bf16[32,120,128]{2,1,0:T(8,128)(2,1)S(1)} %all_to_all.20.store_ref), channel_id=1, source_target_pairs={{0,4},{4,0},{1,5},{5,1},{2,6},{6,2},{3,7},{7,3},{8,12},{12,8},{9,1... | collective-permute-start | bytes 2949128 | tf_op jit(solution)/shard_map/ppermute | solution.py:36
  52.4 2.2 copy-start.1
  116.5 7.7 %collective-permute-start.3 = (f32[208,128]{1,0:T(8,128)}, f32[208,128]{1,0:T(8,128)S(1)}, u32[]{:S(2)}, u32[]{:S(2)}) collective-permute-start(f32[208,128]{1,0:T(8,128)} %get-tuple-element.24.refs_0_), channel_id=1, source_target_pairs={{0,3},{1,0},{2,1},{3,2},{4,7},{5,4},{6,5},{7,6},{8,11},{9,8},{10,9... | collective-permute-start | bytes 319496 | tf_op jit(solution)/shard_map/ppermute | solution.py:36
  119.3 7.4 %collective-permute-start.2 = (f32[208,128]{1,0:T(8,128)}, f32[208,128]{1,0:T(8,128)S(1)}, u32[]{:S(2)}, u32[]{:S(2)}) collective-permute-start(f32[208,128]{1,0:T(8,128)} %get-tuple-element.24.refs_0_), channel_id=1, source_target_pairs={{0,2},{1,3},{2,0},{3,1},{4,6},{5,7},{6,4},{7,5},{8,10},{9,11},{10,... | collective-permute-start | bytes 319496 | tf_op jit(solution)/shard_map/ppermute | solution.py:36
  120.1 7.7 %collective-permute-start.1 = (f32[208,128]{1,0:T(8,128)}, f32[208,128]{1,0:T(8,128)S(1)}, u32[]{:S(2)}, u32[]{:S(2)}) collective-permute-start(f32[208,128]{1,0:T(8,128)} %get-tuple-element.24.refs_0_), channel_id=1, source_target_pairs={{0,1},{1,2},{2,3},{3,0},{4,5},{5,6},{6,7},{7,4},{8,9},{9,10},{10,1... | collective-permute-start | bytes 319496 | tf_op jit(solution)/shard_map/ppermute | solution.py:36
  124.2 3.6 %copy-start.3 = (f32[208,128]{1,0:T(8,128)}, f32[208,128]{1,0:T(8,128)S(1)}, u32[]{:S(2)}) copy-start(f32[208,128]{1,0:T(8,128)S(1)} %collective-permute-done.3.refs_3_) | copy-start | bytes 319492
  126.7 1.1 copy-start.4
  127.8 0.6 copy-start.5
  149.7 1.4 copy-start.2
  193.4 4.1 %collective-permute-start.4 = (bf16[32,184,128]{2,1,0:T(8,128)(2,1)S(1)}, bf16[32,184,128]{2,1,0:T(8,128)(2,1)S(1)}, u32[]{:S(2)}, u32[]{:S(2)}) collective-permute-start(bf16[32,184,128]{2,1,0:T(8,128)(2,1)S(1)} %all_to_all.22.term_ref), channel_id=1, source_target_pairs={{0,4},{4,0},{1,5},{5,1},{2,6},{6,2},{3,7},{7,3},{8,12},{12,8},{9,1... | collective-permute-start | bytes 4521992 | tf_op jit(solution)/shard_map/ppermute | solution.py:36
  200.9 31.5 %all-to-all-start.3 = ((bf16[32,16,896]{2,1,0:T(8,128)(2,1)}), bf16[32,16,896]{2,1,0:T(8,128)(2,1)S(1)}, u32[]{:S(2)}, u32[]{:S(2)}) async-start(bf16[32,16,896]{2,1,0:T(8,128)(2,1)} %bitcast.7), calls=%async_computation.4 | async-start | bytes 1835008 | tf_op jit(solution)/shard_map/all_to_all | solution.py:499
  214.6 1.5 copy-start
Sparse Core Ops, SparseCore 0:
  11.2 75.3 all-gather.2
  149.8 64.6 reduce-scatter.1

commit v5 on v4

--- a/solution.py
+++ b/solution.py
@@ -9,12 +9,12 @@
 SPAN = 64
 NBRS = 2
 SPARE = 8
-TURN = 4
+SIDES = 2
 BF = jnp.bfloat16
 F32 = jnp.float32
 I32 = jnp.int32
 PARAMS = pltpu.CompilerParams(vmem_limit_bytes=48 * 1024 * 1024)
-SMALL = pltpu.CompilerParams(vmem_limit_bytes=48 * 1024 * 1024)
+SMALL = pltpu.CompilerParams(vmem_limit_bytes=50 * 1024 * 1024)
 
 
 def matmul(left, right, left_dim=1, right_dim=0):
@@ -285,32 +285,44 @@
             return out.transpose(1, 0, 2, 3).reshape(spans, keys, 2 * HD).astype(BF)
 
         step = pl.program_id(0)
-        k_ref[step] = project(wk_ref[...])
-        v_ref[step] = project(wv_ref[...])
-        for span in range(spans):
-            tok = pl.ds(span * SPAN, SPAN)
-            scores = matmul(k_ref[step, span], two_heads(moved_ref[0, 0, tok, :]), 1, 1) * factor
-            grad = matmul(v_ref[step, span], two_heads(moved_ref[0, 1, tok, :]), 1, 1)
-            top = jnp.max(scores, axis=0, keepdims=True)
-            weights = jnp.exp(scores - top)
-            w_ref[step, span] = weights
-            gp_ref[step, span] = grad
-            mass = jnp.sum(weights, axis=0, keepdims=True)
-            mean = jnp.sum(weights * grad, axis=0, keepdims=True) / mass
-            top_ref[step, pl.ds(span, 1), :] = top
-            stat_ref[pl.ds(2 * spans * step + span, 1), :] = top + jnp.log(mass)
-            stat_ref[pl.ds(2 * spans * step + spans + span, 1), :] = mean
+        scores, grads = [], []
+        for side in range(SIDES):
+            pair = SIDES * step + side
+            cols = slice(side * 2 * HD, (side + 1) * 2 * HD)
+            k_all = project(wk_ref[:, cols])
+            v_all = project(wv_ref[:, cols])
+            k_ref[pair] = k_all
+            v_ref[pair] = v_all
+            for span in range(spans):
+                tok = slice(span * SPAN, (span + 1) * SPAN)
+                queries = two_heads(moved_ref[0, 0, tok, cols])
+                scores.append(matmul(k_all[span], queries, 1, 1) * factor)
+                grads.append(matmul(v_all[span], two_heads(moved_ref[0, 1, tok, cols]), 1, 1))
+        for side in range(SIDES):
+            pair = SIDES * step + side
+            for span in range(spans):
+                score, grad = scores[side * spans + span], grads[side * spans + span]
+                top = jnp.max(score, axis=0, keepdims=True)
+                weights = jnp.exp(score - top)
+                w_ref[pair, span] = weights
+                gp_ref[pair, span] = grad
+                mass = jnp.sum(weights, axis=0, keepdims=True)
+                mean = jnp.sum(weights * grad, axis=0, keepdims=True) / mass
+                top_ref[pair, pl.ds(span, 1), :] = top
+                stat_ref[pl.ds(2 * spans * pair + span, 1), :] = top + jnp.log(mass)
+                stat_ref[pl.ds(2 * spans * pair + spans + span, 1), :] = mean
 
     whole = pl.BlockSpec(fetched.shape, lambda i: (0, 0, 0))
-    weight_spec = pl.BlockSpec((features, 2 * HD), lambda i: (0, i))
+    weight_spec = pl.BlockSpec((features, SIDES * 2 * HD), lambda i: (0, i))
+    turns = per_group // SIDES
     token_spec = pl.BlockSpec(
-        (1, 2, tokens, 2 * HD), lambda i: (i // per_group, 0, 0, i % per_group)
+        (1, 2, tokens, SIDES * 2 * HD), lambda i: (i // turns, 0, 0, i % turns)
     )
     held = pl.BlockSpec(memory_space=pltpu.VMEM)
     size = (2 * spans * pairs, 2 * SPAN)
     return pl.pallas_call(
         kernel,
-        grid=(pairs,),
+        grid=(pairs // SIDES,),
         in_specs=[whole, weight_spec, weight_spec, token_spec],
         out_specs=[held] * 5 + [pl.BlockSpec(size, lambda i: (0, 0))],
         out_shape=[
@@ -352,64 +364,67 @@
     def kernel(k_ref, v_ref, w_ref, gp_ref, top_ref, *refs):
         stat_refs = refs[:devices]
         wk_ref, wv_ref, moved_ref, out_ref, part_ref = refs[devices : devices + 5]
-        total, keys_ref, values_ref, spread = refs[devices + 5 :]
+        total, spread = refs[devices + 5 :]
         step = pl.program_id(0)
 
-        first = 2 * spans * step
-        logs = [ref[pl.ds(first, spans), :] for ref in stat_refs]
-        means = [ref[pl.ds(first + spans, spans), :] for ref in stat_refs]
-        most = logs[0]
-        for log in logs[1:]:
-            most = jnp.maximum(most, log)
-        shares = [jnp.exp(log - most) for log in logs]
-        whole = shares[0]
-        inner = shares[0] * means[0]
-        for share, mean in zip(shares[1:], means[1:]):
-            whole = whole + share
-            inner = inner + share * mean
-        inner = inner / whole
-        scale = jnp.exp(top_ref[step] - most) / whole
-
-        for span in range(spans):
-            tok = pl.ds(span * SPAN, SPAN)
-            probs = w_ref[step, span] * scale[span : span + 1]
-            probs_b = probs.astype(BF)
-            grad_scores = (
-                probs * (gp_ref[step, span] - inner[span : span + 1]) * factor
-            ).astype(BF)
-            k, v = k_ref[step, span], v_ref[step, span]
-            blended = matmul(probs_b, v, 0, 0)
-            shifted_grad = matmul(grad_scores, k, 0, 0)
-            out_ref[0, 0, tok, :HD] = blended[:SPAN, :HD].astype(BF)
-            out_ref[0, 0, tok, HD:] = blended[SPAN:, HD:].astype(BF)
-            out_ref[0, 1, tok, :HD] = shifted_grad[:SPAN, :HD].astype(BF)
-            out_ref[0, 1, tok, HD:] = shifted_grad[SPAN:, HD:].astype(BF)
-            gk = matmul(grad_scores, two_heads(moved_ref[0, 0, tok, :]))
-            gv = matmul(probs_b, two_heads(moved_ref[0, 1, tok, :]))
-            at = pl.ds(pl.multiple_of(step % TURN * 2 * HD, 2 * HD), 2 * HD)
-            gk = gk.reshape(count, 8, 2 * HD)
-            gv = gv.reshape(count, 8, 2 * HD)
-            keys_ref[:, span, :, at] = gk
-            values_ref[:, span, :, at] = gv
-
-        def project():
-            left = jnp.concatenate([keys_ref[...], values_ref[...]], 3)
-            left = left.reshape(spans * keys, 4 * TURN * HD).astype(BF)
-            return matmul(left, jnp.concatenate([wk_ref[...], wv_ref[...]], 1), 1, 1)
-
-        @pl.when(step == TURN - 1)
+        @pl.when(step == 0)
         def _():
-            term = project()
-            for block in range(blocks):
-                total[block] = term[:, block * HD : (block + 1) * HD]
-
-        @pl.when((step % TURN == TURN - 1) & (step >= TURN))
-        def _():
-            term = project()
-            for block in range(blocks):
-                total[block] += term[:, block * HD : (block + 1) * HD]
-
-        @pl.when(step == pairs - 1)
+            total[...] = jnp.zeros_like(total)
+
+        def merge(pair):
+            first = 2 * spans * pair
+            logs = [ref[pl.ds(first, spans), :] for ref in stat_refs]
+            means = [ref[pl.ds(first + spans, spans), :] for ref in stat_refs]
+            most = logs[0]
+            for log in logs[1:]:
+                most = jnp.maximum(most, log)
+            shares = [jnp.exp(log - most) for log in logs]
+            whole = shares[0]
+            inner = shares[0] * means[0]
+            for share, mean in zip(shares[1:], means[1:]):
+                whole = whole + share
+                inner = inner + share * mean
+            return jnp.exp(top_ref[pair] - most) / whole, inner / whole
+
+        flat = (spans * keys, 2 * HD)
+        terms = []
+        for side in range(SIDES):
+            pair = SIDES * step + side
+            cols = slice(side * 2 * HD, (side + 1) * 2 * HD)
+            scale, inner = merge(pair)
+            gks, gvs = [], []
+            for span in range(spans):
+                tok = slice(span * SPAN, (span + 1) * SPAN)
+                probs = w_ref[pair, span] * scale[span : span + 1]
+                probs_b = probs.astype(BF)
+                grad_scores = (
+                    probs * (gp_ref[pair, span] - inner[span : span + 1]) * factor
+                ).astype(BF)
+                for which, out in enumerate(
+                    (
+                        matmul(probs_b, v_ref[pair, span], 0, 0),
+                        matmul(grad_scores, k_ref[pair, span], 0, 0),
+                    )
+                ):
+                    both = jnp.concatenate([out[:SPAN, :HD], out[SPAN:, HD:]], 1)
+                    out_ref[0, which, tok, cols] = both.astype(BF)
+                gk = matmul(grad_scores, two_heads(moved_ref[0, 0, tok, cols]))
+                gv = matmul(probs_b, two_heads(moved_ref[0, 1, tok, cols]))
+                gks.append(gk.reshape(count, 1, 8, 2 * HD))
+                gvs.append(gv.reshape(count, 1, 8, 2 * HD))
+            left = [
+                jnp.concatenate(parts, 1).reshape(flat).astype(BF) for parts in (gks, gvs)
+            ]
+            right = [wk_ref[:, cols], wv_ref[:, cols]]
+            terms.append(matmul(jnp.concatenate(left, 1), jnp.concatenate(right, 1), 1, 1))
+        for block in range(blocks):
+            at = slice(block * HD, (block + 1) * HD)
+            term = terms[0][:, at]
+            for other in terms[1:]:
+                term = term + other[:, at]
+            total[block] += term
+
+        @pl.when(step == pairs // SIDES - 1)
         def _():
             spread[:, length - 8 :, :] = jnp.zeros((lanes, 8, HD), F32)
             for block in range(blocks):
@@ -420,9 +435,10 @@
                         spread[lane, to, :] = total[block, pl.ds(at, spans, stride=8), :]
             part_ref[...] = spread[...].astype(BF)
 
-    weight_spec = pl.BlockSpec((features, 2 * TURN * HD), lambda i: (0, i // TURN))
+    weight_spec = pl.BlockSpec((features, SIDES * 2 * HD), lambda i: (0, i))
+    turns = per_group // SIDES
     token_spec = pl.BlockSpec(
-        (1, 2, tokens, 2 * HD), lambda i: (i // per_group, 0, 0, i % per_group)
+        (1, 2, tokens, SIDES * 2 * HD), lambda i: (i // turns, 0, 0, i % turns)
     )
     held = pl.BlockSpec(memory_space=pltpu.VMEM)
     stat_spec = pl.BlockSpec(stats[0].shape, lambda i: (0, 0))
@@ -430,19 +446,17 @@
     result = (lanes, length, HD)
     return pl.pallas_call(
         kernel,
-        grid=(pairs,),
+        grid=(pairs // SIDES,),
         in_specs=[held] * 5
         + [stat_spec] * devices
         + [weight_spec, weight_spec, token_spec],
         out_specs=[token_spec, pl.BlockSpec(result, lambda i: (0, 0, 0))],
         out_shape=[
             jax.ShapeDtypeStruct((groups, 2, tokens, width), BF),
-            pltpu.HBM(result, BF),
+            jax.ShapeDtypeStruct(result, BF),
         ],
         scratch_shapes=[
             pltpu.VMEM((blocks, spans * keys, HD), F32),
-            pltpu.VMEM((count, spans, 8, 2 * TURN * HD), F32),
-            pltpu.VMEM((count, spans, 8, 2 * TURN * HD), F32),
             pltpu.VMEM(result, F32),
         ],
         compiler_params=SMALL,
@@ -486,15 +500,17 @@
     fetched = lax.all_to_all(picked, ("z", "y"), 0, 0, tiled=True)
 
     *scored, stat = score_spans(fetched, key_weight, value_weight, moved)
+    own_target = after(own_here, stat).reshape(1, -1)
+    others_target = places(after(others, stat))[0].reshape(1, -1)
     stats = [send_ring(stat, "x", away) for away in range(groups)]
+    stats[0] = after(stats[0], own_target, others_target)
     output, terms = blend_spans(scored, stats, key_weight, value_weight, moved)
     output = lax.psum_scatter(output, "x", scatter_dimension=0)
 
     home = lax.all_to_all(terms, ("z", "y"), 0, 0, tiled=True)
-    others_here = places(after(others, terms))[0]
-    sums = sum_rows(home, own_here.reshape(1, -1), picks, rows, features)
+    sums = sum_rows(home, own_target, picks, rows, features)
     home = send_ring(home, "c", 1)
-    sums = sum_rows(home, others_here.reshape(1, -1), picks, rows, features, sums)
+    sums = sum_rows(home, others_target, picks, rows, features, sums)
     returned = sums.reshape(lanes, stored, features)
     returned = lax.all_to_all(returned, ("z", "y"), 0, 0, tiled=True)
     attended, d_query = move_back(output)

time: 242 us -> 256 us (1.058)
  blocking collectives: 124 us -> 81.2 us
  waiting for transfers between devices: 29.7 us -> 66.3 us
  local copies, waits for them, and re-layouts: 4.9 us -> 20.9 us
  starting transfers between devices: 10.1 us -> 15.7 us
    all_to_all x1 -> x0, blocking collectives: 44 us -> none  [shards(): fetched = lax.all_to_all(picked, ('z', 'y'), 0, 0, tiled=True)]
    all_to_all x0 -> x1, waiting for transfers between devices: none -> 37.5 us  [shards(): fetched = lax.all_to_all(picked, ('z', 'y'), 0, 0, tiled=True)]
    unnamed x12 -> x30, local copies, waits for them, and re-layouts: 3.46 us -> 19.5 us
    all_to_all x0 -> x1, starting transfers between devices: none -> 5.57 us  [shards(): fetched = lax.all_to_all(picked, ('z', 'y'), 0, 0, tiled=True)]
  transfers between devices with their start and end apart: 8 -> 9, of which waited for: 5 -> 7; matrix products, arithmetic and copies ran while one was open for 1% -> 1% of each run, Pallas kernels for 5% -> 5%
where the time goes in v5:
time: 256 us; the launch traced here: 255 us
  blocking collectives  81.2 us (32%)
  waiting for transfers between devices  66.3 us (26%)
  Pallas kernels  55.4 us (22%)
  local copies, waits for them, and re-layouts  20.9 us (8%)
  starting transfers between devices  15.7 us (6%)
  between operations  14.2 us (6%)
    all_to_all x1, blocking collectives, shards(): home = lax.all_to_all(terms, ('z', 'y'), 0, 0, tiled=True)  43.2 us
    all_to_all x1, blocking collectives, shards(): store = lax.all_to_all(pieces, ('z', 'y'), 0, 0, tiled=True)  38 us
    all_to_all x1, waiting for transfers between devices, shards(): fetched = lax.all_to_all(picked, ('z', 'y'), 0, 0, tiled=True)  37.5 us
    unnamed x30, local copies, waits for them, and re-layouts  19.5 us
    pallas_call x1, Pallas kernels, blend_spans(): pl.pallas_call(kernel, grid=(pairs // SIDES,), in_specs=[held] * 5 + [sta...  19.4 us
    pallas_call x1, Pallas kernels, score_spans(): pl.pallas_call(kernel, grid=(pairs // SIDES,), in_specs=[whole, weight_sp...  17.6 us
    all_to_all x1, waiting for transfers between devices, shards(): returned = lax.all_to_all(returned, ('z', 'y'), 0, 0, tiled=True)  13.6 us
    reduce_scatter x1, waiting for transfers between devices, shards(): output = lax.psum_scatter(output, 'x', scatter_dimension=0)  8.85 us
  transfers between devices with their start and end apart: 9, of which 7 were waited for; matrix products, arithmetic and copies ran while one was open for 1% of the time, Pallas kernels for 5%

profile of v5, /device:TPU:16, one launch (start us, length us, event | category | flops | bytes accessed | tf_op | source)
XLA Modules:
  0.0 254.9 jit_solution(3839669628640570189)
XLA Ops:
  7.2 3.8 %prepare.1 = (bf16[32,120,128]{2,1,0:T(8,128)(2,1)S(1)}, bf16[2,832,512]{2,1,0:T(8,128)(2,1)}) custom-call(bf16[512,896]{1,0:T(8,128)(2,1)} %bitcast.19, s32[2,13]{1,0:T(2,128)} %bitcast.20, s32[2,13]{1,0:T(2,128)} %bitcast.21, bf16[832,512]{1,0:T(8,128)(2,1)} %refs_3_.1, bf16[832,512]{1,0:T(8,128)(2,1)} %refs_4_.2), custom_call_target="tpu_custom_call" | custom-call | flops 469762048 | bytes 5242880 | tf_op jit(solution)/shard_map/prepare/pallas_call | solution.py:96
  11.1 38.0 %all_to_all.20.store_ref = bf16[32,120,128]{2,1,0:T(8,128)(2,1)S(1)} all-to-all(bf16[32,120,128]{2,1,0:T(8,128)(2,1)S(1)} %get-tuple-element.19), channel_id=1, replica_groups=mesh['z'=8,'y'=4,'c'=2,'x'=4] {'z','y'}, dimensions={0} | all-to-all | bytes 1966080 | tf_op jit(solution)/shard_map/all_to_all | solution.py:484
  50.2 2.1 pick_rows.2.refs_0_
  52.3 3.4 %pick_rows.3 = bf16[32,184,128]{2,1,0:T(8,128)(2,1)} custom-call(s32[1024,1]{1,0:T(8,128)S(1)} %reshape_reshape.12.target_ref, bf16[32,120,128]{2,1,0:T(8,128)(2,1)S(1)} %collective-permute-done.store_ref, bf16[1024,896]{1,0:T(8,128)(2,1)S(1)} %pick_rows.2.refs_0_), custom_call_target="tpu_custom_call" | custom-call | flops 939524096 | bytes 4587520 | tf_op jit(solution)/shard_map/pick_rows/pallas_call | solution.py:167
  55.7 5.6 %all-to-all-start.1 = ((bf16[32,184,128]{2,1,0:T(8,128)(2,1)}), bf16[32,184,128]{2,1,0:T(8,128)(2,1)S(1)}, u32[]{:S(2)}, u32[]{:S(2)}) async-start(bf16[32,184,128]{2,1,0:T(8,128)(2,1)} %pick_rows.3), calls=%async_computation.1 | async-start | bytes 3014656 | tf_op jit(solution)/shard_map/all_to_all | solution.py:500
  61.5 37.5 %all-to-all-done.1.part_ref = bf16[32,184,128]{2,1,0:T(8,128)(2,1)S(1)} async-done(((bf16[32,184,128]{2,1,0:T(8,128)(2,1)}), bf16[32,184,128]{2,1,0:T(8,128)(2,1)S(1)}, u32[]{:S(2)}, u32[]{:S(2)}) %all-to-all-start.1) | async-done | bytes 1507360 | tf_op jit(solution)/shard_map/all_to_all | solution.py:500
  100.2 17.6 %score_spans.1 = (bf16[8,13,64,256]{3,2,1,0:T(8,128)(2,1)S(1)}, bf16[8,13,64,256]{3,2,1,0:T(8,128)(2,1)S(1)}, f32[8,13,64,128]{3,2,1,0:T(8,128)S(1)}, f32[8,13,6...) custom-call(bf16[32,184,128]{2,1,0:T(8,128)(2,1)} %copy-done.10, bf16[896,2048]{1,0:T(8,128)(2,1)} %refs_4_.3, ...), custom_call_target="tpu_custom_call" | custom-call | flops 6543114240 | bytes 13631488 | tf_op jit(solution)/shard_map/score_spans/pallas_call | solution.py:323
  117.8 1.8 copy-done
  119.6 1.8 copy-done.2
  123.1 1.7 copy-done.6
  124.8 2.8 %collective-permute-start.3 = (f32[208,128]{1,0:T(8,128)}, f32[208,128]{1,0:T(8,128)S(1)}, u32[]{:S(2)}, u32[]{:S(2)}) collective-permute-start(f32[208,128]{1,0:T(8,128)} %get-tuple-element.29.refs_0_), channel_id=1, source_target_pairs={{0,3},{1,0},{2,1},{3,2},{4,7},{5,4},{6,5},{7,6},{8,11},{9,8},{10,9... | collective-permute-start | bytes 319496 | tf_op jit(solution)/shard_map/ppermute | solution.py:36
  130.7 1.8 collective-permute-done.3.refs_3_
  132.6 2.4 collective-permute-done.2.refs_2_
  136.8 2.0 copy-done.1
  138.7 2.0 copy-done.3
  140.7 2.0 copy-done.5
  142.7 2.0 copy-done.7
  144.6 19.4 %blend_spans.1 = (bf16[4,2,832,512]{3,2,1,0:T(8,128)(2,1)}, bf16[32,184,128]{2,1,0:T(8,128)(2,1)}) custom-call(bf16[8,13,64,256]{3,2,1,0:T(8,128)(2,1)S(1)} %copy-done.1, bf16[8,13,64,256]{3,2,1,0:T(8,128)(2,1)S(1)} %copy-done.3, f32[8,13,64,128]{3,2,1,0:T(8,128)S(1)} %copy-done.5, f32[8,13,64,128]{3,2,1,0:T(8,128)S(1)} %copy-done.7, ...), custom_call_target="tpu_custom_call" | custom-call | flops 6979321856 | bytes 20447232 | tf_op jit(solution)/shard_map/blend_spans/pallas_call | solution.py:447
  165.4 43.2 %all_to_all.21.term_ref = bf16[32,184,128]{2,1,0:T(8,128)(2,1)S(1)} all-to-all(bf16[32,184,128]{2,1,0:T(8,128)(2,1)S(1)} %copy-done.11), channel_id=1, replica_groups=mesh['z'=8,'y'=4,'c'=2,'x'=4] {'z','y'}, dimensions={0} | all-to-all | bytes 3014656 | tf_op jit(solution)/shard_map/all_to_all | solution.py:510
  208.6 2.4 sum_rows.2.refs_0_
  211.9 3.4 %sum_rows.3 = bf16[512,896]{1,0:T(8,128)(2,1)} custom-call(s32[1,1024]{1,0:T(1,128)S(1)} %reshape_reshape.11.target_ref, bf16[32,184,128]{2,1,0:T(8,128)(2,1)S(1)} %collective-permute-done.4.term_ref, f32[512,896]{1,0:T(8,128)S(1)} %sum_rows.2.refs_0_), custom_call_target="tpu_custom_call" | custom-call | flops 939524096 | bytes 3670016 | tf_op jit(solution)/shard_map/sum_rows/pallas_call | solution.py:202
  215.2 5.6 %all-to-all-start.3 = ((bf16[32,16,896]{2,1,0:T(8,128)(2,1)}), bf16[32,16,896]{2,1,0:T(8,128)(2,1)S(1)}, u32[]{:S(2)}, u32[]{:S(2)}) async-start(bf16[32,16,896]{2,1,0:T(8,128)(2,1)} %bitcast.8), calls=%async_computation.4 | async-start | bytes 1835008 | tf_op jit(solution)/shard_map/all_to_all | solution.py:515
  220.8 8.8 %reduce-scatter.2.cloned.1.call-done = bf16[1,2,832,512]{3,2,1,0:T(8,128)(2,1)} async-done(((bf16[4,2,832,512]{3,2,1,0:T(8,128)(2,1)}), bf16[1,2,832,512]{3,2,1,0:T(8,128)(2,1)}) %reduce-scatter.2.cloned.1.call-update) | async-done | bytes 1703952 | tf_op jit(solution)/shard_map/reduce_scatter | solution.py:508
  232.7 13.6 %all-to-all-done.3 = bf16[32,16,896]{2,1,0:T(8,128)(2,1)S(1)} async-done(((bf16[32,16,896]{2,1,0:T(8,128)(2,1)}), bf16[32,16,896]{2,1,0:T(8,128)(2,1)S(1)}, u32[]{:S(2)}, u32[]{:S(2)}) %all-to-all-start.3) | async-done | bytes 917536 | tf_op jit(solution)/shard_map/all_to_all | solution.py:515
  (50 shorter events, 16.1 us)
Async XLA Ops:
  7.2 91.9 %all-gather.3.cloned.1.call-start = ((), (), s32[]{:S(2)}) async-start(), calls=%async_computation.6 | async-start | bytes 8519680 | tf_op jit(solution)/shard_map/all_gather | solution.py:486
  49.1 3.2 %collective-permute-start = (bf16[32,120,128]{2,1,0:T(8,128)(2,1)S(1)}, bf16[32,120,128]{2,1,0:T(8,128)(2,1)S(1)}, u32[]{:S(2)}, u32[]{:S(2)}) collective-permute-start(bf16[32,120,128]{2,1,0:T(8,128)(2,1)S(1)} %all_to_all.20.store_ref), channel_id=1, source_target_pairs={{0,4},{4,0},{1,5},{5,1},{2,6},{6,2},{3,7},{7,3},{8,12},{12,8},{9,1... | collective-permute-start | bytes 2949128 | tf_op jit(solution)/shard_map/ppermute | solution.py:36
  52.3 3.4 %copy-start.9 = (bf16[32,120,128]{2,1,0:T(8,128)(2,1)}, bf16[32,120,128]{2,1,0:T(8,128)(2,1)S(1)}, u32[]{:S(2)}) copy-start(bf16[32,120,128]{2,1,0:T(8,128)(2,1)S(1)} %collective-permute-done.store_ref) | copy-start | bytes 2949124
  55.7 43.3 %all-to-all-start.1 = ((bf16[32,184,128]{2,1,0:T(8,128)(2,1)}), bf16[32,184,128]{2,1,0:T(8,128)(2,1)S(1)}, u32[]{:S(2)}, u32[]{:S(2)}) async-start(bf16[32,184,128]{2,1,0:T(8,128)(2,1)} %pick_rows.3), calls=%async_computation.1 | async-start | bytes 3014656 | tf_op jit(solution)/shard_map/all_to_all | solution.py:500
  61.3 168.4 %reduce-scatter.2.cloned.1.call-start = ((), (), s32[]{:S(2)}) async-start(), calls=%async_computation.5 | async-start | bytes 8519680 | tf_op jit(solution)/shard_map/reduce_scatter | solution.py:508
  99.0 1.1 copy-start.10
  117.8 1.8 copy-start
  119.6 1.8 copy-start.2
  121.4 1.7 copy-start.4
  123.1 1.7 copy-start.6
  124.8 7.7 %collective-permute-start.3 = (f32[208,128]{1,0:T(8,128)}, f32[208,128]{1,0:T(8,128)S(1)}, u32[]{:S(2)}, u32[]{:S(2)}) collective-permute-start(f32[208,128]{1,0:T(8,128)} %get-tuple-element.29.refs_0_), channel_id=1, source_target_pairs={{0,3},{1,0},{2,1},{3,2},{4,7},{5,4},{6,5},{7,6},{8,11},{9,8},{10,9... | collective-permute-start | bytes 319496 | tf_op jit(solution)/shard_map/ppermute | solution.py:36
  127.6 7.4 %collective-permute-start.2 = (f32[208,128]{1,0:T(8,128)}, f32[208,128]{1,0:T(8,128)S(1)}, u32[]{:S(2)}, u32[]{:S(2)}) collective-permute-start(f32[208,128]{1,0:T(8,128)} %get-tuple-element.29.refs_0_), channel_id=1, source_target_pairs={{0,2},{1,3},{2,0},{3,1},{4,6},{5,7},{6,4},{7,5},{8,10},{9,11},{10,... | collective-permute-start | bytes 319496 | tf_op jit(solution)/shard_map/ppermute | solution.py:36
  128.4 7.8 %collective-permute-start.1 = (f32[208,128]{1,0:T(8,128)}, f32[208,128]{1,0:T(8,128)S(1)}, u32[]{:S(2)}, u32[]{:S(2)}) collective-permute-start(f32[208,128]{1,0:T(8,128)} %get-tuple-element.29.refs_0_), channel_id=1, source_target_pairs={{0,1},{1,2},{2,3},{3,0},{4,5},{5,6},{6,7},{7,4},{8,9},{9,10},{10,1... | collective-permute-start | bytes 319496 | tf_op jit(solution)/shard_map/ppermute | solution.py:36
  132.6 3.6 %copy-start.12 = (f32[208,128]{1,0:T(8,128)}, f32[208,128]{1,0:T(8,128)S(1)}, u32[]{:S(2)}) copy-start(f32[208,128]{1,0:T(8,128)S(1)} %collective-permute-done.3.refs_3_) | copy-start | bytes 319492
  135.0 1.1 copy-start.13
  136.1 0.6 copy-start.14
  136.8 2.0 copy-start.1
  138.7 2.0 copy-start.3
  140.7 2.0 copy-start.5
  142.7 2.0 copy-start.7
  164.0 1.4 copy-start.11
  208.6 3.3 %collective-permute-start.4 = (bf16[32,184,128]{2,1,0:T(8,128)(2,1)S(1)}, bf16[32,184,128]{2,1,0:T(8,128)(2,1)S(1)}, u32[]{:S(2)}, u32[]{:S(2)}) collective-permute-start(bf16[32,184,128]{2,1,0:T(8,128)(2,1)S(1)} %all_to_all.21.term_ref), channel_id=1, source_target_pairs={{0,4},{4,0},{1,5},{5,1},{2,6},{6,2},{3,7},{7,3},{8,12},{12,8},{9,1... | collective-permute-start | bytes 4521992 | tf_op jit(solution)/shard_map/ppermute | solution.py:36
  215.2 31.1 %all-to-all-start.3 = ((bf16[32,16,896]{2,1,0:T(8,128)(2,1)}), bf16[32,16,896]{2,1,0:T(8,128)(2,1)S(1)}, u32[]{:S(2)}, u32[]{:S(2)}) async-start(bf16[32,16,896]{2,1,0:T(8,128)(2,1)} %bitcast.8), calls=%async_computation.4 | async-start | bytes 1835008 | tf_op jit(solution)/shard_map/all_to_all | solution.py:515
  229.7 1.5 copy-start.8
Sparse Core Ops, SparseCore 0:
  11.2 75.3 all-gather.2
  164.1 65.4 reduce-scatter.1

commit v6 on v5

--- a/solution.py
+++ b/solution.py
@@ -14,7 +14,7 @@
 F32 = jnp.float32
 I32 = jnp.int32
 PARAMS = pltpu.CompilerParams(vmem_limit_bytes=48 * 1024 * 1024)
-SMALL = pltpu.CompilerParams(vmem_limit_bytes=50 * 1024 * 1024)
+SMALL = pltpu.CompilerParams(vmem_limit_bytes=48 * 1024 * 1024)
 
 
 def matmul(left, right, left_dim=1, right_dim=0):

time: 256 us -> 255 us (level)
    unnamed x30 -> x26, local copies, waits for them, and re-layouts: 19.5 us -> 18.3 us
where the time goes in v6:
time: 255 us; the launch traced here: 254 us
  blocking collectives  81.2 us (32%)
  waiting for transfers between devices  67.2 us (26%)
  Pallas kernels  55.4 us (22%)
  local copies, waits for them, and re-layouts  19.8 us (8%)
  starting transfers between devices  15.7 us (6%)
  between operations  14.2 us (6%)
    all_to_all x1, blocking collectives, shards(): home = lax.all_to_all(terms, ('z', 'y'), 0, 0, tiled=True)  43.2 us
    all_to_all x1, blocking collectives, shards(): store = lax.all_to_all(pieces, ('z', 'y'), 0, 0, tiled=True)  38 us
    all_to_all x1, waiting for transfers between devices, shards(): fetched = lax.all_to_all(picked, ('z', 'y'), 0, 0, tiled=True)  37.6 us
    pallas_call x1, Pallas kernels, blend_spans(): pl.pallas_call(kernel, grid=(pairs // SIDES,), in_specs=[held] * 5 + [sta...  19.4 us
    unnamed x26, local copies, waits for them, and re-layouts  18.3 us
    pallas_call x1, Pallas kernels, score_spans(): pl.pallas_call(kernel, grid=(pairs // SIDES,), in_specs=[whole, weight_sp...  17.6 us
    all_to_all x1, waiting for transfers between devices, shards(): returned = lax.all_to_all(returned, ('z', 'y'), 0, 0, tiled=True)  13.6 us
    reduce_scatter x1, waiting for transfers between devices, shards(): output = lax.psum_scatter(output, 'x', scatter_dimension=0)  8.84 us
  transfers between devices with their start and end apart: 9, of which 7 were waited for; matrix products, arithmetic and copies ran while one was open for 1% of the time, Pallas kernels for 5%

profile of v6, /device:TPU:16, one launch (start us, length us, event | category | flops | bytes accessed | tf_op | source)
XLA Modules:
  0.0 253.8 jit_solution(12324834301481918246)
XLA Ops:
  7.2 3.8 %prepare.1 = (bf16[32,120,128]{2,1,0:T(8,128)(2,1)S(1)}, bf16[2,832,512]{2,1,0:T(8,128)(2,1)}) custom-call(bf16[512,896]{1,0:T(8,128)(2,1)} %bitcast.19, s32[2,13]{1,0:T(2,128)} %bitcast.20, s32[2,13]{1,0:T(2,128)} %bitcast.21, bf16[832,512]{1,0:T(8,128)(2,1)} %refs_3_.1, bf16[832,512]{1,0:T(8,128)(2,1)} %refs_4_.2), custom_call_target="tpu_custom_call" | custom-call | flops 469762048 | bytes 5242880 | tf_op jit(solution)/shard_map/prepare/pallas_call | solution.py:96
  11.1 38.0 %all_to_all.20.store_ref = bf16[32,120,128]{2,1,0:T(8,128)(2,1)S(1)} all-to-all(bf16[32,120,128]{2,1,0:T(8,128)(2,1)S(1)} %get-tuple-element.19), channel_id=1, replica_groups=mesh['z'=8,'y'=4,'c'=2,'x'=4] {'z','y'}, dimensions={0} | all-to-all | bytes 1966080 | tf_op jit(solution)/shard_map/all_to_all | solution.py:484
  50.2 2.1 pick_rows.2.refs_0_
  52.3 3.4 %pick_rows.3 = bf16[32,184,128]{2,1,0:T(8,128)(2,1)} custom-call(s32[1024,1]{1,0:T(8,128)S(1)} %reshape_reshape.12.target_ref, bf16[32,120,128]{2,1,0:T(8,128)(2,1)S(1)} %collective-permute-done.store_ref, bf16[1024,896]{1,0:T(8,128)(2,1)S(1)} %pick_rows.2.refs_0_), custom_call_target="tpu_custom_call" | custom-call | flops 939524096 | bytes 4587520 | tf_op jit(solution)/shard_map/pick_rows/pallas_call | solution.py:167
  55.7 5.6 %all-to-all-start.1 = ((bf16[32,184,128]{2,1,0:T(8,128)(2,1)}), bf16[32,184,128]{2,1,0:T(8,128)(2,1)}, u32[]{:S(2)}, u32[]{:S(2)}) async-start(bf16[32,184,128]{2,1,0:T(8,128)(2,1)} %pick_rows.3), calls=%async_computation.1 | async-start | bytes 3014656 | tf_op jit(solution)/shard_map/all_to_all | solution.py:500
  61.5 37.6 %all-to-all-done.1.part_ref = bf16[32,184,128]{2,1,0:T(8,128)(2,1)} async-done(((bf16[32,184,128]{2,1,0:T(8,128)(2,1)}), bf16[32,184,128]{2,1,0:T(8,128)(2,1)}, u32[]{:S(2)}, u32[]{:S(2)}) %all-to-all-start.1) | async-done | bytes 1507360 | tf_op jit(solution)/shard_map/all_to_all | solution.py:500
  99.1 17.6 %score_spans.1 = (bf16[8,13,64,256]{3,2,1,0:T(8,128)(2,1)S(1)}, bf16[8,13,64,256]{3,2,1,0:T(8,128)(2,1)S(1)}, f32[8,13,64,128]{3,2,1,0:T(8,128)S(1)}, f32[8,13,6...) custom-call(bf16[32,184,128]{2,1,0:T(8,128)(2,1)} %all-to-all-done.1.part_ref, ...), custom_call_target="tpu_custom_call" | custom-call | flops 6543114240 | bytes 13631488 | tf_op jit(solution)/shard_map/score_spans/pallas_call | solution.py:323
  116.7 1.8 copy-done
  118.5 1.8 copy-done.2
  120.4 1.7 copy-done.4
  123.7 2.8 %collective-permute-start.3 = (f32[208,128]{1,0:T(8,128)}, f32[208,128]{1,0:T(8,128)S(1)}, u32[]{:S(2)}, u32[]{:S(2)}) collective-permute-start(f32[208,128]{1,0:T(8,128)} %get-tuple-element.29.refs_0_), channel_id=1, source_target_pairs={{0,3},{1,0},{2,1},{3,2},{4,7},{5,4},{6,5},{7,6},{8,11},{9,8},{10,9... | collective-permute-start | bytes 319496 | tf_op jit(solution)/shard_map/ppermute | solution.py:36
  128.8 2.7 %collective-permute-done.3.refs_3_ = f32[208,128]{1,0:T(8,128)S(1)} collective-permute-done((f32[208,128]{1,0:T(8,128)}, f32[208,128]{1,0:T(8,128)S(1)}, u32[]{:S(2)}, u32[]{:S(2)}) %collective-permute-start.3) | collective-permute-done | bytes 106528 | tf_op jit(solution)/shard_map/ppermute | solution.py:36
  131.5 2.4 collective-permute-done.2.refs_2_
  135.7 2.0 copy-done.1
  137.7 2.0 copy-done.3
  139.6 2.0 copy-done.5
  141.6 2.0 copy-done.7
  143.6 19.4 %blend_spans.1 = (bf16[4,2,832,512]{3,2,1,0:T(8,128)(2,1)}, bf16[32,184,128]{2,1,0:T(8,128)(2,1)}) custom-call(bf16[8,13,64,256]{3,2,1,0:T(8,128)(2,1)S(1)} %copy-done.1, bf16[8,13,64,256]{3,2,1,0:T(8,128)(2,1)S(1)} %copy-done.3, f32[8,13,64,128]{3,2,1,0:T(8,128)S(1)} %copy-done.5, f32[8,13,64,128]{3,2,1,0:T(8,128)S(1)} %copy-done.7, ...), custom_call_target="tpu_custom_call" | custom-call | flops 6979321856 | bytes 20447232 | tf_op jit(solution)/shard_map/blend_spans/pallas_call | solution.py:447
  164.3 43.2 %all_to_all.21.term_ref = bf16[32,184,128]{2,1,0:T(8,128)(2,1)S(1)} all-to-all(bf16[32,184,128]{2,1,0:T(8,128)(2,1)S(1)} %copy-done.9), channel_id=1, replica_groups=mesh['z'=8,'y'=4,'c'=2,'x'=4] {'z','y'}, dimensions={0} | all-to-all | bytes 3014656 | tf_op jit(solution)/shard_map/all_to_all | solution.py:510
  207.5 2.4 sum_rows.2.refs_0_
  210.8 3.4 %sum_rows.3 = bf16[512,896]{1,0:T(8,128)(2,1)} custom-call(s32[1,1024]{1,0:T(1,128)S(1)} %reshape_reshape.11.target_ref, bf16[32,184,128]{2,1,0:T(8,128)(2,1)S(1)} %collective-permute-done.4.term_ref, f32[512,896]{1,0:T(8,128)S(1)} %sum_rows.2.refs_0_), custom_call_target="tpu_custom_call" | custom-call | flops 939524096 | bytes 3670016 | tf_op jit(solution)/shard_map/sum_rows/pallas_call | solution.py:202
  214.2 5.6 %all-to-all-start.3 = ((bf16[32,16,896]{2,1,0:T(8,128)(2,1)}), bf16[32,16,896]{2,1,0:T(8,128)(2,1)S(1)}, u32[]{:S(2)}, u32[]{:S(2)}) async-start(bf16[32,16,896]{2,1,0:T(8,128)(2,1)} %bitcast.8), calls=%async_computation.4 | async-start | bytes 1835008 | tf_op jit(solution)/shard_map/all_to_all | solution.py:515
  219.8 8.8 %reduce-scatter.2.cloned.1.call-done = bf16[1,2,832,512]{3,2,1,0:T(8,128)(2,1)} async-done(((bf16[4,2,832,512]{3,2,1,0:T(8,128)(2,1)}), bf16[1,2,832,512]{3,2,1,0:T(8,128)(2,1)}) %reduce-scatter.2.cloned.1.call-update) | async-done | bytes 1703952 | tf_op jit(solution)/shard_map/reduce_scatter | solution.py:508
  231.7 13.6 %all-to-all-done.3 = bf16[32,16,896]{2,1,0:T(8,128)(2,1)S(1)} async-done(((bf16[32,16,896]{2,1,0:T(8,128)(2,1)}), bf16[32,16,896]{2,1,0:T(8,128)(2,1)S(1)}, u32[]{:S(2)}, u32[]{:S(2)}) %all-to-all-start.3) | async-done | bytes 917536 | tf_op jit(solution)/shard_map/all_to_all | solution.py:515
  (46 shorter events, 14.1 us)
Async XLA Ops:
  7.2 91.9 %all-gather.3.cloned.1.call-start = ((), (), s32[]{:S(2)}) async-start(), calls=%async_computation.6 | async-start | bytes 8519680 | tf_op jit(solution)/shard_map/all_gather | solution.py:486
  49.1 3.2 %collective-permute-start = (bf16[32,120,128]{2,1,0:T(8,128)(2,1)S(1)}, bf16[32,120,128]{2,1,0:T(8,128)(2,1)S(1)}, u32[]{:S(2)}, u32[]{:S(2)}) collective-permute-start(bf16[32,120,128]{2,1,0:T(8,128)(2,1)S(1)} %all_to_all.20.store_ref), channel_id=1, source_target_pairs={{0,4},{4,0},{1,5},{5,1},{2,6},{6,2},{3,7},{7,3},{8,12},{12,8},{9,1... | collective-permute-start | bytes 2949128 | tf_op jit(solution)/shard_map/ppermute | solution.py:36
  55.7 43.4 %all-to-all-start.1 = ((bf16[32,184,128]{2,1,0:T(8,128)(2,1)}), bf16[32,184,128]{2,1,0:T(8,128)(2,1)}, u32[]{:S(2)}, u32[]{:S(2)}) async-start(bf16[32,184,128]{2,1,0:T(8,128)(2,1)} %pick_rows.3), calls=%async_computation.1 | async-start | bytes 3014656 | tf_op jit(solution)/shard_map/all_to_all | solution.py:500
  61.3 167.3 %reduce-scatter.2.cloned.1.call-start = ((), (), s32[]{:S(2)}) async-start(), calls=%async_computation.5 | async-start | bytes 8519680 | tf_op jit(solution)/shard_map/reduce_scatter | solution.py:508
  116.7 1.8 copy-start
  118.5 1.8 copy-start.2
  120.4 1.7 copy-start.4
  122.1 1.7 copy-start.6
  123.7 7.7 %collective-permute-start.3 = (f32[208,128]{1,0:T(8,128)}, f32[208,128]{1,0:T(8,128)S(1)}, u32[]{:S(2)}, u32[]{:S(2)}) collective-permute-start(f32[208,128]{1,0:T(8,128)} %get-tuple-element.29.refs_0_), channel_id=1, source_target_pairs={{0,3},{1,0},{2,1},{3,2},{4,7},{5,4},{6,5},{7,6},{8,11},{9,8},{10,9... | collective-permute-start | bytes 319496 | tf_op jit(solution)/shard_map/ppermute | solution.py:36
  126.5 7.4 %collective-permute-start.2 = (f32[208,128]{1,0:T(8,128)}, f32[208,128]{1,0:T(8,128)S(1)}, u32[]{:S(2)}, u32[]{:S(2)}) collective-permute-start(f32[208,128]{1,0:T(8,128)} %get-tuple-element.29.refs_0_), channel_id=1, source_target_pairs={{0,2},{1,3},{2,0},{3,1},{4,6},{5,7},{6,4},{7,5},{8,10},{9,11},{10,... | collective-permute-start | bytes 319496 | tf_op jit(solution)/shard_map/ppermute | solution.py:36
  127.3 7.8 %collective-permute-start.1 = (f32[208,128]{1,0:T(8,128)}, f32[208,128]{1,0:T(8,128)S(1)}, u32[]{:S(2)}, u32[]{:S(2)}) collective-permute-start(f32[208,128]{1,0:T(8,128)} %get-tuple-element.29.refs_0_), channel_id=1, source_target_pairs={{0,1},{1,2},{2,3},{3,0},{4,5},{5,6},{6,7},{7,4},{8,9},{9,10},{10,1... | collective-permute-start | bytes 319496 | tf_op jit(solution)/shard_map/ppermute | solution.py:36
  131.5 3.6 %copy-start.10 = (f32[208,128]{1,0:T(8,128)}, f32[208,128]{1,0:T(8,128)S(1)}, u32[]{:S(2)}) copy-start(f32[208,128]{1,0:T(8,128)S(1)} %collective-permute-done.3.refs_3_) | copy-start | bytes 319492
  133.9 1.1 copy-start.11
  135.1 0.6 copy-start.12
  135.7 2.0 copy-start.1
  137.7 2.0 copy-start.3
  139.6 2.0 copy-start.5
  141.6 2.0 copy-start.7
  162.9 1.4 copy-start.9
  207.5 3.3 %collective-permute-start.4 = (bf16[32,184,128]{2,1,0:T(8,128)(2,1)S(1)}, bf16[32,184,128]{2,1,0:T(8,128)(2,1)S(1)}, u32[]{:S(2)}, u32[]{:S(2)}) collective-permute-start(bf16[32,184,128]{2,1,0:T(8,128)(2,1)S(1)} %all_to_all.21.term_ref), channel_id=1, source_target_pairs={{0,4},{4,0},{1,5},{5,1},{2,6},{6,2},{3,7},{7,3},{8,12},{12,8},{9,1... | collective-permute-start | bytes 4521992 | tf_op jit(solution)/shard_map/ppermute | solution.py:36
  214.2 31.1 %all-to-all-start.3 = ((bf16[32,16,896]{2,1,0:T(8,128)(2,1)}), bf16[32,16,896]{2,1,0:T(8,128)(2,1)S(1)}, u32[]{:S(2)}, u32[]{:S(2)}) async-start(bf16[32,16,896]{2,1,0:T(8,128)(2,1)} %bitcast.8), calls=%async_computation.4 | async-start | bytes 1835008 | tf_op jit(solution)/shard_map/all_to_all | solution.py:515
  228.6 1.5 copy-start.8
Sparse Core Ops, SparseCore 0:
  11.2 75.3 all-gather.2
  163.1 65.4 reduce-scatter.1

commit v7 on v6

--- a/solution.py
+++ b/solution.py
@@ -500,17 +500,15 @@
     fetched = lax.all_to_all(picked, ("z", "y"), 0, 0, tiled=True)
 
     *scored, stat = score_spans(fetched, key_weight, value_weight, moved)
-    own_target = after(own_here, stat).reshape(1, -1)
-    others_target = places(after(others, stat))[0].reshape(1, -1)
     stats = [send_ring(stat, "x", away) for away in range(groups)]
-    stats[0] = after(stats[0], own_target, others_target)
     output, terms = blend_spans(scored, stats, key_weight, value_weight, moved)
     output = lax.psum_scatter(output, "x", scatter_dimension=0)
 
     home = lax.all_to_all(terms, ("z", "y"), 0, 0, tiled=True)
-    sums = sum_rows(home, own_target, picks, rows, features)
+    others_here = places(after(others, terms))[0]
+    sums = sum_rows(home, own_here.reshape(1, -1), picks, rows, features)
     home = send_ring(home, "c", 1)
-    sums = sum_rows(home, others_target, picks, rows, features, sums)
+    sums = sum_rows(home, others_here.reshape(1, -1), picks, rows, features, sums)
     returned = sums.reshape(lanes, stored, features)
     returned = lax.all_to_all(returned, ("z", "y"), 0, 0, tiled=True)
     attended, d_query = move_back(output)

time: 255 us -> 239 us (0.937)
  blocking collectives: 81.2 us -> 124 us
  waiting for transfers between devices: 67.2 us -> 29.7 us
  local copies, waits for them, and re-layouts: 19.8 us -> 4.9 us
  starting transfers between devices: 15.7 us -> 10.1 us
    all_to_all x0 -> x1, blocking collectives: none -> 44 us  [shards(): fetched = lax.all_to_all(picked, ('z', 'y'), 0, 0, tiled=True)]
    all_to_all x1 -> x0, waiting for transfers between devices: 37.6 us -> none  [shards(): fetched = lax.all_to_all(picked, ('z', 'y'), 0, 0, tiled=True)]
    unnamed x26 -> x12, local copies, waits for them, and re-layouts: 18.3 us -> 3.46 us
    all_to_all x1 -> x0, starting transfers between devices: 5.61 us -> none  [shards(): fetched = lax.all_to_all(picked, ('z', 'y'), 0, 0, tiled=True)]
  transfers between devices with their start and end apart: 9 -> 8, of which waited for: 7 -> 5; matrix products, arithmetic and copies ran while one was open for 1% -> 1% of each run, Pallas kernels for 5% -> 5%
where the time goes in v7:
time: 239 us
  blocking collectives  124 us (52%)
  Pallas kernels  54.3 us (23%)
  waiting for transfers between devices  29.7 us (12%)
  between operations  14.2 us (6%)
  starting transfers between devices  10.1 us (4%)
  local copies, waits for them, and re-layouts  4.9 us (2%)
    all_to_all x1, blocking collectives, shards(): fetched = lax.all_to_all(picked, ('z', 'y'), 0, 0, tiled=True)  44 us
    all_to_all x1, blocking collectives, shards(): home = lax.all_to_all(terms, ('z', 'y'), 0, 0, tiled=True)  42.4 us
    all_to_all x1, blocking collectives, shards(): store = lax.all_to_all(pieces, ('z', 'y'), 0, 0, tiled=True)  38 us
    pallas_call x1, Pallas kernels, blend_spans(): pl.pallas_call(kernel, grid=(pairs // SIDES,), in_specs=[held] * 5 + [sta...  19.4 us
    pallas_call x1, Pallas kernels, score_spans(): pl.pallas_call(kernel, grid=(pairs // SIDES,), in_specs=[whole, weight_sp...  17.6 us
    all_to_all x1, waiting for transfers between devices, shards(): returned = lax.all_to_all(returned, ('z', 'y'), 0, 0, tiled=True)  14.7 us
    reduce_scatter x1, waiting for transfers between devices, shards(): output = lax.psum_scatter(output, 'x', scatter_dimension=0)  8.08 us
    ppermute x5, waiting for transfers between devices, send_ring(): lax.ppermute(array, axis, [(i, (i + step) % size) for i in range(size)])  6.79 us
  transfers between devices with their start and end apart: 8, of which 5 were waited for; matrix products, arithmetic and copies ran while one was open for 1% of the time, Pallas kernels for 5%

profile of v7, /device:TPU:16, one launch (start us, length us, event | category | flops | bytes accessed | tf_op | source)
XLA Modules:
  0.0 238.8 jit_solution(8995602918427451376)
XLA Ops:
  7.2 3.8 %prepare.1 = (bf16[32,120,128]{2,1,0:T(8,128)(2,1)S(1)}, bf16[2,832,512]{2,1,0:T(8,128)(2,1)}) custom-call(bf16[512,896]{1,0:T(8,128)(2,1)} %bitcast.17, s32[2,13]{1,0:T(2,128)} %bitcast.18, s32[2,13]{1,0:T(2,128)} %bitcast.19, bf16[832,512]{1,0:T(8,128)(2,1)} %refs_3_.1, bf16[832,512]{1,0:T(8,128)(2,1)} %refs_4_.2), custom_call_target="tpu_custom_call" | custom-call | flops 469762048 | bytes 5242880 | tf_op jit(solution)/shard_map/prepare/pallas_call | solution.py:96
  11.1 38.0 %all_to_all.20.store_ref = bf16[32,120,128]{2,1,0:T(8,128)(2,1)S(1)} all-to-all(bf16[32,120,128]{2,1,0:T(8,128)(2,1)S(1)} %get-tuple-element.17), channel_id=1, replica_groups=mesh['z'=8,'y'=4,'c'=2,'x'=4] {'z','y'}, dimensions={0} | all-to-all | bytes 1966080 | tf_op jit(solution)/shard_map/all_to_all | solution.py:484
  50.2 2.1 pick_rows.2.refs_0_
  52.4 2.2 pick_rows.3
  54.6 44.0 %all_to_all.21.part_ref = bf16[32,184,128]{2,1,0:T(8,128)(2,1)} all-to-all(bf16[32,184,128]{2,1,0:T(8,128)(2,1)S(1)} %pick_rows.3), channel_id=1, replica_groups=mesh['z'=8,'y'=4,'c'=2,'x'=4] {'z','y'}, dimensions={0} | all-to-all | bytes 3014656 | tf_op jit(solution)/shard_map/all_to_all | solution.py:500
  98.7 17.6 %score_spans.1 = (bf16[8,13,64,256]{3,2,1,0:T(8,128)(2,1)S(1)}, bf16[8,13,64,256]{3,2,1,0:T(8,128)(2,1)S(1)}, f32[8,13,64,128]{3,2,1,0:T(8,128)S(1)}, f32[8,13,6...) custom-call(bf16[32,184,128]{2,1,0:T(8,128)(2,1)} %all_to_all.21.part_ref, ...), custom_call_target="tpu_custom_call" | custom-call | flops 6543114240 | bytes 13631488 | tf_op jit(solution)/shard_map/score_spans/pallas_call | solution.py:323
  116.3 2.8 %collective-permute-start.3 = (f32[208,128]{1,0:T(8,128)}, f32[208,128]{1,0:T(8,128)S(1)}, u32[]{:S(2)}, u32[]{:S(2)}) collective-permute-start(f32[208,128]{1,0:T(8,128)} %get-tuple-element.24.refs_0_), channel_id=1, source_target_pairs={{0,3},{1,0},{2,1},{3,2},{4,7},{5,4},{6,5},{7,6},{8,11},{9,8},{10,9... | collective-permute-start | bytes 319496 | tf_op jit(solution)/shard_map/ppermute | solution.py:36
  119.0 0.8 collective-permute-start.2
  119.8 0.9 collective-permute-start.1
  120.7 3.2 %collective-permute-done.3.refs_3_ = f32[208,128]{1,0:T(8,128)S(1)} collective-permute-done((f32[208,128]{1,0:T(8,128)}, f32[208,128]{1,0:T(8,128)S(1)}, u32[]{:S(2)}, u32[]{:S(2)}) %collective-permute-start.3) | collective-permute-done | bytes 106528 | tf_op jit(solution)/shard_map/ppermute | solution.py:36
  124.0 2.5 %collective-permute-done.2.refs_2_ = f32[208,128]{1,0:T(8,128)S(1)} collective-permute-done((f32[208,128]{1,0:T(8,128)}, f32[208,128]{1,0:T(8,128)S(1)}, u32[]{:S(2)}, u32[]{:S(2)}) %collective-permute-start.2) | collective-permute-done | bytes 106528 | tf_op jit(solution)/shard_map/ppermute | solution.py:36
  126.4 1.1 collective-permute-done.1.refs_1_
  128.2 19.4 %blend_spans.1 = (bf16[4,2,832,512]{3,2,1,0:T(8,128)(2,1)}, bf16[32,184,128]{2,1,0:T(8,128)(2,1)}) custom-call(bf16[8,13,64,256]{3,2,1,0:T(8,128)(2,1)S(1)} %get-tuple-element.19.k_ref, bf16[8,13,64,256]{3,2,1,0:T(8,128)(2,1)S(1)} %get-tuple-element.20.v_ref, f32[8,13,64,128]{3,2,1,0:T(8,128)S(1)} %get-tuple-element.21.w_ref, ...), custom_call_target="tpu_custom_call" | custom-call | flops 6979321856 | bytes 20447232 | tf_op jit(solution)/shard_map/blend_spans/pallas_call | solution.py:447
  147.6 1.4 copy-done.2
  148.9 42.4 %all_to_all.22.term_ref = bf16[32,184,128]{2,1,0:T(8,128)(2,1)S(1)} all-to-all(bf16[32,184,128]{2,1,0:T(8,128)(2,1)S(1)} %copy-done.2), channel_id=1, replica_groups=mesh['z'=8,'y'=4,'c'=2,'x'=4] {'z','y'}, dimensions={0} | all-to-all | bytes 3014656 | tf_op jit(solution)/shard_map/all_to_all | solution.py:507
  191.5 0.9 convert_bitcast_fusion
  192.9 2.4 %sum_rows.2.refs_0_ = f32[512,896]{1,0:T(8,128)S(1)} custom-call(s32[1,1024]{1,0:T(1,128)S(1)} %reshape_reshape.15.target_ref, bf16[32,184,128]{2,1,0:T(8,128)(2,1)S(1)} %all_to_all.22.term_ref), custom_call_target="tpu_custom_call" | custom-call | flops 939524096 | bytes 3670016 | tf_op jit(solution)/shard_map/sum_rows/pallas_call | solution.py:202
  195.4 3.4 %sum_rows.3 = bf16[512,896]{1,0:T(8,128)(2,1)} custom-call(s32[1,1024]{1,0:T(1,128)S(1)} %reshape_reshape.14.target_ref, bf16[32,184,128]{2,1,0:T(8,128)(2,1)S(1)} %collective-permute-done.4.term_ref, f32[512,896]{1,0:T(8,128)S(1)} %sum_rows.2.refs_0_), custom_call_target="tpu_custom_call" | custom-call | flops 939524096 | bytes 3670016 | tf_op jit(solution)/shard_map/sum_rows/pallas_call | solution.py:202
  198.7 5.6 %all-to-all-start.3 = ((bf16[32,16,896]{2,1,0:T(8,128)(2,1)}), bf16[32,16,896]{2,1,0:T(8,128)(2,1)S(1)}, u32[]{:S(2)}, u32[]{:S(2)}) async-start(bf16[32,16,896]{2,1,0:T(8,128)(2,1)} %bitcast.7), calls=%async_computation.4 | async-start | bytes 1835008 | tf_op jit(solution)/shard_map/all_to_all | solution.py:513
  204.3 8.1 %reduce-scatter.2.cloned.1.call-done = bf16[1,2,832,512]{3,2,1,0:T(8,128)(2,1)} async-done(((bf16[4,2,832,512]{3,2,1,0:T(8,128)(2,1)}), bf16[1,2,832,512]{3,2,1,0:T(8,128)(2,1)}) %reduce-scatter.2.cloned.1.call-update) | async-done | bytes 1703952 | tf_op jit(solution)/shard_map/reduce_scatter | solution.py:505
  212.4 1.5 copy-done
  213.9 1.6 move_back.1
  215.5 14.7 %all-to-all-done.3 = bf16[32,16,896]{2,1,0:T(8,128)(2,1)S(1)} async-done(((bf16[32,16,896]{2,1,0:T(8,128)(2,1)}), bf16[32,16,896]{2,1,0:T(8,128)(2,1)S(1)}, u32[]{:S(2)}, u32[]{:S(2)}) %all-to-all-start.3) | async-done | bytes 917536 | tf_op jit(solution)/shard_map/all_to_all | solution.py:513
  230.3 1.7 join_pieces.1
  (31 shorter events, 2.6 us)
Async XLA Ops:
  7.2 91.5 %all-gather.3.cloned.1.call-start = ((), (), s32[]{:S(2)}) async-start(), calls=%async_computation.6 | async-start | bytes 8519680 | tf_op jit(solution)/shard_map/all_gather | solution.py:486
  11.1 201.3 %reduce-scatter.2.cloned.1.call-start = ((), (), s32[]{:S(2)}) async-start(), calls=%async_computation.5 | async-start | bytes 8519680 | tf_op jit(solution)/shard_map/reduce_scatter | solution.py:505
  49.2 3.2 %collective-permute-start = (bf16[32,120,128]{2,1,0:T(8,128)(2,1)S(1)}, bf16[32,120,128]{2,1,0:T(8,128)(2,1)S(1)}, u32[]{:S(2)}, u32[]{:S(2)}) collective-permute-start(bf16[32,120,128]{2,1,0:T(8,128)(2,1)S(1)} %all_to_all.20.store_ref), channel_id=1, source_target_pairs={{0,4},{4,0},{1,5},{5,1},{2,6},{6,2},{3,7},{7,3},{8,12},{12,8},{9,1... | collective-permute-start | bytes 2949128 | tf_op jit(solution)/shard_map/ppermute | solution.py:36
  52.4 2.2 copy-start.1
  116.3 7.7 %collective-permute-start.3 = (f32[208,128]{1,0:T(8,128)}, f32[208,128]{1,0:T(8,128)S(1)}, u32[]{:S(2)}, u32[]{:S(2)}) collective-permute-start(f32[208,128]{1,0:T(8,128)} %get-tuple-element.24.refs_0_), channel_id=1, source_target_pairs={{0,3},{1,0},{2,1},{3,2},{4,7},{5,4},{6,5},{7,6},{8,11},{9,8},{10,9... | collective-permute-start | bytes 319496 | tf_op jit(solution)/shard_map/ppermute | solution.py:36
  119.0 7.4 %collective-permute-start.2 = (f32[208,128]{1,0:T(8,128)}, f32[208,128]{1,0:T(8,128)S(1)}, u32[]{:S(2)}, u32[]{:S(2)}) collective-permute-start(f32[208,128]{1,0:T(8,128)} %get-tuple-element.24.refs_0_), channel_id=1, source_target_pairs={{0,2},{1,3},{2,0},{3,1},{4,6},{5,7},{6,4},{7,5},{8,10},{9,11},{10,... | collective-permute-start | bytes 319496 | tf_op jit(solution)/shard_map/ppermute | solution.py:36
  119.8 7.7 %collective-permute-start.1 = (f32[208,128]{1,0:T(8,128)}, f32[208,128]{1,0:T(8,128)S(1)}, u32[]{:S(2)}, u32[]{:S(2)}) collective-permute-start(f32[208,128]{1,0:T(8,128)} %get-tuple-element.24.refs_0_), channel_id=1, source_target_pairs={{0,1},{1,2},{2,3},{3,0},{4,5},{5,6},{6,7},{7,4},{8,9},{9,10},{10,1... | collective-permute-start | bytes 319496 | tf_op jit(solution)/shard_map/ppermute | solution.py:36
  124.0 3.6 %copy-start.3 = (f32[208,128]{1,0:T(8,128)}, f32[208,128]{1,0:T(8,128)S(1)}, u32[]{:S(2)}) copy-start(f32[208,128]{1,0:T(8,128)S(1)} %collective-permute-done.3.refs_3_) | copy-start | bytes 319492
  126.4 1.1 copy-start.4
  127.5 0.6 copy-start.5
  147.5 1.4 copy-start.2
  191.3 4.1 %collective-permute-start.4 = (bf16[32,184,128]{2,1,0:T(8,128)(2,1)S(1)}, bf16[32,184,128]{2,1,0:T(8,128)(2,1)S(1)}, u32[]{:S(2)}, u32[]{:S(2)}) collective-permute-start(bf16[32,184,128]{2,1,0:T(8,128)(2,1)S(1)} %all_to_all.22.term_ref), channel_id=1, source_target_pairs={{0,4},{4,0},{1,5},{5,1},{2,6},{6,2},{3,7},{7,3},{8,12},{12,8},{9,1... | collective-permute-start | bytes 4521992 | tf_op jit(solution)/shard_map/ppermute | solution.py:36
  198.7 31.5 %all-to-all-start.3 = ((bf16[32,16,896]{2,1,0:T(8,128)(2,1)}), bf16[32,16,896]{2,1,0:T(8,128)(2,1)S(1)}, u32[]{:S(2)}, u32[]{:S(2)}) async-start(bf16[32,16,896]{2,1,0:T(8,128)(2,1)} %bitcast.7), calls=%async_computation.4 | async-start | bytes 1835008 | tf_op jit(solution)/shard_map/all_to_all | solution.py:513
  212.4 1.5 copy-start
Sparse Core Ops, SparseCore 0:
  11.2 75.3 all-gather.2
  147.7 64.6 reduce-scatter.1
